TPU v7x, 128 devices: a whole 4x4x4 slice. The times are simulated.
128 devices in a mesh: rows: 16 (over y, x), grp: 8 (over z, core).
Axes of the slice: x: 4, y: 4, z: 4, core: 2. Of those that a mesh axis runs over, the one named last changes fastest.
Arguments:
- descriptors: bfloat16 [262144, 1024], P(('rows', 'grp')), may hold values from -6 to 6
- derivatives: bfloat16 [3, 262144, 1024], P(None, ('rows', 'grp')), may hold values from -6 to 6
- force_targets: bfloat16 [3, 262144], P(None, ('rows', 'grp')), may hold values from -6 to 6
- energies: float32 [4096], P(('rows', 'grp')), may hold values from -6 to 6
- struct_atoms: int32 [128, 32], replicated, may hold values from 0 to 64, as said below
- sparse_points: bfloat16 [128, 512, 1024], P(('rows', 'grp')), may hold values from -6 to 6
- owner: int32 [1], replicated, may hold values from 0 to 127
Outputs:
- r_factor: float32 [512, 512], replicated
- projected: float32 [512], replicated
Inputs may be any that keep to these rules, and one draw needn't show every extreme that they name: `struct_atoms`: every structure slot holds 0 or 8 to 64 atoms; the slots with atoms come first in each device's row and there is at least one; in every draw one device has all 32 slots with 64 atoms each, so a device holds at most and reaches 2048 atoms.
All inputs are finite; a program needn't handle non-finite values.
Results may differ from a plain program's by a relative error of at most 0.0003.
Values may be sent and summed in bfloat16 or wider, within the bound.
No kernel may reach another device: no remote copies, remote signals or barrier semaphores. Data moves between devices by JAX's collectives and lax.ppermute only.
A program may use at most 128 MiB of HBM per device.

v0:
```python
import math

import jax
import jax.numpy as jnp
from jax import lax
from jax.sharding import PartitionSpec as P

exact_mode = lax.Precision.HIGHEST
ridge_total = 1.0


def spread(value, axis, root):
    mine = lax.axis_index(axis) == root
    return lax.psum(jnp.where(mine, value, jnp.zeros_like(value)), axis)


def gram_terms(design_rows, targets):
    gram = lax.dot_general(
        design_rows,
        design_rows,
        (((0,), (0,)), ((), ())),
        precision=exact_mode,
        preferred_element_type=jnp.float32,
    )
    rhs = jnp.dot(targets, design_rows, precision=exact_mode)
    return (gram, rhs)


def panel_block(atoms, derivs, forces, first, sizes, upper_end, panel, scale, weight):
    block_rows = atoms.shape[0]
    atom_index = first + jnp.arange(block_rows, dtype=jnp.int32)
    ends = jnp.cumsum(sizes)
    owner_struct = jnp.sum((atom_index[:, None] >= ends[None, :]).astype(jnp.int32), axis=1)
    live = atom_index < upper_end
    scores = jnp.einsum("ad,pd->ap", atoms, panel, preferred_element_type=jnp.float32) * scale
    slopes = jnp.einsum("cad,pd->cap", derivs, panel, preferred_element_type=jnp.float32) * scale
    square = scores * scores
    kernel = jnp.where(live[:, None], square * square, 0.0)
    member = (
        (jnp.arange(sizes.shape[0], dtype=jnp.int32)[:, None] == owner_struct[None, :])
        & live[None, :]
    ).astype(jnp.float32)
    energy_part = jnp.dot(member, kernel, precision=exact_mode)
    force_rows = jnp.where(live[None, :, None], -4.0 * weight * square * scores * slopes, 0.0)
    gram, rhs = gram_terms(
        force_rows.reshape(-1, panel.shape[0]), forces.astype(jnp.float32).reshape(-1)
    )
    return (gram, rhs, energy_part)


def sweep(
    atoms, derivs, forces, last_block, block_rows, sizes, upper_end, panel, scale, weight, state
):

    def visit(block_num, carried):
        start = (block_num * block_rows).astype(jnp.int32)
        atom_part = lax.dynamic_slice_in_dim(atoms, start, block_rows, 0)
        deriv_part = lax.dynamic_slice_in_dim(derivs, start, block_rows, 1)
        force_part = lax.dynamic_slice_in_dim(forces, start, block_rows, 1)
        gram, rhs, energy_part = panel_block(
            atom_part, deriv_part, force_part, start, sizes, upper_end, panel, scale, weight
        )
        return (carried[0] + gram, carried[1] + rhs, carried[2] + energy_part)

    return lax.fori_loop(0, last_block, visit, state)


def per_device(
    descriptors, derivatives, force_targets, energies, struct_atoms, sparse_points, owner
):
    rows_count = lax.axis_size("rows")
    group_count = lax.axis_size("grp")
    devices_all = rows_count * group_count
    capacity, width = descriptors.shape
    points = sparse_points.shape[1]
    slots = struct_atoms.shape[1]
    panel = spread(sparse_points[0], ("rows", "grp"), owner[0])
    device_id = lax.axis_index("rows") * group_count + lax.axis_index("grp")
    own_sizes = lax.dynamic_index_in_dim(struct_atoms, device_id, 0, keepdims=False)
    own_total = jnp.sum(own_sizes)
    scale = 1.0 / math.sqrt(width)
    weight = 1.0 / math.sqrt(48.0 * capacity * devices_all)
    block_rows = min(512, capacity // 2)
    ridge_share = 0.0
    start_state = (
        ridge_share * jnp.eye(points, dtype=jnp.float32),
        jnp.zeros((points,), jnp.float32),
        jnp.zeros((slots, points), jnp.float32),
    )
    gram, rhs, energy_sums = sweep(
        descriptors,
        derivatives,
        force_targets,
        (own_total + block_rows - 1) // block_rows,
        block_rows,
        own_sizes,
        own_total,
        panel,
        scale,
        weight,
        start_state,
    )
    norms = jnp.sqrt(jnp.maximum(own_sizes, 1).astype(jnp.float32))
    energy_rows = weight * energy_sums / norms[:, None]
    energy_gram, energy_rhs = gram_terms(energy_rows, energies)
    gram = gram + energy_gram
    rhs = rhs + energy_rhs
    gram, rhs = lax.psum((gram, rhs), ("rows", "grp"))
    gram = gram + ridge_total * jnp.eye(points, dtype=jnp.float32)
    lower = jnp.linalg.cholesky(gram)
    projected = jax.scipy.linalg.solve_triangular(lower, rhs, lower=True)
    return (lower.T, projected)


def solution(mesh):
    in_specs = (
        P(("rows", "grp"), None),
        P(None, ("rows", "grp"), None),
        P(None, ("rows", "grp")),
        P(("rows", "grp")),
        P(),
        P(("rows", "grp"), None, None),
        P(),
    )
    out_specs = (P(), P())
    return jax.shard_map(
        per_device, mesh=mesh, in_specs=in_specs, out_specs=out_specs, check_vma=False
    )
```

profile of v0, /device:TPU:1, one launch (start us, length us, event | category | flops | bytes accessed | tf_op | source)
XLA Modules:
  0.0 518.5 jit_solution(14196100541430753485)
XLA Ops:
  10.9 153.1 %all-reduce.4.cloned.1.call-done = bf16[512,1024]{1,0:T(8,128)(2,1)} async-done(((bf16[512,1024]{1,0:T(8,128)(2,1)}), bf16[512,1024]{1,0:T(8,128)(2,1)}) %all-reduce.4.cloned.1.call-update) | async-done | bytes 1048592 | tf_op jit(solution)/shard_map/psum | solution.py:14
  164.1 48.9 %while.17 = (s32[]{:T(128)}, f32[512,512]{1,0:T(8,128)S(1)}, f32[512]{0:T(512)S(1)}, f32[32,512]{1,0:T(8,128)S(1)}, s32[]{:T(128)}, /*index=5*/s32[]{:T(128)}, b...) while((s32[]{:T(128)}, f32[512,512]{1,0:T(8,128)S(1)}, ...), condition=%wide.region_5.6_spmd, body=%wide.region_3.5_spmd.sunk | while | flops 7095027200 | bytes 27422064 | solution.py:65
  165.7 2.3 multiply_multiply_fusion.2
  168.7 3.7 fusion.91
  172.5 1.4 fusion.93
  173.9 6.5 %fusion.92 = f32[512,512]{1,0:T(8,128)S(1)} fusion(f32[512,512]{1,0:T(8,128)S(1)} %get-tuple-element.320, f32[3,512,512]{2,1,0:T(8,128)S(1)} %fusion.91, f32[512,512]{1,0:T(8,128)S(1)} %get-tuple-element.296, pred[512]{0:T(512)(128)(4,1)S(1)} %broadcast_compare_fusion.2), kind=kOutput, calls=%fused_computation.13.clone.1 | convolution fusion | flops 4833673216 | bytes 6291968 | tf_op jit(solution)/shard_map/while/body/dot_general | solution.py:18
  182.0 2.3 multiply_multiply_fusion.2
  185.0 3.7 fusion.91
  188.8 1.4 fusion.93
  190.2 6.5 %fusion.92 = f32[512,512]{1,0:T(8,128)S(1)} fusion(f32[512,512]{1,0:T(8,128)S(1)} %get-tuple-element.320, f32[3,512,512]{2,1,0:T(8,128)S(1)} %fusion.91, f32[512,512]{1,0:T(8,128)S(1)} %get-tuple-element.296, pred[512]{0:T(512)(128)(4,1)S(1)} %broadcast_compare_fusion.2), kind=kOutput, calls=%fused_computation.13.clone.1 | convolution fusion | flops 4833673216 | bytes 6291968 | tf_op jit(solution)/shard_map/while/body/dot_general | solution.py:18
  198.3 2.3 multiply_multiply_fusion.2
  201.3 3.7 fusion.91
  205.0 1.4 fusion.93
  206.5 6.5 %fusion.92 = f32[512,512]{1,0:T(8,128)S(1)} fusion(f32[512,512]{1,0:T(8,128)S(1)} %get-tuple-element.320, f32[3,512,512]{2,1,0:T(8,128)S(1)} %fusion.91, f32[512,512]{1,0:T(8,128)S(1)} %get-tuple-element.296, pred[512]{0:T(512)(128)(4,1)S(1)} %broadcast_compare_fusion.2), kind=kOutput, calls=%fused_computation.13.clone.1 | convolution fusion | flops 4833673216 | bytes 6291968 | tf_op jit(solution)/shard_map/while/body/dot_general | solution.py:18
  213.3 2.1 convolution_add_fusion.1
  215.7 75.8 %psum.23 = f32[512]{0:T(512)S(1)} all-reduce(f32[512]{0:T(512)S(1)} %add.130), channel_id=1, replica_groups=mesh['rows'=16,'grp'=8] {'rows','grp'}, use_global_device_ids=true, to_apply=%region_15.16 | all-reduce | flops 512 | bytes 4096 | tf_op jit(solution)/shard_map/psum | solution.py:108
  291.5 83.1 %all-reduce.6.cloned.1.call-done = f32[512,512]{0,1:T(8,128)} async-done(((f32[512,512]{0,1:T(8,128)}), f32[512,512]{0,1:T(8,128)}) %all-reduce.6.cloned.1.call-update) | async-done | bytes 1048592 | tf_op jit(solution)/shard_map/psum | solution.py:108
  374.6 1.4 convert_add_fusion
  376.6 11.7 %cholesky.103 = f32[128,128]{1,0:T(8,128)S(1)} custom-call(f32[128,128]{1,0:T(8,128)S(1)} %cholesky.263), custom_call_target="Cholesky" | custom-call | tf_op jit(solution)/shard_map/jit(cholesky)/cholesky | solution.py:110
  388.5 9.8 %custom-call.31 = f32[1,128,128]{1,2,0:T(8,128)S(1)} custom-call(f32[1,128,128]{2,1,0:T(8,128)S(1)} %get-tuple-element.198), custom_call_target="InvertDiagBlocksLowerTriangular" | custom-call | tf_op jit(solution)/shard_map/jit(cholesky)/cholesky | solution.py:110
  399.0 11.7 %cholesky.215 = f32[128,128]{1,0:T(8,128)S(1)} custom-call(f32[128,128]{1,0:T(8,128)S(1)} %cholesky.267), custom_call_target="Cholesky" | custom-call | tf_op jit(solution)/shard_map/jit(cholesky)/cholesky | solution.py:110
  410.7 10.0 %custom-call.32 = f32[1,128,128]{1,2,0:T(8,128)S(1)} custom-call(f32[1,128,128]{2,1,0:T(8,128)S(1)} %get-tuple-element.195), custom_call_target="InvertDiagBlocksLowerTriangular" | custom-call | tf_op jit(solution)/shard_map/jit(cholesky)/cholesky | solution.py:110
  421.4 11.7 %cholesky.236 = f32[128,128]{1,0:T(8,128)S(1)} custom-call(f32[128,128]{1,0:T(8,128)S(1)} %cholesky.272), custom_call_target="Cholesky" | custom-call | tf_op jit(solution)/shard_map/jit(cholesky)/cholesky | solution.py:110
  433.9 9.8 %custom-call.33 = f32[1,128,128]{1,2,0:T(8,128)S(1)} custom-call(f32[1,128,128]{2,1,0:T(8,128)S(1)} %get-tuple-element.192), custom_call_target="InvertDiagBlocksLowerTriangular" | custom-call | tf_op jit(solution)/shard_map/jit(cholesky)/cholesky | solution.py:110
  444.3 11.7 %cholesky.253 = f32[128,128]{1,0:T(8,128)S(1)} custom-call(f32[128,128]{1,0:T(8,128)S(1)} %convolution_subtract_fusion.2), custom_call_target="Cholesky" | custom-call | tf_op jit(solution)/shard_map/jit(cholesky)/cholesky | solution.py:110
  460.4 1.3 copy.26
  461.7 8.1 %while.18 = (s32[]{:T(128)}, f32[512,512]{1,0:T(8,128)S(1)}, s32[4,2]{0,1:T(2,128)S(1)}, f32[4,128,128]{2,1,0:T(8,128)S(1)}, s32[]{:T(128)}) while((s32[]{:T(128)}, f32[512,512]{1,0:T(8,128)S(1)}, s32[4,2]{0,1:T(2,128)S(1)}, f32[4,128,128]{2,1,0:T(8,128)S(1)}, s32[]{:T(128)}) %tuple.62), condition=%wide.while_cond, body=%wide.while_body.sunk | while | flops 2 | bytes 131189 | solution.py:111
  462.4 1.3 bitcast_dynamic-update-slice_fusion.2
  464.4 1.3 bitcast_dynamic-update-slice_fusion.2
  466.5 1.3 bitcast_dynamic-update-slice_fusion.2
  468.5 1.3 bitcast_dynamic-update-slice_fusion.2
  469.8 39.3 %custom-call.34 = f32[4,128,128]{1,2,0:T(8,128)S(1)} custom-call(f32[4,128,128]{2,1,0:T(8,128)S(1)} %get-tuple-element.144), custom_call_target="InvertDiagBlocksLowerTriangular" | custom-call | tf_op jit(solution)/shard_map/jit(_solve_triangular)/triangular_solve | solution.py:111
  (84 shorter events, 19.8 us)
Async XLA Ops:
  7.2 208.3 %copy-start = (f32[32]{0:T(128)S(1)}, f32[32]{0:T(128)}, u32[]{:S(2)}) copy-start(f32[32]{0:T(128)} %param.12) | copy-start | bytes 388
  7.2 1.8 copy-start.2
  7.2 156.8 %all-reduce.4.cloned.1.call-start = ((), (), s32[]{:S(2)}) async-start(), calls=%async_computation | async-start | bytes 2097152 | tf_op jit(solution)/shard_map/psum | solution.py:14
  9.0 365.6 %all-reduce.6.cloned.1.call-start = ((), (), s32[]{:S(2)}) async-start(), calls=%async_computation.1 | async-start | bytes 2097152 | tf_op jit(solution)/shard_map/psum | solution.py:108
  164.1 4.6 copy-start.3
  180.4 4.6 copy-start.3
  196.7 4.6 copy-start.3
  374.6 1.8 copy-start.1
Sparse Core Ops, SparseCore 0:
  13.4 150.5 all-reduce.3
  215.5 159.0 all-reduce.5
where the time goes:
time: 529 us; the launch traced here: 518 us
  waiting for transfers between devices  236 us (45%)
  other arithmetic  126 us (24%)
  blocking collectives  75.8 us (14%)
  matrix products  49.4 us (9%)
  between operations  18.6 us (4%)
  local copies, waits for them, and re-layouts  12.5 us (2%)
    psum x1, waiting for transfers between devices, spread(): return lax.psum(jnp.where(mine, value, jnp.zeros_like(value)), axis)  153 us
    psum x1, waiting for transfers between devices, per_device(): gram, rhs = lax.psum((gram, rhs), ('rows', 'grp'))  83.1 us
    another operation x14, other arithmetic, per_device(): lower = jnp.linalg.cholesky(gram)  78.6 us
    psum x1, blocking collectives, per_device(): gram, rhs = lax.psum((gram, rhs), ('rows', 'grp'))  75.8 us
    another operation x4, other arithmetic, per_device(): projected = jax.scipy.linalg.solve_triangular(lower, rhs, lower=True)  40.4 us
    dot_general x4, matrix products, gram_terms(): lax.dot_general(design_rows, design_rows, (((0,), (0,)), ((), ())), preci...  21.4 us
    dot_general x3, matrix products, panel_block(): jnp.einsum('cad,pd->cap', derivs, panel, preferred_element_type=jnp.float32)  11.2 us
  transfers between devices with their start and end apart: 2, of which 2 were waited for; matrix products, arithmetic and copies ran while one was open for 0% of the time, Pallas kernels for 0%

commit v1 on v0

v1 whole, which is shorter than its diff:
```python
import functools
import math

import jax
import jax.numpy as jnp
from jax import lax
from jax.experimental import pallas as pl
from jax.experimental.pallas import tpu as pltpu
from jax.sharding import PartitionSpec as P

TILE = 128
GROUP = 32


def spread_lane(value, lane):
    return jnp.broadcast_to(value[:, lane : lane + 1], value.shape)


def spread_row(value, row):
    return jnp.broadcast_to(value[row : row + 1, :], value.shape)


def inverse_of(value):
    guess = pl.reciprocal(value, approx=True)
    guess = guess * (2.0 - value * guess)
    return guess * (2.0 - value * guess)


def inverse_root(value):
    guess = lax.rsqrt(value)
    return guess * (1.5 - 0.5 * value * guess * guess)


def factor_group(rows, first):
    groups = GROUP // 8
    sub = lax.broadcasted_iota(jnp.int32, (8, TILE), 0)
    columns = [
        [spread_lane(rows[s][0], first + j) if s >= j // 8 else None for s in range(groups)]
        for j in range(GROUP)
    ]
    pivots = [jnp.ones((8, TILE), jnp.float32) for _ in range(groups)]
    for k in range(0, GROUP, 2):
        s0, r0, r1 = k // 8, k % 8, k % 8 + 1
        one, two = columns[k], columns[k + 1]
        a = spread_row(one[s0], r0)
        b = spread_row(one[s0], r1)
        c = spread_row(two[s0], r1)
        det = a * c - b * b
        inv_a = inverse_of(a)
        inv_det = inverse_of(det)
        ratio = b * inv_a
        inv_s = a * inv_det
        live = range(s0, groups)
        two_next = {s: two[s] - one[s] * ratio for s in live}
        m1 = {s: one[s] * inv_a for s in live}
        m2 = {s: two_next[s] * inv_s for s in live}
        for j in range(k + 2, GROUP):
            sj, rj = j // 8, j % 8
            u1 = spread_row(one[sj], rj)
            u2 = spread_row(two[sj], rj) - u1 * ratio
            for s in range(sj, groups):
                columns[j][s] = columns[j][s] - m1[s] * u1 - m2[s] * u2
        pivots[s0] = jnp.where(sub == r0, a, jnp.where(sub == r1, det * inv_a, pivots[s0]))
        m1[s0] = jnp.where(sub > r0, m1[s0], 0.0)
        m2[s0] = jnp.where(sub > r1, m2[s0], 0.0)
        for t in range(len(rows[0])):
            x1 = spread_row(rows[s0][t], r0)
            x2 = spread_row(rows[s0][t], r1) - x1 * ratio
            for s in live:
                rows[s][t] = rows[s][t] - m1[s] * x1 - m2[s] * x2
    scales = [inverse_root(value) for value in pivots]
    return [[piece * scales[s] for piece in rows[s]] for s in range(groups)]


def factor_kernel(core_ref, own_ref, other_ref, factor_ref, solved_ref, work, done, slabs):
    points = factor_ref.shape[0]
    tiles = points // TILE
    half = own_ref.shape[0]
    core = core_ref[0]
    slabs[pl.ds(pl.multiple_of(core * half, half), half), :] = own_ref[...]
    slabs[pl.ds(pl.multiple_of((1 - core) * half, half), half), :] = other_ref[...]
    for t in range(tiles):
        line = slabs[points - tiles + t : points - tiles + t + 1, :]
        work[t * TILE : (t + 1) * TILE, points:] = jnp.transpose(
            jnp.broadcast_to(line, (TILE, TILE))
        )
    for t in range(tiles):
        work[:, t * TILE : (t + 1) * TILE] = slabs[t * points : (t + 1) * points, :]
    lane = lax.broadcasted_iota(jnp.int32, (8, TILE), 1)
    sub = lax.broadcasted_iota(jnp.int32, (8, TILE), 0)

    def take_off(at, count, first, last):
        if last > first:
            left = at - at % TILE
            work[at : at + count, left:] -= lax.dot_general(
                done[first:last, at : at + count],
                done[first:last, left:],
                (((0,), (0,)), ((), ())),
                precision=lax.Precision.HIGHEST,
                preferred_element_type=jnp.float32,
            )

    for start in range(0, points, GROUP):
        top = start - start % TILE
        follow = start + GROUP
        if follow % TILE:
            take_off(follow, GROUP, top, start)
        elif follow < points:
            take_off(follow, TILE, 0, start)
        count = tiles - top // TILE + 1
        rows = []
        for s in range(GROUP // 8):
            at = start + s * 8
            rows.append(
                [work[at : at + 8, top + t * TILE : top + (t + 1) * TILE] for t in range(count)]
            )
            diagonal = lane == sub + (at - top)
            rows[s][0] = rows[s][0] + jnp.where(diagonal, ridge_total, 0.0)
        rows = factor_group(rows, start - top)
        for s in range(GROUP // 8):
            at = start + s * 8
            rows[s][0] = jnp.where(lane >= sub + (at - top), rows[s][0], 0.0)
            for t in range(count):
                done[at : at + 8, top + t * TILE : top + (t + 1) * TILE] = rows[s][t]
            for t in range(tiles):
                own = t - top // TILE
                factor_ref[at : at + 8, t * TILE : (t + 1) * TILE] = (
                    rows[s][own] if own >= 0 else jnp.zeros((8, TILE), jnp.float32)
                )
        if follow % TILE:
            take_off(follow, GROUP, start, follow)
        elif follow < points:
            take_off(follow, GROUP, start, follow)
            take_off(follow + GROUP, TILE - GROUP, start, follow)
    for t in range(tiles):
        flipped = jnp.transpose(done[t * TILE : (t + 1) * TILE, points:])
        solved_ref[t : t + 1, :] = flipped[0:1, :]


def factor_and_solve(core, own, other, points):
    tiles = points // TILE
    return pl.pallas_call(
        factor_kernel,
        out_shape=(
            jax.ShapeDtypeStruct((points, points), jnp.float32),
            jax.ShapeDtypeStruct((tiles, TILE), jnp.float32),
        ),
        in_specs=[
            pl.BlockSpec(memory_space=pltpu.SMEM),
            pl.BlockSpec(memory_space=pltpu.VMEM),
            pl.BlockSpec(memory_space=pltpu.VMEM),
        ],
        out_specs=(pl.BlockSpec(memory_space=pltpu.VMEM),) * 2,
        scratch_shapes=[
            pltpu.VMEM((points, points + TILE), jnp.float32),
            pltpu.VMEM((points, points + TILE), jnp.float32),
            pltpu.VMEM((points * tiles, TILE), jnp.float32),
        ],
        compiler_params=pltpu.CompilerParams(vmem_limit_bytes=32 * 1024 * 1024),
        name="factor_and_solve",
    )(core, own, other)

exact_mode = lax.Precision.HIGHEST


def against(left, right, precision=None):
    return lax.dot_general(
        left,
        right,
        (((1,), (1,)), ((), ())),
        precision=precision,
        preferred_element_type=jnp.float32,
    )


def split(value):
    high = value.astype(jnp.bfloat16)
    return high, (value - high.astype(jnp.float32)).astype(jnp.bfloat16)


def gram_kernel(
    scale, weight, info_ref, sizes_ref, energies_ref, own_ref, other_ref, atoms_ref, derivs_ref,
    forces_ref, slabs_ref, panel_ref, square, cross, rhs_part, energy_part,
):
    step = pl.program_id(0)
    points = panel_ref.shape[0]
    block_rows = atoms_ref.shape[0]
    slots = sizes_ref.shape[1]
    half = points // 2

    @pl.when(step == 0)
    def _():
        core = info_ref[2]
        panel_ref[pl.ds(pl.multiple_of(core * half, half), half), :] = own_ref[...]
        panel_ref[pl.ds(pl.multiple_of((1 - core) * half, half), half), :] = other_ref[...]
        square[...] = jnp.zeros_like(square)
        cross[...] = jnp.zeros_like(cross)
        rhs_part[...] = jnp.zeros_like(rhs_part)
        energy_part[...] = jnp.zeros_like(energy_part)

    @pl.when(step < info_ref[1])
    def _():
        panel = panel_ref[...]
        before = lax.broadcasted_iota(jnp.int32, (slots, slots), 1)
        after = lax.broadcasted_iota(jnp.int32, (slots, slots), 0)
        wide = jnp.broadcast_to(sizes_ref[...], (slots, slots))
        ends = jnp.sum(jnp.where(before <= after, wide, 0), axis=1, keepdims=True)
        starts = jnp.sum(jnp.where(before < after, wide, 0), axis=1, keepdims=True)
        slot = step * block_rows + lax.broadcasted_iota(jnp.int32, (slots, block_rows), 1)
        member = jnp.where((slot >= starts) & (slot < ends), 1.0, 0.0).astype(jnp.bfloat16)
        atom = step * block_rows + lax.broadcasted_iota(jnp.int32, (1, block_rows), 1)
        live = jnp.where(atom < info_ref[0], 1.0, 0.0)
        scores = against(panel, atoms_ref[...])
        squares = scores * scores
        high, low = split(squares * squares)
        energy_part[...] += against(high, member) + against(low, member)
        cubes = squares * scores * (live * (-4.0 * weight * scale**4))
        highs, lows = [], []
        rhs = None
        for c in range(3):
            slopes = against(panel, derivs_ref[c])
            design = cubes * slopes
            high, low = split(design)
            highs.append(high)
            lows.append(low)
            term = design * forces_ref[c : c + 1, :]
            rhs = term if rhs is None else rhs + term
        folded = rhs[:, :TILE]
        for t in range(1, block_rows // TILE):
            folded = folded + rhs[:, t * TILE : (t + 1) * TILE]
        rhs_part[...] += folded
        high = jnp.concatenate(highs, axis=1)
        low = jnp.concatenate(lows, axis=1)
        square[:half, :] += against(high[:half], high)
        square[half:, half:] += against(high[half:], high[half:])
        cross[...] += against(high, low)

    @pl.when(step == pl.num_programs(0) - 1)
    def _():
        norms = jnp.sqrt(jnp.maximum(sizes_ref[...], 1).astype(jnp.float32))
        energy_ratio = energy_part[...] / norms
        energy_rows = energy_ratio * (weight * scale**4)
        gram = square[...] + cross[...] + jnp.transpose(cross[...])
        gram = gram + against(energy_rows, energy_rows, exact_mode)
        for t in range(points // TILE):
            slabs_ref[t * points : (t + 1) * points, :] = gram[:, t * TILE : (t + 1) * TILE]
        ones = jnp.ones((8, TILE), jnp.float32)
        rhs = against(ones, rhs_part[...], exact_mode)
        rhs = rhs + against(
            jnp.broadcast_to(energies_ref[...], (8, slots)), energy_ratio, exact_mode
        )
        tiles = points // TILE
        for t in range(tiles):
            at = points - tiles + t
            slabs_ref[at : at + 1, :] = rhs[0:1, t * TILE : (t + 1) * TILE]


def gram_slabs(
    core, own, other, atoms, derivs, forces, energies, sizes, scale, weight, block_rows=512
):
    capacity, width = atoms.shape
    points = 2 * own.shape[0]
    slots = sizes.shape[0]
    total = jnp.sum(sizes)
    blocks = lax.div(total + (block_rows - 1), block_rows)
    info = jnp.stack([total, blocks, core]).astype(jnp.int32)

    def row_block(i, info):
        return jnp.minimum(i, info[1] - 1)

    return pl.pallas_call(
        functools.partial(gram_kernel, scale, weight),
        out_shape=jax.ShapeDtypeStruct((points * points // TILE, TILE), jnp.float32),
        grid_spec=pltpu.PrefetchScalarGridSpec(
            num_scalar_prefetch=1,
            grid=(capacity // block_rows,),
            in_specs=[
                pl.BlockSpec((1, slots), lambda i, info: (0, 0)),
                pl.BlockSpec((1, slots), lambda i, info: (0, 0)),
                pl.BlockSpec((points // 2, width), lambda i, info: (0, 0)),
                pl.BlockSpec((points // 2, width), lambda i, info: (0, 0)),
                pl.BlockSpec((block_rows, width), lambda i, info: (row_block(i, info), 0)),
                pl.BlockSpec((3, block_rows, width), lambda i, info: (0, row_block(i, info), 0)),
                pl.BlockSpec((3, block_rows), lambda i, info: (0, row_block(i, info))),
            ],
            out_specs=pl.BlockSpec(
                (points * points // TILE, TILE), lambda i, info: (0, 0)
            ),
            scratch_shapes=[
                pltpu.VMEM((points, width), jnp.bfloat16),
                pltpu.VMEM((points, points), jnp.float32),
                pltpu.VMEM((points, points), jnp.float32),
                pltpu.VMEM((points, TILE), jnp.float32),
                pltpu.VMEM((points, slots), jnp.float32),
            ],
        ),
        compiler_params=pltpu.CompilerParams(vmem_limit_bytes=48 * 1024 * 1024),
        name="gram_slabs",
    )(
        info,
        sizes.reshape(1, slots),
        (energies * (weight * scale**4)).reshape(1, slots),
        own,
        other,
        atoms,
        derivs,
        forces.astype(jnp.float32),
    )
CHIPS = ("rows", "z")
ridge_total = 1.0


def exchange(pieces, axes):
    return lax.all_to_all(pieces, axes, 0, 0, tiled=True)


def swap(value):
    return lax.ppermute(value, "core", [(0, 1), (1, 0)])


def panel_halves(panels, owner):
    core = lax.axis_index("core")
    chips = lax.axis_size(CHIPS)
    points, width = panels.shape
    half = points // 2
    near = lax.dynamic_slice_in_dim(panels, core * half, half, 0)
    far = swap(lax.dynamic_slice_in_dim(panels, (1 - core) * half, half, 0))
    held = jnp.where(lax.rem(owner, 2) == core, near, far)
    tall = half // 8
    wide = chips // tall
    cut = held.reshape(tall, 8, wide, width // wide).transpose(0, 2, 1, 3)
    pieces = exchange(cut.reshape(chips, 8, width // wide), CHIPS)
    piece = lax.dynamic_index_in_dim(pieces, lax.div(owner, 2), 0, keepdims=True)
    own = exchange(jnp.broadcast_to(piece, pieces.shape), CHIPS)
    own = own.reshape(tall, wide, 8, width // wide).transpose(0, 2, 1, 3).reshape(half, width)
    return own, swap(own)


def sum_halves(value):
    chips = lax.axis_size(CHIPS)
    lanes = value.shape[1]
    pair = exchange(value.reshape(2, -1, lanes), "core")
    pieces = exchange(jnp.sum(pair, axis=0).reshape(chips, -1, lanes), CHIPS)
    piece = jnp.sum(pieces, axis=0, keepdims=True)
    own = exchange(jnp.broadcast_to(piece, pieces.shape), CHIPS).reshape(-1, lanes)
    return own, swap(own)


def per_device(
    descriptors, derivatives, force_targets, energies, struct_atoms, sparse_points, owner
):
    capacity, width = descriptors.shape
    points = sparse_points.shape[1]
    own, other = panel_halves(sparse_points[0], owner[0])
    core = lax.axis_index("core")
    sizes = lax.dynamic_index_in_dim(
        struct_atoms, 2 * lax.axis_index(CHIPS) + core, 0, keepdims=False
    )
    scale = 1.0 / math.sqrt(width)
    weight = 1.0 / math.sqrt(48.0 * capacity * lax.axis_size(("rows", "z", "core")))
    slabs = gram_slabs(
        core, own, other, descriptors, derivatives, force_targets, energies, sizes, scale, weight
    )
    own, other = sum_halves(slabs)
    factor, solved = factor_and_solve(core.reshape(1), own, other, points)
    return (factor, solved.reshape(points))


def solution(mesh):
    rows, group = mesh.devices.shape
    chips = jax.sharding.Mesh(
        mesh.devices.reshape(rows, group // 2, 2), ("rows", "z", "core")
    )
    every = ("rows", "z", "core")
    in_specs = (
        P(every, None),
        P(None, every, None),
        P(None, every),
        P(every),
        P(),
        P(every, None, None),
        P(),
    )
    out_specs = (P(), P())
    return jax.shard_map(
        per_device, mesh=chips, in_specs=in_specs, out_specs=out_specs, check_vma=False
    )
```

time: 529 us -> 134 us (0.25); the launches traced: 518 us -> 133 us
  waiting for transfers between devices: 236 us -> 14.6 us
  other arithmetic: 126 us -> 5.74 us
  matrix products: 49.4 us -> 0 us
  Pallas kernels: 0 us -> 26.8 us
  starting transfers between devices: 0.08 us -> 19.1 us
  between operations: 18.6 us -> 2.01 us
  blocking collectives: 75.8 us -> 63.2 us
  local copies, waits for them, and re-layouts: 12.5 us -> 1.23 us
    psum x2 -> x0, waiting for transfers between devices: 236 us -> none  [the longest x1 153 us: spread(): return lax.psum(jnp.where(mine, value, jnp.zeros_like(value)), axis)]
    another operation x18 -> x1, other arithmetic: 119 us -> 0.72 us  [gram_slabs(): info = jnp.stack([total, blocks, core]).astype(jnp.int32)]
    psum x1 -> x0, blocking collectives: 75.8 us -> none  [per_device(): gram, rhs = lax.psum((gram, rhs), ('rows', 'grp'))]
    all_to_all x0 -> x4, blocking collectives: none -> 63.2 us  [exchange(): return lax.all_to_all(pieces, axes, 0, 0, tiled=True)]
    dot_general x17 -> x0, matrix products: 46.1 us -> none  [the longest x4 21.4 us: gram_terms(): lax.dot_general(design_rows, design_rows, (((0,), (0,)), ((), ())), preci...]
    pallas_call x0 -> x2, Pallas kernels: none -> 26.8 us  [the longest x1 18 us: factor_and_solve(): pl.pallas_call(factor_kernel, out_shape=(jax.ShapeDtypeStruct((points, po...]
    all_to_all x0 -> x1, waiting for transfers between devices: none -> 12.2 us  [exchange(): return lax.all_to_all(pieces, axes, 0, 0, tiled=True)]
    all_to_all x0 -> x1, starting transfers between devices: none -> 11.2 us  [exchange(): return lax.all_to_all(pieces, axes, 0, 0, tiled=True)]
  transfers between devices with their start and end apart: 2 -> 4, of which waited for: 2 -> 3; matrix products, arithmetic and copies ran while one was open for 0% -> 3% of each run, Pallas kernels for 0% -> 0%
where the time goes in v1:
time: 134 us; the launch traced here: 133 us
  blocking collectives  63.2 us (47%)
  Pallas kernels  26.8 us (20%)
  starting transfers between devices  19.1 us (14%)
  waiting for transfers between devices  14.6 us (11%)
  other arithmetic  5.74 us (4%)
  between operations  2.01 us (1%)
    all_to_all x4, blocking collectives, exchange(): return lax.all_to_all(pieces, axes, 0, 0, tiled=True)  63.2 us
    pallas_call x1, Pallas kernels, factor_and_solve(): pl.pallas_call(factor_kernel, out_shape=(jax.ShapeDtypeStruct((points, po...  18 us
    all_to_all x1, waiting for transfers between devices, exchange(): return lax.all_to_all(pieces, axes, 0, 0, tiled=True)  12.2 us
    all_to_all x1, starting transfers between devices, exchange(): return lax.all_to_all(pieces, axes, 0, 0, tiled=True)  11.2 us
    pallas_call x1, Pallas kernels, gram_slabs(): pl.pallas_call(functools.partial(gram_kernel, scale, weight), out_shape=j...  8.8 us
    ppermute x3, starting transfers between devices, swap(): return lax.ppermute(value, 'core', [(0, 1), (1, 0)])  7.89 us
  transfers between devices with their start and end apart: 4, of which 3 were waited for; matrix products, arithmetic and copies ran while one was open for 3% of the time, Pallas kernels for 0%

profile of v1, /device:TPU:1, one launch (start us, length us, event | category | flops | bytes accessed | tf_op | source)
XLA Modules:
  0.0 132.8 jit_solution(7857060164330718705)
XLA Ops:
  0.6 1.1 dynamic-slice_bitcast_fusion
  1.7 1.5 %collective-permute-start = (bf16[256,1024]{1,0:T(8,128)(2,1)S(1)}, bf16[256,1024]{1,0:T(8,128)(2,1)S(1)}, u32[]{:S(2)}, u32[]{:S(2)}) collective-permute-start(bf16[256,1024]{1,0:T(8,128)(2,1)S(1)} %dynamic-slice_bitcast_fusion), channel_id=1, source_target_pairs={{0,1},{1,0},{2,3},{3,2},{4,5},{5,4},{6,7},{7,6},{8,9},{9,8},{10,11... | collective-permute-start | bytes 1572872 | tf_op jit(solution)/shard_map/ppermute | solution.py:318
  3.9 0.9 collective-permute-done
  4.8 2.0 %bitcast_select_fusion = bf16[256,1024]{1,0:T(8,128)(2,1)} fusion(bf16[256,1024]{1,0:T(8,128)(2,1)S(1)} %collective-permute-done, bf16[1,512,1024]{2,1,0:T(8,128)(2,1)} %param.12, s32[]{:T(128)S(6)} %select_n.24, pred[]{:T(512)S(6)} %eq.3), kind=kLoop, calls=%fused_computation | loop fusion | flops 262144 | bytes 1572869 | tf_op jit(solution)/shard_map/jit(_where)/select_n | solution.py:328
  6.8 11.2 %all-to-all-start = ((bf16[64,8,512]{2,1,0:T(8,128)(2,1)}), bf16[64,8,512]{2,1,0:T(8,128)(2,1)S(1)}, u32[]{:S(2)}, u32[]{:S(2)}) async-start(bf16[64,8,512]{2,1,0:T(8,128)(2,1)} %bitcast.9), calls=%async_computation | async-start | bytes 1048576 | tf_op jit(solution)/shard_map/all_to_all | solution.py:314
  18.0 12.2 %all-to-all-done = bf16[64,8,512]{2,1,0:T(8,128)(2,1)S(1)} async-done(((bf16[64,8,512]{2,1,0:T(8,128)(2,1)}), bf16[64,8,512]{2,1,0:T(8,128)(2,1)S(1)}, u32[]{:S(2)}, u32[]{:S(2)}) %all-to-all-start) | async-done | bytes 524320 | tf_op jit(solution)/shard_map/all_to_all | solution.py:314
  30.3 15.5 %all_to_all.25 = bf16[64,8,512]{2,1,0:T(8,128)(2,1)S(1)} all-to-all(bf16[64,8,512]{2,1,0:T(8,128)(2,1)S(1)} %broadcast_in_dim.14), channel_id=1, replica_groups=mesh['rows'=16,'z'=4,'core'=2] {'rows','z'}, dimensions={0} | all-to-all | bytes 1048576 | tf_op jit(solution)/shard_map/all_to_all | solution.py:314
  45.8 3.2 %collective-permute-start.1 = (bf16[256,1024]{1,0:T(8,128)(2,1)S(1)}, bf16[256,1024]{1,0:T(8,128)(2,1)S(1)}, u32[]{:S(2)}, u32[]{:S(2)}) collective-permute-start(bf16[256,1024]{1,0:T(8,128)(2,1)S(1)} %bitcast.30), channel_id=1, source_target_pairs={{0,1},{1,0},{2,3},{3,2},{4,5},{5,4},{6,7},{7,6},{8,9},{9,8},{10,11... | collective-permute-start | bytes 1572872 | tf_op jit(solution)/shard_map/ppermute | solution.py:318
  49.0 1.4 %fusion = (s32[]{:T(128)}, s32[1,32]{0,1:T(8,128)S(1)}) fusion(s32[128,32]{0,1:T(8,128)} %param.11, s32[]{:T(128)S(6)} %select_n.22), kind=kLoop, calls=%fused_computation.6 | loop fusion | flops 31 | bytes 264 | tf_op jit(solution)/shard_map/reduce_sum | solution.py:264
  51.1 0.1 copy.11.sizes_ref
  51.2 0.7 convert_element_type.3.forces_ref
  51.9 0.7 pad_add_fusion.info_ref
  52.6 0.7 multiply_bitcast_fusion.energies_ref
  53.3 0.0 collective-permute-done.1.other_ref
  53.3 8.8 %gram_slabs.1 = f32[2048,128]{1,0:T(8,128)S(1)} custom-call(s32[3]{0:T(128)S(1)} %pad_add_fusion.info_ref, s32[1,32]{1,0:T(1,128)S(1)} %copy.11.sizes_ref, f32[1,32]{1,0:T(1,128)S(1)} %multiply_bitcast_fusion.energies_ref, bf16[256,1024]{1,0:T(8,128)(2,1)S(1)} %bitcast.31, bf16[256,1024]{1,0:T(8,128)(2,1)S(1)} %collective-permute-done.1.other_ref, ...), custom_call_target="tpu_custom_call" | custom-call | tf_op jit(solution)/shard_map/gram_slabs/pallas_call | solution.py:271
  62.1 8.4 %all_to_all.26 = f32[2,1024,128]{2,1,0:T(8,128)S(1)} all-to-all(f32[2,1024,128]{2,1,0:T(8,128)S(1)} %bitcast.29), channel_id=1, replica_groups=mesh['rows'=16,'z'=4,'core'=2] {'core'}, dimensions={0} | all-to-all | bytes 2097152 | tf_op jit(solution)/shard_map/all_to_all | solution.py:314
  70.5 0.1 reduce_sum.28
  70.6 23.7 %all_to_all.27 = f32[64,16,128]{2,1,0:T(8,128)S(1)} all-to-all(f32[64,16,128]{2,1,0:T(8,128)S(1)} %bitcast.34), channel_id=1, replica_groups=mesh['rows'=16,'z'=4,'core'=2] {'rows','z'}, dimensions={0} | all-to-all | bytes 1048576 | tf_op jit(solution)/shard_map/all_to_all | solution.py:314
  94.4 0.1 reduce_sum.29
  94.5 15.5 %all_to_all.28 = f32[64,16,128]{2,1,0:T(8,128)S(1)} all-to-all(f32[64,16,128]{2,1,0:T(8,128)S(1)} %broadcast_in_dim.15), channel_id=1, replica_groups=mesh['rows'=16,'z'=4,'core'=2] {'rows','z'}, dimensions={0} | all-to-all | bytes 1048576 | tf_op jit(solution)/shard_map/all_to_all | solution.py:314
  110.0 3.2 %collective-permute-start.2 = (f32[1024,128]{1,0:T(8,128)S(1)}, f32[1024,128]{1,0:T(8,128)S(1)}, u32[]{:S(2)}, u32[]{:S(2)}) collective-permute-start(f32[1024,128]{1,0:T(8,128)S(1)} %bitcast.32), channel_id=1, source_target_pairs={{0,1},{1,0},{2,3},{3,2},{4,5},{5,4},{6,7},{7,6},{8,9},{9,8},{10,11... | collective-permute-start | bytes 1572872 | tf_op jit(solution)/shard_map/ppermute | solution.py:318
  113.2 1.5 %collective-permute-done.2.other_ref = f32[1024,128]{1,0:T(8,128)S(1)} collective-permute-done((f32[1024,128]{1,0:T(8,128)S(1)}, f32[1024,128]{1,0:T(8,128)S(1)}, u32[]{:S(2)}, u32[]{:S(2)}) %collective-permute-start.2) | collective-permute-done | bytes 524320 | tf_op jit(solution)/shard_map/ppermute | solution.py:318
  114.7 18.0 %factor_and_solve.1 = (f32[512,512]{1,0:T(8,128)}, f32[4,128]{1,0:T(4,128)}) custom-call(s32[1]{0:T(128)} %bitcast.core_ref, f32[1024,128]{1,0:T(8,128)S(1)} %bitcast.33, f32[1024,128]{1,0:T(8,128)S(1)} %collective-permute-done.2.other_ref), custom_call_target="tpu_custom_call" | custom-call | tf_op jit(solution)/shard_map/factor_and_solve/pallas_call | solution.py:142
  (3 shorter events, 0.1 us)
Async XLA Ops:
  1.7 3.0 %collective-permute-start = (bf16[256,1024]{1,0:T(8,128)(2,1)S(1)}, bf16[256,1024]{1,0:T(8,128)(2,1)S(1)}, u32[]{:S(2)}, u32[]{:S(2)}) collective-permute-start(bf16[256,1024]{1,0:T(8,128)(2,1)S(1)} %dynamic-slice_bitcast_fusion), channel_id=1, source_target_pairs={{0,1},{1,0},{2,3},{3,2},{4,5},{5,4},{6,7},{7,6},{8,9},{9,8},{10,11... | collective-permute-start | bytes 1572872 | tf_op jit(solution)/shard_map/ppermute | solution.py:318
  6.8 23.5 %all-to-all-start = ((bf16[64,8,512]{2,1,0:T(8,128)(2,1)}), bf16[64,8,512]{2,1,0:T(8,128)(2,1)S(1)}, u32[]{:S(2)}, u32[]{:S(2)}) async-start(bf16[64,8,512]{2,1,0:T(8,128)(2,1)} %bitcast.9), calls=%async_computation | async-start | bytes 1048576 | tf_op jit(solution)/shard_map/all_to_all | solution.py:314
  45.8 7.5 %collective-permute-start.1 = (bf16[256,1024]{1,0:T(8,128)(2,1)S(1)}, bf16[256,1024]{1,0:T(8,128)(2,1)S(1)}, u32[]{:S(2)}, u32[]{:S(2)}) collective-permute-start(bf16[256,1024]{1,0:T(8,128)(2,1)S(1)} %bitcast.30), channel_id=1, source_target_pairs={{0,1},{1,0},{2,3},{3,2},{4,5},{5,4},{6,7},{7,6},{8,9},{9,8},{10,11... | collective-permute-start | bytes 1572872 | tf_op jit(solution)/shard_map/ppermute | solution.py:318
  110.0 4.7 %collective-permute-start.2 = (f32[1024,128]{1,0:T(8,128)S(1)}, f32[1024,128]{1,0:T(8,128)S(1)}, u32[]{:S(2)}, u32[]{:S(2)}) collective-permute-start(f32[1024,128]{1,0:T(8,128)S(1)} %bitcast.32), channel_id=1, source_target_pairs={{0,1},{1,0},{2,3},{3,2},{4,5},{5,4},{6,7},{7,6},{8,9},{9,8},{10,11... | collective-permute-start | bytes 1572872 | tf_op jit(solution)/shard_map/ppermute | solution.py:318

commit v2 on v1

--- a/solution.py
+++ b/solution.py
@@ -21,14 +21,17 @@
 
 
 def inverse_of(value):
-    guess = pl.reciprocal(value, approx=True)
-    guess = guess * (2.0 - value * guess)
-    return guess * (2.0 - value * guess)
-
-
-def inverse_root(value):
-    guess = lax.rsqrt(value)
-    return guess * (1.5 - 0.5 * value * guess * guess)
+    return pltpu.reciprocal(value, approx=True)
+
+
+def packed_blocks(tiles):
+    return [(p, t) for p in range(tiles) for t in range(p, tiles)]
+
+
+def packed_rows(points, devices):
+    tiles = points // TILE
+    rows = len(packed_blocks(tiles)) * TILE + tiles
+    return -(-rows // devices) * devices
 
 
 def factor_group(rows, first):
@@ -68,24 +71,27 @@
             x2 = spread_row(rows[s0][t], r1) - x1 * ratio
             for s in live:
                 rows[s][t] = rows[s][t] - m1[s] * x1 - m2[s] * x2
-    scales = [inverse_root(value) for value in pivots]
+    scales = [lax.rsqrt(value) for value in pivots]
     return [[piece * scales[s] for piece in rows[s]] for s in range(groups)]
 
 
-def factor_kernel(core_ref, own_ref, other_ref, factor_ref, solved_ref, work, done, slabs):
+def factor_kernel(core_ref, own_ref, other_ref, factor_ref, solved_ref, work, done, packed):
     points = factor_ref.shape[0]
     tiles = points // TILE
     half = own_ref.shape[0]
     core = core_ref[0]
-    slabs[pl.ds(pl.multiple_of(core * half, half), half), :] = own_ref[...]
-    slabs[pl.ds(pl.multiple_of((1 - core) * half, half), half), :] = other_ref[...]
+    packed[pl.ds(pl.multiple_of(core * half, 8), half), :] = own_ref[...]
+    packed[pl.ds(pl.multiple_of((1 - core) * half, 8), half), :] = other_ref[...]
+    blocks = packed_blocks(tiles)
+    for n, (p, t) in enumerate(blocks):
+        work[p * TILE : (p + 1) * TILE, t * TILE : (t + 1) * TILE] = packed[
+            n * TILE : (n + 1) * TILE, :
+        ]
     for t in range(tiles):
-        line = slabs[points - tiles + t : points - tiles + t + 1, :]
+        at = len(blocks) * TILE + t
         work[t * TILE : (t + 1) * TILE, points:] = jnp.transpose(
-            jnp.broadcast_to(line, (TILE, TILE))
+            jnp.broadcast_to(packed[at : at + 1, :], (TILE, TILE))
         )
-    for t in range(tiles):
-        work[:, t * TILE : (t + 1) * TILE] = slabs[t * points : (t + 1) * points, :]
     lane = lax.broadcasted_iota(jnp.int32, (8, TILE), 1)
     sub = lax.broadcasted_iota(jnp.int32, (8, TILE), 0)
 
@@ -154,7 +160,7 @@
         scratch_shapes=[
             pltpu.VMEM((points, points + TILE), jnp.float32),
             pltpu.VMEM((points, points + TILE), jnp.float32),
-            pltpu.VMEM((points * tiles, TILE), jnp.float32),
+            pltpu.VMEM((2 * own.shape[0], TILE), jnp.float32),
         ],
         compiler_params=pltpu.CompilerParams(vmem_limit_bytes=32 * 1024 * 1024),
         name="factor_and_solve",
@@ -180,7 +186,7 @@
 
 def gram_kernel(
     scale, weight, info_ref, sizes_ref, energies_ref, own_ref, other_ref, atoms_ref, derivs_ref,
-    forces_ref, slabs_ref, panel_ref, square, cross, rhs_part, energy_part,
+    forces_ref, keep_ref, send_ref, panel_ref, square, cross, rhs_part, energy_part, packed,
 ):
     step = pl.program_id(0)
     points = panel_ref.shape[0]
@@ -211,26 +217,26 @@
         atom = step * block_rows + lax.broadcasted_iota(jnp.int32, (1, block_rows), 1)
         live = jnp.where(atom < info_ref[0], 1.0, 0.0)
         scores = against(panel, atoms_ref[...])
+        slopes = against(panel, derivs_ref[0])
         squares = scores * scores
-        high, low = split(squares * squares)
-        energy_part[...] += against(high, member) + against(low, member)
+        kernel_high, kernel_low = split(squares * squares)
         cubes = squares * scores * (live * (-4.0 * weight * scale**4))
-        highs, lows = [], []
-        rhs = None
+        grams = []
+        folded = rhs_part[...]
         for c in range(3):
-            slopes = against(panel, derivs_ref[c])
             design = cubes * slopes
+            if c < 2:
+                slopes = against(panel, derivs_ref[c + 1])
+            else:
+                energy_part[...] += against(kernel_high, member) + against(kernel_low, member)
             high, low = split(design)
-            highs.append(high)
-            lows.append(low)
             term = design * forces_ref[c : c + 1, :]
-            rhs = term if rhs is None else rhs + term
-        folded = rhs[:, :TILE]
-        for t in range(1, block_rows // TILE):
-            folded = folded + rhs[:, t * TILE : (t + 1) * TILE]
-        rhs_part[...] += folded
-        high = jnp.concatenate(highs, axis=1)
-        low = jnp.concatenate(lows, axis=1)
+            for t in range(block_rows // TILE):
+                folded = folded + term[:, t * TILE : (t + 1) * TILE]
+            grams.append((high, low))
+        rhs_part[...] = folded
+        high = jnp.concatenate([pair[0] for pair in grams], axis=1)
+        low = jnp.concatenate([pair[1] for pair in grams], axis=1)
         square[:half, :] += against(high[:half], high)
         square[half:, half:] += against(high[half:], high[half:])
         cross[...] += against(high, low)
@@ -242,35 +248,42 @@
         energy_rows = energy_ratio * (weight * scale**4)
         gram = square[...] + cross[...] + jnp.transpose(cross[...])
         gram = gram + against(energy_rows, energy_rows, exact_mode)
-        for t in range(points // TILE):
-            slabs_ref[t * points : (t + 1) * points, :] = gram[:, t * TILE : (t + 1) * TILE]
+        tiles = points // TILE
+        blocks = packed_blocks(tiles)
+        for n, (p, t) in enumerate(blocks):
+            packed[n * TILE : (n + 1) * TILE, :] = gram[
+                p * TILE : (p + 1) * TILE, t * TILE : (t + 1) * TILE
+            ]
         ones = jnp.ones((8, TILE), jnp.float32)
         rhs = against(ones, rhs_part[...], exact_mode)
         rhs = rhs + against(
             jnp.broadcast_to(energies_ref[...], (8, slots)), energy_ratio, exact_mode
         )
-        tiles = points // TILE
         for t in range(tiles):
-            at = points - tiles + t
-            slabs_ref[at : at + 1, :] = rhs[0:1, t * TILE : (t + 1) * TILE]
-
-
-def gram_slabs(
-    core, own, other, atoms, derivs, forces, energies, sizes, scale, weight, block_rows=512
-):
+            at = len(blocks) * TILE + t
+            packed[at : at + 1, :] = rhs[0:1, t * TILE : (t + 1) * TILE]
+        core = info_ref[2]
+        count = keep_ref.shape[0]
+        keep_ref[...] = packed[pl.ds(pl.multiple_of(core * count, 8), count), :]
+        send_ref[...] = packed[pl.ds(pl.multiple_of((1 - core) * count, 8), count), :]
+
+
+def block_rows_of(capacity):
+    return min(512, capacity)
+
+
+def gram_halves(info, sizes, energies, own, other, atoms, derivs, forces, scale, weight, rows):
     capacity, width = atoms.shape
     points = 2 * own.shape[0]
-    slots = sizes.shape[0]
-    total = jnp.sum(sizes)
-    blocks = lax.div(total + (block_rows - 1), block_rows)
-    info = jnp.stack([total, blocks, core]).astype(jnp.int32)
+    slots = sizes.shape[1]
+    block_rows = block_rows_of(capacity)
 
     def row_block(i, info):
         return jnp.minimum(i, info[1] - 1)
 
     return pl.pallas_call(
         functools.partial(gram_kernel, scale, weight),
-        out_shape=jax.ShapeDtypeStruct((points * points // TILE, TILE), jnp.float32),
+        out_shape=(jax.ShapeDtypeStruct((rows // 2, TILE), jnp.float32),) * 2,
         grid_spec=pltpu.PrefetchScalarGridSpec(
             num_scalar_prefetch=1,
             grid=(capacity // block_rows,),
@@ -283,30 +296,21 @@
                 pl.BlockSpec((3, block_rows, width), lambda i, info: (0, row_block(i, info), 0)),
                 pl.BlockSpec((3, block_rows), lambda i, info: (0, row_block(i, info))),
             ],
-            out_specs=pl.BlockSpec(
-                (points * points // TILE, TILE), lambda i, info: (0, 0)
-            ),
+            out_specs=(pl.BlockSpec((rows // 2, TILE), lambda i, info: (0, 0)),) * 2,
             scratch_shapes=[
                 pltpu.VMEM((points, width), jnp.bfloat16),
                 pltpu.VMEM((points, points), jnp.float32),
                 pltpu.VMEM((points, points), jnp.float32),
                 pltpu.VMEM((points, TILE), jnp.float32),
                 pltpu.VMEM((points, slots), jnp.float32),
+                pltpu.VMEM((rows, TILE), jnp.float32),
             ],
         ),
-        compiler_params=pltpu.CompilerParams(vmem_limit_bytes=48 * 1024 * 1024),
-        name="gram_slabs",
-    )(
-        info,
-        sizes.reshape(1, slots),
-        (energies * (weight * scale**4)).reshape(1, slots),
-        own,
-        other,
-        atoms,
-        derivs,
-        forces.astype(jnp.float32),
-    )
+        compiler_params=pltpu.CompilerParams(vmem_limit_bytes=58 * 1024 * 1024),
+        name="gram_halves",
+    )(info, sizes, energies, own, other, atoms, derivs, forces)
 CHIPS = ("rows", "z")
+EVERY = ("rows", "z", "core")
 ridge_total = 1.0
 
 
@@ -318,31 +322,30 @@
     return lax.ppermute(value, "core", [(0, 1), (1, 0)])
 
 
-def panel_halves(panels, owner):
+def panel_halves(panels, owner, others):
     core = lax.axis_index("core")
     chips = lax.axis_size(CHIPS)
     points, width = panels.shape
     half = points // 2
-    near = lax.dynamic_slice_in_dim(panels, core * half, half, 0)
     far = swap(lax.dynamic_slice_in_dim(panels, (1 - core) * half, half, 0))
+    near = lax.optimization_barrier(lax.dynamic_slice_in_dim(panels, core * half, half, 0))
     held = jnp.where(lax.rem(owner, 2) == core, near, far)
     tall = half // 8
     wide = chips // tall
     cut = held.reshape(tall, 8, wide, width // wide).transpose(0, 2, 1, 3)
     pieces = exchange(cut.reshape(chips, 8, width // wide), CHIPS)
     piece = lax.dynamic_index_in_dim(pieces, lax.div(owner, 2), 0, keepdims=True)
+    piece, others = lax.optimization_barrier((piece, others))
     own = exchange(jnp.broadcast_to(piece, pieces.shape), CHIPS)
     own = own.reshape(tall, wide, 8, width // wide).transpose(0, 2, 1, 3).reshape(half, width)
-    return own, swap(own)
-
-
-def sum_halves(value):
+    return own, swap(own), others
+
+
+def sum_halves(keep, send):
     chips = lax.axis_size(CHIPS)
-    lanes = value.shape[1]
-    pair = exchange(value.reshape(2, -1, lanes), "core")
-    pieces = exchange(jnp.sum(pair, axis=0).reshape(chips, -1, lanes), CHIPS)
-    piece = jnp.sum(pieces, axis=0, keepdims=True)
-    own = exchange(jnp.broadcast_to(piece, pieces.shape), CHIPS).reshape(-1, lanes)
+    pair = (keep + swap(send)).reshape(chips, 1, -1)
+    piece = jnp.sum(exchange(pair, CHIPS), axis=0, keepdims=True)
+    own = exchange(jnp.broadcast_to(piece, pair.shape), CHIPS).reshape(keep.shape)
     return own, swap(own)
 
 
@@ -351,34 +354,47 @@
 ):
     capacity, width = descriptors.shape
     points = sparse_points.shape[1]
-    own, other = panel_halves(sparse_points[0], owner[0])
     core = lax.axis_index("core")
-    sizes = lax.dynamic_index_in_dim(
-        struct_atoms, 2 * lax.axis_index(CHIPS) + core, 0, keepdims=False
+    scale = 1.0 / math.sqrt(width)
+    weight = 1.0 / math.sqrt(48.0 * capacity * lax.axis_size(EVERY))
+    sizes = lax.dynamic_slice_in_dim(struct_atoms, lax.axis_index(EVERY), 1, 0)
+    total = jnp.sum(sizes)
+    block_rows = block_rows_of(capacity)
+    blocks = lax.div(total + (block_rows - 1), block_rows)
+    info = jnp.stack([total, blocks, core]).astype(jnp.int32)
+    scaled = energies[None, :] * (weight * scale**4)
+    forces = force_targets.astype(jnp.float32)
+    own, other, (info, sizes, scaled, forces) = panel_halves(
+        sparse_points[0], owner[0], (info, sizes, scaled, forces)
     )
-    scale = 1.0 / math.sqrt(width)
-    weight = 1.0 / math.sqrt(48.0 * capacity * lax.axis_size(("rows", "z", "core")))
-    slabs = gram_slabs(
-        core, own, other, descriptors, derivatives, force_targets, energies, sizes, scale, weight
+    keep, send = gram_halves(
+        info,
+        sizes,
+        scaled,
+        own,
+        other,
+        descriptors,
+        derivatives,
+        forces,
+        scale,
+        weight,
+        packed_rows(points, lax.axis_size(EVERY)),
     )
-    own, other = sum_halves(slabs)
+    own, other = sum_halves(keep, send)
     factor, solved = factor_and_solve(core.reshape(1), own, other, points)
     return (factor, solved.reshape(points))
 
 
 def solution(mesh):
     rows, group = mesh.devices.shape
-    chips = jax.sharding.Mesh(
-        mesh.devices.reshape(rows, group // 2, 2), ("rows", "z", "core")
-    )
-    every = ("rows", "z", "core")
+    chips = jax.sharding.Mesh(mesh.devices.reshape(rows, group // 2, 2), EVERY)
     in_specs = (
-        P(every, None),
-        P(None, every, None),
-        P(None, every),
-        P(every),
+        P(EVERY, None),
+        P(None, EVERY, None),
+        P(None, EVERY),
+        P(EVERY),
         P(),
-        P(every, None, None),
+        P(EVERY, None, None),
         P(),
     )
     out_specs = (P(), P())

time: 134 us -> 126 us (0.940)
  blocking collectives: 63.2 us -> 47.5 us
  Pallas kernels: 26.8 us -> 31.5 us
  starting transfers between devices: 19.1 us -> 23.5 us
  waiting for transfers between devices: 14.6 us -> 11 us
  local copies, waits for them, and re-layouts: 1.23 us -> 2.95 us
  other arithmetic: 5.74 us -> 7.25 us
    all_to_all x4 -> x3, blocking collectives: 63.2 us -> 47.5 us  [exchange(): return lax.all_to_all(pieces, axes, 0, 0, tiled=True)]
    all_to_all x1, waiting for transfers between devices: 12.2 us -> 5.77 us  [exchange(): return lax.all_to_all(pieces, axes, 0, 0, tiled=True)]
    pallas_call x1, Pallas kernels: 8.8 us -> 14.2 us  [gram_halves(): pl.pallas_call(functools.partial(gram_kernel, scale, weight), out_shape=(...]
    ppermute x3 -> x4, starting transfers between devices: 7.89 us -> 12.3 us  [swap(): return lax.ppermute(value, 'core', [(0, 1), (1, 0)])]
    ppermute x3 -> x4, waiting for transfers between devices: 2.41 us -> 5.22 us  [swap(): return lax.ppermute(value, 'core', [(0, 1), (1, 0)])]
  transfers between devices with their start and end apart: 4 -> 5, of which waited for: 3 -> 5; matrix products, arithmetic and copies ran while one was open for 3% -> 5% of each run, Pallas kernels for 0% -> 0%
where the time goes in v2:
time: 126 us
  blocking collectives  47.5 us (38%)
  Pallas kernels  31.5 us (25%)
  starting transfers between devices  23.5 us (19%)
  waiting for transfers between devices  11 us (9%)
  other arithmetic  7.25 us (6%)
  local copies, waits for them, and re-layouts  2.95 us (2%)
  between operations  2.02 us (2%)
    all_to_all x3, blocking collectives, exchange(): return lax.all_to_all(pieces, axes, 0, 0, tiled=True)  47.5 us
    pallas_call x1, Pallas kernels, factor_and_solve(): pl.pallas_call(factor_kernel, out_shape=(jax.ShapeDtypeStruct((points, po...  17.2 us
    pallas_call x1, Pallas kernels, gram_halves(): pl.pallas_call(functools.partial(gram_kernel, scale, weight), out_shape=(...  14.2 us
    ppermute x4, starting transfers between devices, swap(): return lax.ppermute(value, 'core', [(0, 1), (1, 0)])  12.3 us
    all_to_all x1, starting transfers between devices, exchange(): return lax.all_to_all(pieces, axes, 0, 0, tiled=True)  11.2 us
    all_to_all x1, waiting for transfers between devices, exchange(): return lax.all_to_all(pieces, axes, 0, 0, tiled=True)  5.77 us
    ppermute x4, waiting for transfers between devices, swap(): return lax.ppermute(value, 'core', [(0, 1), (1, 0)])  5.22 us
  transfers between devices with their start and end apart: 5, of which 5 were waited for; matrix products, arithmetic and copies ran while one was open for 5% of the time, Pallas kernels for 0%

profile of v2, /device:TPU:1, one launch (start us, length us, event | category | flops | bytes accessed | tf_op | source)
XLA Modules:
  0.0 125.7 jit_solution(13325166588381544649)
XLA Ops:
  0.6 1.3 %dynamic-slice_bitcast_fusion = (bf16[256,1024]{1,0:T(8,128)(2,1)S(1)}, bf16[256,1024]{1,0:T(8,128)(2,1)S(1)}) fusion(bf16[1,512,1024]{2,1,0:T(8,128)(2,1)} %param.12, s32[]{:T(128)S(6)} %select_n.23, s32[]{:T(128)S(6)} %select_n.22), kind=kLoop, calls=%fused_computation | loop fusion | bytes 2097160 | tf_op jit(solution)/shard_map/dynamic_slice | solution.py:330
  1.9 1.5 %collective-permute-start = (bf16[256,1024]{1,0:T(8,128)(2,1)S(1)}, bf16[256,1024]{1,0:T(8,128)(2,1)S(1)}, u32[]{:S(2)}, u32[]{:S(2)}) collective-permute-start(bf16[256,1024]{1,0:T(8,128)(2,1)S(1)} %get-tuple-element.22), channel_id=1, source_target_pairs={{0,1},{1,0},{2,3},{3,2},{4,5},{5,4},{6,7},{7,6},{8,9},{9,8},{10,11... | collective-permute-start | bytes 1572872 | tf_op jit(solution)/shard_map/ppermute | solution.py:322
  4.1 0.9 collective-permute-done
  5.0 0.8 broadcast_select_fusion
  5.8 11.2 %all-to-all-start = ((bf16[64,8,512]{2,1,0:T(8,128)(2,1)}), bf16[64,8,512]{2,1,0:T(8,128)(2,1)S(1)}, u32[]{:S(2)}, u32[]{:S(2)}) async-start(bf16[64,8,512]{2,1,0:T(8,128)(2,1)} %bitcast.6), calls=%async_computation | async-start | bytes 1048576 | tf_op jit(solution)/shard_map/all_to_all | solution.py:318
  17.0 1.4 %fusion = (s32[]{:T(128)}, s32[1,32]{0,1:T(8,128)S(1)}) fusion(s32[128,32]{0,1:T(8,128)} %param.11, s32[]{:T(128)S(6)} %select_n.26), kind=kLoop, calls=%fused_computation.7 | loop fusion | flops 31 | bytes 264 | tf_op jit(solution)/shard_map/reduce_sum | solution.py:361
  19.1 0.6 copy.12.sizes_ref
  19.8 1.3 %convert_element_type.3.forces_ref = f32[3,2048]{1,0:T(4,128)} convert(bf16[3,2048]{1,0:T(4,128)(2,1)} %param.9) | non-fusion elementwise | flops 6144 | bytes 36864 | tf_op jit(solution)/shard_map/convert_element_type | solution.py:366
  21.1 1.2 pad_add_fusion.info_ref
  22.3 1.2 multiply_bitcast_fusion.energies_ref
  23.5 5.8 %all-to-all-done = bf16[64,8,512]{2,1,0:T(8,128)(2,1)S(1)} async-done(((bf16[64,8,512]{2,1,0:T(8,128)(2,1)}), bf16[64,8,512]{2,1,0:T(8,128)(2,1)S(1)}, u32[]{:S(2)}, u32[]{:S(2)}) %all-to-all-start) | async-done | bytes 524320 | tf_op jit(solution)/shard_map/all_to_all | solution.py:318
  29.3 15.5 %all_to_all.20 = bf16[64,8,512]{2,1,0:T(8,128)(2,1)S(1)} all-to-all(bf16[64,8,512]{2,1,0:T(8,128)(2,1)S(1)} %broadcast_in_dim.7), channel_id=1, replica_groups=mesh['rows'=16,'z'=4,'core'=2] {'rows','z'}, dimensions={0} | all-to-all | bytes 1048576 | tf_op jit(solution)/shard_map/all_to_all | solution.py:318
  44.8 0.0 copy-start
  44.8 3.2 %collective-permute-start.1 = (bf16[256,1024]{1,0:T(8,128)(2,1)S(1)}, bf16[256,1024]{1,0:T(8,128)(2,1)S(1)}, u32[]{:S(2)}, u32[]{:S(2)}) collective-permute-start(bf16[256,1024]{1,0:T(8,128)(2,1)S(1)} %bitcast.29), channel_id=1, source_target_pairs={{0,1},{1,0},{2,3},{3,2},{4,5},{5,4},{6,7},{7,6},{8,9},{9,8},{10,11... | collective-permute-start | bytes 1572872 | tf_op jit(solution)/shard_map/ppermute | solution.py:322
  48.0 1.5 %collective-permute-done.1.other_ref = bf16[256,1024]{1,0:T(8,128)(2,1)S(1)} collective-permute-done((bf16[256,1024]{1,0:T(8,128)(2,1)S(1)}, bf16[256,1024]{1,0:T(8,128)(2,1)S(1)}, u32[]{:S(2)}, u32[]{:S(2)}) %collective-permute-start.1) | collective-permute-done | bytes 524320 | tf_op jit(solution)/shard_map/ppermute | solution.py:322
  49.6 0.0 copy-done
  49.6 0.0 copy-start.1
  49.6 0.8 copy-done.1
  50.4 14.2 %gram_halves.1 = (f32[704,128]{1,0:T(8,128)}, f32[704,128]{1,0:T(8,128)}) custom-call(s32[3]{0:T(128)} %pad_add_fusion.info_ref, s32[1,32]{1,0:T(1,128)} %copy.12.sizes_ref, f32[1,32]{1,0:T(1,128)} %multiply_bitcast_fusion.energies_ref, bf16[256,1024]{1,0:T(8,128)(2,1)} %bitcast.30, bf16[256,1024]{1,0:T(8,128)(2,1)} %copy-done.1, ...), custom_call_target="tpu_custom_call" | custom-call | tf_op jit(solution)/shard_map/gram_halves/pallas_call | solution.py:284
  64.6 4.5 %collective-permute-start.2 = (f32[704,128]{1,0:T(8,128)}, f32[704,128]{1,0:T(8,128)S(1)}, u32[]{:S(2)}, u32[]{:S(2)}) collective-permute-start(f32[704,128]{1,0:T(8,128)} %get-tuple-element.17), channel_id=1, source_target_pairs={{0,1},{1,0},{2,3},{3,2},{4,5},{5,4},{6,7},{7,6},{8,9},{9,8},{10,11... | collective-permute-start | bytes 1081352 | tf_op jit(solution)/shard_map/ppermute | solution.py:322
  69.1 1.5 %collective-permute-done.2 = f32[704,128]{1,0:T(8,128)S(1)} collective-permute-done((f32[704,128]{1,0:T(8,128)}, f32[704,128]{1,0:T(8,128)S(1)}, u32[]{:S(2)}, u32[]{:S(2)}) %collective-permute-start.2) | collective-permute-done | bytes 360480 | tf_op jit(solution)/shard_map/ppermute | solution.py:322
  70.6 1.0 add.32
  71.6 17.4 %all_to_all.21 = f32[64,1,1408]{2,1,0:T(1,128)S(1)} all-to-all(f32[64,1,1408]{2,1,0:T(1,128)S(1)} %bitcast.31), channel_id=1, replica_groups=mesh['rows'=16,'z'=4,'core'=2] {'rows','z'}, dimensions={0} | all-to-all | bytes 720896 | tf_op jit(solution)/shard_map/all_to_all | solution.py:318
  89.1 0.2 reduce_sum.19
  89.3 0.2 broadcast_in_dim.16
  89.5 14.5 %all_to_all.22 = f32[64,1,1408]{2,1,0:T(1,128)S(1)} all-to-all(f32[64,1,1408]{2,1,0:T(1,128)S(1)} %broadcast_in_dim.16), channel_id=1, replica_groups=mesh['rows'=16,'z'=4,'core'=2] {'rows','z'}, dimensions={0} | all-to-all | bytes 720896 | tf_op jit(solution)/shard_map/all_to_all | solution.py:318
  104.0 3.1 %collective-permute-start.3 = (f32[704,128]{1,0:T(8,128)S(1)}, f32[704,128]{1,0:T(8,128)S(1)}, u32[]{:S(2)}, u32[]{:S(2)}) collective-permute-start(f32[704,128]{1,0:T(8,128)S(1)} %bitcast.27), channel_id=1, source_target_pairs={{0,1},{1,0},{2,3},{3,2},{4,5},{5,4},{6,7},{7,6},{8,9},{9,8},{10,11... | collective-permute-start | bytes 1081352 | tf_op jit(solution)/shard_map/ppermute | solution.py:322
  107.2 1.3 %collective-permute-done.3.other_ref = f32[704,128]{1,0:T(8,128)S(1)} collective-permute-done((f32[704,128]{1,0:T(8,128)S(1)}, f32[704,128]{1,0:T(8,128)S(1)}, u32[]{:S(2)}, u32[]{:S(2)}) %collective-permute-start.3) | collective-permute-done | bytes 360480 | tf_op jit(solution)/shard_map/ppermute | solution.py:322
  108.5 17.2 %factor_and_solve.1 = (f32[512,512]{1,0:T(8,128)}, f32[4,128]{1,0:T(4,128)}) custom-call(s32[1]{0:T(128)} %bitcast.core_ref, f32[704,128]{1,0:T(8,128)S(1)} %bitcast.28, f32[704,128]{1,0:T(8,128)S(1)} %collective-permute-done.3.other_ref), custom_call_target="tpu_custom_call" | custom-call | tf_op jit(solution)/shard_map/factor_and_solve/pallas_call | solution.py:148
  (2 shorter events, 0.0 us)
Async XLA Ops:
  1.9 3.0 %collective-permute-start = (bf16[256,1024]{1,0:T(8,128)(2,1)S(1)}, bf16[256,1024]{1,0:T(8,128)(2,1)S(1)}, u32[]{:S(2)}, u32[]{:S(2)}) collective-permute-start(bf16[256,1024]{1,0:T(8,128)(2,1)S(1)} %get-tuple-element.22), channel_id=1, source_target_pairs={{0,1},{1,0},{2,3},{3,2},{4,5},{5,4},{6,7},{7,6},{8,9},{9,8},{10,11... | collective-permute-start | bytes 1572872 | tf_op jit(solution)/shard_map/ppermute | solution.py:322
  5.8 23.5 %all-to-all-start = ((bf16[64,8,512]{2,1,0:T(8,128)(2,1)}), bf16[64,8,512]{2,1,0:T(8,128)(2,1)S(1)}, u32[]{:S(2)}, u32[]{:S(2)}) async-start(bf16[64,8,512]{2,1,0:T(8,128)(2,1)} %bitcast.6), calls=%async_computation | async-start | bytes 1048576 | tf_op jit(solution)/shard_map/all_to_all | solution.py:318
  44.8 4.7 %copy-start = (bf16[64,8,512]{2,1,0:T(8,128)(2,1)}, bf16[64,8,512]{2,1,0:T(8,128)(2,1)S(1)}, u32[]{:S(2)}) copy-start(bf16[64,8,512]{2,1,0:T(8,128)(2,1)S(1)} %all_to_all.20) | copy-start | bytes 1572868
  44.8 4.7 %collective-permute-start.1 = (bf16[256,1024]{1,0:T(8,128)(2,1)S(1)}, bf16[256,1024]{1,0:T(8,128)(2,1)S(1)}, u32[]{:S(2)}, u32[]{:S(2)}) collective-permute-start(bf16[256,1024]{1,0:T(8,128)(2,1)S(1)} %bitcast.29), channel_id=1, source_target_pairs={{0,1},{1,0},{2,3},{3,2},{4,5},{5,4},{6,7},{7,6},{8,9},{9,8},{10,11... | collective-permute-start | bytes 1572872 | tf_op jit(solution)/shard_map/ppermute | solution.py:322
  49.6 0.8 copy-start.1
  64.6 6.0 %collective-permute-start.2 = (f32[704,128]{1,0:T(8,128)}, f32[704,128]{1,0:T(8,128)S(1)}, u32[]{:S(2)}, u32[]{:S(2)}) collective-permute-start(f32[704,128]{1,0:T(8,128)} %get-tuple-element.17), channel_id=1, source_target_pairs={{0,1},{1,0},{2,3},{3,2},{4,5},{5,4},{6,7},{7,6},{8,9},{9,8},{10,11... | collective-permute-start | bytes 1081352 | tf_op jit(solution)/shard_map/ppermute | solution.py:322
  104.0 4.5 %collective-permute-start.3 = (f32[704,128]{1,0:T(8,128)S(1)}, f32[704,128]{1,0:T(8,128)S(1)}, u32[]{:S(2)}, u32[]{:S(2)}) collective-permute-start(f32[704,128]{1,0:T(8,128)S(1)} %bitcast.27), channel_id=1, source_target_pairs={{0,1},{1,0},{2,3},{3,2},{4,5},{5,4},{6,7},{7,6},{8,9},{9,8},{10,11... | collective-permute-start | bytes 1081352 | tf_op jit(solution)/shard_map/ppermute | solution.py:322

commit v3 on v2

--- a/solution.py
+++ b/solution.py
@@ -10,6 +10,7 @@
 
 TILE = 128
 GROUP = 32
+PART = 16
 
 
 def spread_lane(value, lane):
@@ -37,12 +38,13 @@
 def factor_group(rows, first):
     groups = GROUP // 8
     sub = lax.broadcasted_iota(jnp.int32, (8, TILE), 0)
-    columns = [
-        [spread_lane(rows[s][0], first + j) if s >= j // 8 else None for s in range(groups)]
-        for j in range(GROUP)
-    ]
     pivots = [jnp.ones((8, TILE), jnp.float32) for _ in range(groups)]
     for k in range(0, GROUP, 2):
+        if k % PART == 0:
+            columns = {
+                j: [spread_lane(rows[s][0], first + j) if s >= j // 8 else None for s in range(groups)]
+                for j in range(k, k + PART)
+            }
         s0, r0, r1 = k // 8, k % 8, k % 8 + 1
         one, two = columns[k], columns[k + 1]
         a = spread_row(one[s0], r0)
@@ -57,7 +59,7 @@
         two_next = {s: two[s] - one[s] * ratio for s in live}
         m1 = {s: one[s] * inv_a for s in live}
         m2 = {s: two_next[s] * inv_s for s in live}
-        for j in range(k + 2, GROUP):
+        for j in range(k + 2, k - k % PART + PART):
             sj, rj = j // 8, j % 8
             u1 = spread_row(one[sj], rj)
             u2 = spread_row(two[sj], rj) - u1 * ratio
@@ -306,10 +308,9 @@
                 pltpu.VMEM((rows, TILE), jnp.float32),
             ],
         ),
-        compiler_params=pltpu.CompilerParams(vmem_limit_bytes=58 * 1024 * 1024),
+        compiler_params=pltpu.CompilerParams(vmem_limit_bytes=50 * 1024 * 1024),
         name="gram_halves",
     )(info, sizes, energies, own, other, atoms, derivs, forces)
-CHIPS = ("rows", "z")
 EVERY = ("rows", "z", "core")
 ridge_total = 1.0
 
@@ -322,30 +323,54 @@
     return lax.ppermute(value, "core", [(0, 1), (1, 0)])
 
 
+def along_z(pieces):
+    count = lax.axis_size("z")
+    return [pieces(0)] + [
+        lax.ppermute(pieces(d), "z", [(i, (i + d) % count) for i in range(count)])
+        for d in range(1, count)
+    ]
+
+
 def panel_halves(panels, owner, others):
-    core = lax.axis_index("core")
-    chips = lax.axis_size(CHIPS)
+    core, z = lax.axis_index("core"), lax.axis_index("z")
+    count, deep = lax.axis_size("rows"), lax.axis_size("z")
     points, width = panels.shape
     half = points // 2
     far = swap(lax.dynamic_slice_in_dim(panels, (1 - core) * half, half, 0))
     near = lax.optimization_barrier(lax.dynamic_slice_in_dim(panels, core * half, half, 0))
     held = jnp.where(lax.rem(owner, 2) == core, near, far)
     tall = half // 8
-    wide = chips // tall
+    wide = count * deep // tall
     cut = held.reshape(tall, 8, wide, width // wide).transpose(0, 2, 1, 3)
-    pieces = exchange(cut.reshape(chips, 8, width // wide), CHIPS)
-    piece = lax.dynamic_index_in_dim(pieces, lax.div(owner, 2), 0, keepdims=True)
+    pieces = exchange(cut.reshape(count, deep, 8, width // wide), "rows")
+    line = lax.dynamic_index_in_dim(pieces, lax.div(owner, 2 * deep), 0, keepdims=False)
+
+    def part(d):
+        return lax.dynamic_slice_in_dim(line, lax.rem(z + d, deep), 1, 0)
+
+    owner_z = lax.rem(lax.div(owner, 2), deep)
+    came = along_z(part)
+    piece = came[0]
+    for d in range(1, deep):
+        piece = jnp.where(lax.rem(owner_z + d, deep) == z, came[d], piece)
     piece, others = lax.optimization_barrier((piece, others))
-    own = exchange(jnp.broadcast_to(piece, pieces.shape), CHIPS)
+    came = along_z(lambda d: piece)
+    behind = lax.rem(z + deep - lax.broadcasted_iota(jnp.int32, pieces.shape, 1), deep)
+    line = jnp.broadcast_to(came[0], pieces.shape)
+    for d in range(1, deep):
+        line = jnp.where(behind == d, came[d], line)
+    own = exchange(line, "rows")
     own = own.reshape(tall, wide, 8, width // wide).transpose(0, 2, 1, 3).reshape(half, width)
     return own, swap(own), others
 
 
 def sum_halves(keep, send):
-    chips = lax.axis_size(CHIPS)
-    pair = (keep + swap(send)).reshape(chips, 1, -1)
-    piece = jnp.sum(exchange(pair, CHIPS), axis=0, keepdims=True)
-    own = exchange(jnp.broadcast_to(piece, pair.shape), CHIPS).reshape(keep.shape)
+    count, deep = lax.axis_size("rows"), lax.axis_size("z")
+    pair = (keep + swap(send)).reshape(count, deep, 1, -1)
+    line = jnp.sum(exchange(pair, "rows"), axis=0)
+    piece = jnp.sum(exchange(line, "z"), axis=0, keepdims=True)
+    line = exchange(jnp.broadcast_to(piece, line.shape), "z")
+    own = exchange(jnp.broadcast_to(line[None], pair.shape), "rows").reshape(keep.shape)
     return own, swap(own)
 
 

time: 126 us -> 138 us (1.095)
  blocking collectives: 47.5 us -> 56.1 us
  starting transfers between devices: 23.5 us -> 28.5 us
  waiting for transfers between devices: 11 us -> 15.8 us
  Pallas kernels: 31.5 us -> 28 us
  other arithmetic: 7.25 us -> 4.67 us
    ppermute x0 -> x6, starting transfers between devices: none -> 9.02 us  [along_z(): lax.ppermute(pieces(d), 'z', [(i, (i + d) % count) for i in range(count)])]
    all_to_all x3 -> x5, blocking collectives: 47.5 us -> 56.1 us  [exchange(): return lax.all_to_all(pieces, axes, 0, 0, tiled=True)]
    all_to_all x1, starting transfers between devices: 11.2 us -> 6.84 us  [exchange(): return lax.all_to_all(pieces, axes, 0, 0, tiled=True)]
    ppermute x0 -> x6, waiting for transfers between devices: none -> 2.56 us  [along_z(): lax.ppermute(pieces(d), 'z', [(i, (i + d) % count) for i in range(count)])]
    all_to_all x1, waiting for transfers between devices: 5.77 us -> 7.88 us  [exchange(): return lax.all_to_all(pieces, axes, 0, 0, tiled=True)]
    pallas_call x1, Pallas kernels: 17.2 us -> 15.1 us  [factor_and_solve(): pl.pallas_call(factor_kernel, out_shape=(jax.ShapeDtypeStruct((points, po...]
  transfers between devices with their start and end apart: 5 -> 11, of which waited for: 5 -> 9; matrix products, arithmetic and copies ran while one was open for 5% -> 3% of each run, Pallas kernels for 0% -> 0%
where the time goes in v3:
time: 138 us; the launch traced here: 137 us
  blocking collectives  56.1 us (41%)
  starting transfers between devices  28.5 us (21%)
  Pallas kernels  28 us (20%)
  waiting for transfers between devices  15.8 us (11%)
  other arithmetic  4.67 us (3%)
  between operations  2.13 us (2%)
  local copies, waits for them, and re-layouts  1.71 us (1%)
    all_to_all x5, blocking collectives, exchange(): return lax.all_to_all(pieces, axes, 0, 0, tiled=True)  56.1 us
    pallas_call x1, Pallas kernels, factor_and_solve(): pl.pallas_call(factor_kernel, out_shape=(jax.ShapeDtypeStruct((points, po...  15.1 us
    pallas_call x1, Pallas kernels, gram_halves(): pl.pallas_call(functools.partial(gram_kernel, scale, weight), out_shape=(...  12.9 us
    ppermute x4, starting transfers between devices, swap(): return lax.ppermute(value, 'core', [(0, 1), (1, 0)])  12.6 us
    ppermute x6, starting transfers between devices, along_z(): lax.ppermute(pieces(d), 'z', [(i, (i + d) % count) for i in range(count)])  9.02 us
    all_to_all x1, waiting for transfers between devices, exchange(): return lax.all_to_all(pieces, axes, 0, 0, tiled=True)  7.88 us
    all_to_all x1, starting transfers between devices, exchange(): return lax.all_to_all(pieces, axes, 0, 0, tiled=True)  6.84 us
    ppermute x4, waiting for transfers between devices, swap(): return lax.ppermute(value, 'core', [(0, 1), (1, 0)])  5.37 us
  transfers between devices with their start and end apart: 11, of which 9 were waited for; matrix products, arithmetic and copies ran while one was open for 3% of the time, Pallas kernels for 0%

profile of v3, /device:TPU:1, one launch (start us, length us, event | category | flops | bytes accessed | tf_op | source)
XLA Modules:
  0.0 136.9 jit_solution(11601485014080439536)
XLA Ops:
  0.6 1.3 dynamic-slice_bitcast_fusion
  1.9 1.5 %collective-permute-start = (bf16[256,1024]{1,0:T(8,128)(2,1)S(1)}, bf16[256,1024]{1,0:T(8,128)(2,1)S(1)}, u32[]{:S(2)}, u32[]{:S(2)}) collective-permute-start(bf16[256,1024]{1,0:T(8,128)(2,1)S(1)} %get-tuple-element.22), channel_id=1, source_target_pairs={{0,1},{1,0},{2,3},{3,2},{4,5},{5,4},{6,7},{7,6},{8,9},{9,8},{10,11... | collective-permute-start | bytes 1572872 | tf_op jit(solution)/shard_map/ppermute | solution.py:323
  4.1 0.9 collective-permute-done
  5.0 0.8 broadcast_select_fusion
  5.8 6.8 %all-to-all-start = ((bf16[16,4,8,512]{3,2,1,0:T(8,128)(2,1)}), bf16[16,4,8,512]{3,2,1,0:T(8,128)(2,1)S(1)}, u32[]{:S(2)}, u32[]{:S(2)}) async-start(bf16[16,4,8,512]{3,2,1,0:T(8,128)(2,1)} %bitcast.6), calls=%async_computation | async-start | bytes 1048576 | tf_op jit(solution)/shard_map/all_to_all | solution.py:319
  12.7 1.4 %fusion.9 = (s32[]{:T(128)}, s32[1,32]{0,1:T(8,128)S(1)}) fusion(s32[128,32]{0,1:T(8,128)} %param.11, s32[]{:T(128)S(6)} %select_n.93), kind=kLoop, calls=%fused_computation.23 | loop fusion | flops 31 | bytes 264 | tf_op jit(solution)/shard_map/reduce_sum | solution.py:386
  14.8 0.7 multiply_bitcast_fusion.energies_ref
  15.5 7.9 %all-to-all-done = bf16[16,4,8,512]{3,2,1,0:T(8,128)(2,1)S(1)} async-done(((bf16[16,4,8,512]{3,2,1,0:T(8,128)(2,1)}), bf16[16,4,8,512]{3,2,1,0:T(8,128)(2,1)S(1)}, u32[]{:S(2)}, u32[]{:S(2)}) %all-to-all-start) | async-done | bytes 524320 | tf_op jit(solution)/shard_map/all_to_all | solution.py:319
  23.4 1.6 %collective-permute-start.3 = (bf16[1,8,512]{2,1,0:T(8,128)(2,1)S(1)}, bf16[1,8,512]{2,1,0:T(8,128)(2,1)S(1)}, u32[]{:S(2)}, u32[]{:S(2)}) collective-permute-start(bf16[1,8,512]{2,1,0:T(8,128)(2,1)S(1)} %get-tuple-element.24), channel_id=1, source_target_pairs={{0,2},{2,4},{4,6},{6,0},{1,3},{3,5},{5,7},{7,1},{8,10},{10,12},{12... | collective-permute-start | bytes 24584 | tf_op jit(solution)/shard_map/ppermute | solution.py:329
  25.0 3.3 %collective-permute-start.2 = (bf16[1,8,512]{2,1,0:T(8,128)(2,1)S(1)}, bf16[1,8,512]{2,1,0:T(8,128)(2,1)S(1)}, u32[]{:S(2)}, u32[]{:S(2)}) collective-permute-start(bf16[1,8,512]{2,1,0:T(8,128)(2,1)S(1)} %get-tuple-element.25), channel_id=1, source_target_pairs={{0,4},{2,6},{4,0},{6,2},{1,5},{3,7},{5,1},{7,3},{8,12},{10,14},{12... | collective-permute-start | bytes 24584 | tf_op jit(solution)/shard_map/ppermute | solution.py:329
  28.3 0.7 collective-permute-start.1
  29.0 0.7 pad_add_fusion.info_ref
  29.8 0.7 convert_element_type.3.forces_ref
  30.6 0.5 collective-permute-done.1
  31.1 0.3 collective-permute-start.6
  31.4 2.6 %collective-permute-start.5 = (bf16[1,8,512]{2,1,0:T(8,128)(2,1)S(1)}, bf16[1,8,512]{2,1,0:T(8,128)(2,1)S(1)}, u32[]{:S(2)}, u32[]{:S(2)}) collective-permute-start(bf16[1,8,512]{2,1,0:T(8,128)(2,1)S(1)} %fusion.7), channel_id=1, source_target_pairs={{0,4},{2,6},{4,0},{6,2},{1,5},{3,7},{5,1},{7,3},{8,12},{10,14},{12... | collective-permute-start | bytes 24584 | tf_op jit(solution)/shard_map/ppermute | solution.py:329
  34.0 0.5 collective-permute-start.4
  34.5 0.4 collective-permute-done.6
  34.9 0.5 collective-permute-done.5
  35.4 1.1 collective-permute-done.4
  36.6 12.6 %all_to_all.30 = bf16[16,4,8,512]{3,2,1,0:T(8,128)(2,1)S(1)} all-to-all(bf16[16,4,8,512]{3,2,1,0:T(8,128)(2,1)S(1)} %fusion.3), channel_id=1, replica_groups=mesh['rows'=16,'z'=4,'core'=2] {'rows'}, dimensions={0} | all-to-all | bytes 1048576 | tf_op jit(solution)/shard_map/all_to_all | solution.py:319
  49.2 5.7 %collective-permute-start.7 = (bf16[256,1024]{1,0:T(8,128)(2,1)S(1)}, bf16[256,1024]{1,0:T(8,128)(2,1)S(1)}, u32[]{:S(2)}, u32[]{:S(2)}) collective-permute-start(bf16[256,1024]{1,0:T(8,128)(2,1)S(1)} %bitcast.46), channel_id=1, source_target_pairs={{0,1},{1,0},{2,3},{3,2},{4,5},{5,4},{6,7},{7,6},{8,9},{9,8},{10,11... | collective-permute-start | bytes 1572872 | tf_op jit(solution)/shard_map/ppermute | solution.py:323
  54.9 1.5 %collective-permute-done.7.other_ref = bf16[256,1024]{1,0:T(8,128)(2,1)S(1)} collective-permute-done((bf16[256,1024]{1,0:T(8,128)(2,1)S(1)}, bf16[256,1024]{1,0:T(8,128)(2,1)S(1)}, u32[]{:S(2)}, u32[]{:S(2)}) %collective-permute-start.7) | collective-permute-done | bytes 524320 | tf_op jit(solution)/shard_map/ppermute | solution.py:323
  56.5 12.9 %gram_halves.1 = (f32[704,128]{1,0:T(8,128)S(1)}, f32[704,128]{1,0:T(8,128)S(1)}) custom-call(s32[3]{0:T(128)S(1)} %pad_add_fusion.info_ref, s32[1,32]{1,0:T(1,128)S(1)} %copy.13.sizes_ref, f32[1,32]{1,0:T(1,128)S(1)} %multiply_bitcast_fusion.energies_ref, bf16[256,1024]{1,0:T(8,128)(2,1)S(1)} %bitcast.47, ...), custom_call_target="tpu_custom_call" | custom-call | tf_op jit(solution)/shard_map/gram_halves/pallas_call | solution.py:286
  69.4 1.7 %collective-permute-done.8 = f32[704,128]{1,0:T(8,128)S(1)} collective-permute-done((f32[704,128]{1,0:T(8,128)S(1)}, f32[704,128]{1,0:T(8,128)S(1)}, u32[]{:S(2)}, u32[]{:S(2)}) %collective-permute-start.8) | collective-permute-done | bytes 360480 | tf_op jit(solution)/shard_map/ppermute | solution.py:323
  71.3 15.0 %all_to_all.31 = f32[16,4,1,1408]{3,1,2,0:T(4,128)S(1)} all-to-all(f32[16,4,1,1408]{3,1,2,0:T(4,128)S(1)} %bitcast.48), channel_id=1, replica_groups=mesh['rows'=16,'z'=4,'core'=2] {'rows'}, dimensions={0} | all-to-all | bytes 720896 | tf_op jit(solution)/shard_map/all_to_all | solution.py:319
  86.4 10.8 %all_to_all.32 = f32[4,1,1408]{2,1,0:T(1,128)S(1)} all-to-all(f32[4,1,1408]{2,1,0:T(1,128)S(1)} %reduce_sum.31), channel_id=1, replica_groups=mesh['rows'=16,'z'=4,'core'=2] {'z'}, dimensions={0} | all-to-all | bytes 45056 | tf_op jit(solution)/shard_map/all_to_all | solution.py:319
  97.3 6.6 %all_to_all.33 = f32[4,1,1408]{2,1,0:T(1,128)S(1)} all-to-all(f32[4,1,1408]{2,1,0:T(1,128)S(1)} %broadcast_in_dim.42), channel_id=1, replica_groups=mesh['rows'=16,'z'=4,'core'=2] {'z'}, dimensions={0} | all-to-all | bytes 45056 | tf_op jit(solution)/shard_map/all_to_all | solution.py:319
  103.9 11.1 %all_to_all.34 = f32[16,4,1,1408]{3,1,2,0:T(4,128)S(1)} all-to-all(f32[16,4,1,1408]{3,1,2,0:T(4,128)S(1)} %broadcast_in_dim.44), channel_id=1, replica_groups=mesh['rows'=16,'z'=4,'core'=2] {'rows'}, dimensions={0} | all-to-all | bytes 720896 | tf_op jit(solution)/shard_map/all_to_all | solution.py:319
  115.2 5.3 %collective-permute-start.9 = (f32[704,128]{1,0:T(8,128)S(1)}, f32[704,128]{1,0:T(8,128)S(1)}, u32[]{:S(2)}, u32[]{:S(2)}) collective-permute-start(f32[704,128]{1,0:T(8,128)S(1)} %reshape.54.own_ref), channel_id=1, source_target_pairs={{0,1},{1,0},{2,3},{3,2},{4,5},{5,4},{6,7},{7,6},{8,9},{9,8},{10,11... | collective-permute-start | bytes 1081352 | tf_op jit(solution)/shard_map/ppermute | solution.py:323
  120.5 1.3 collective-permute-done.9.other_ref
  121.8 15.1 %factor_and_solve.1 = (f32[512,512]{1,0:T(8,128)}, f32[4,128]{1,0:T(4,128)}) custom-call(s32[1]{0:T(128)} %bitcast.core_ref, f32[704,128]{1,0:T(8,128)S(1)} %reshape.54.own_ref, f32[704,128]{1,0:T(8,128)S(1)} %collective-permute-done.9.other_ref), custom_call_target="tpu_custom_call" | custom-call | tf_op jit(solution)/shard_map/factor_and_solve/pallas_call | solution.py:150
  (18 shorter events, 0.8 us)
Async XLA Ops:
  1.9 3.0 %collective-permute-start = (bf16[256,1024]{1,0:T(8,128)(2,1)S(1)}, bf16[256,1024]{1,0:T(8,128)(2,1)S(1)}, u32[]{:S(2)}, u32[]{:S(2)}) collective-permute-start(bf16[256,1024]{1,0:T(8,128)(2,1)S(1)} %get-tuple-element.22), channel_id=1, source_target_pairs={{0,1},{1,0},{2,3},{3,2},{4,5},{5,4},{6,7},{7,6},{8,9},{9,8},{10,11... | collective-permute-start | bytes 1572872 | tf_op jit(solution)/shard_map/ppermute | solution.py:323
  5.8 17.6 %all-to-all-start = ((bf16[16,4,8,512]{3,2,1,0:T(8,128)(2,1)}), bf16[16,4,8,512]{3,2,1,0:T(8,128)(2,1)S(1)}, u32[]{:S(2)}, u32[]{:S(2)}) async-start(bf16[16,4,8,512]{3,2,1,0:T(8,128)(2,1)} %bitcast.6), calls=%async_computation | async-start | bytes 1048576 | tf_op jit(solution)/shard_map/all_to_all | solution.py:319
  23.4 7.2 %collective-permute-start.3 = (bf16[1,8,512]{2,1,0:T(8,128)(2,1)S(1)}, bf16[1,8,512]{2,1,0:T(8,128)(2,1)S(1)}, u32[]{:S(2)}, u32[]{:S(2)}) collective-permute-start(bf16[1,8,512]{2,1,0:T(8,128)(2,1)S(1)} %get-tuple-element.24), channel_id=1, source_target_pairs={{0,2},{2,4},{4,6},{6,0},{1,3},{3,5},{5,7},{7,1},{8,10},{10,12},{12... | collective-permute-start | bytes 24584 | tf_op jit(solution)/shard_map/ppermute | solution.py:329
  25.0 5.6 %collective-permute-start.2 = (bf16[1,8,512]{2,1,0:T(8,128)(2,1)S(1)}, bf16[1,8,512]{2,1,0:T(8,128)(2,1)S(1)}, u32[]{:S(2)}, u32[]{:S(2)}) collective-permute-start(bf16[1,8,512]{2,1,0:T(8,128)(2,1)S(1)} %get-tuple-element.25), channel_id=1, source_target_pairs={{0,4},{2,6},{4,0},{6,2},{1,5},{3,7},{5,1},{7,3},{8,12},{10,14},{12... | collective-permute-start | bytes 24584 | tf_op jit(solution)/shard_map/ppermute | solution.py:329
  28.3 2.8 %collective-permute-start.1 = (bf16[1,8,512]{2,1,0:T(8,128)(2,1)S(1)}, bf16[1,8,512]{2,1,0:T(8,128)(2,1)S(1)}, u32[]{:S(2)}, u32[]{:S(2)}) collective-permute-start(bf16[1,8,512]{2,1,0:T(8,128)(2,1)S(1)} %get-tuple-element.26), channel_id=1, source_target_pairs={{0,6},{2,0},{4,2},{6,4},{1,7},{3,1},{5,3},{7,5},{8,14},{10,8},{12,... | collective-permute-start | bytes 24584 | tf_op jit(solution)/shard_map/ppermute | solution.py:329
  31.1 3.8 %collective-permute-start.6 = (bf16[1,8,512]{2,1,0:T(8,128)(2,1)S(1)}, bf16[1,8,512]{2,1,0:T(8,128)(2,1)S(1)}, u32[]{:S(2)}, u32[]{:S(2)}) collective-permute-start(bf16[1,8,512]{2,1,0:T(8,128)(2,1)S(1)} %fusion.7), channel_id=1, source_target_pairs={{0,2},{2,4},{4,6},{6,0},{1,3},{3,5},{5,7},{7,1},{8,10},{10,12},{12... | collective-permute-start | bytes 24584 | tf_op jit(solution)/shard_map/ppermute | solution.py:329
  31.4 4.0 %collective-permute-start.5 = (bf16[1,8,512]{2,1,0:T(8,128)(2,1)S(1)}, bf16[1,8,512]{2,1,0:T(8,128)(2,1)S(1)}, u32[]{:S(2)}, u32[]{:S(2)}) collective-permute-start(bf16[1,8,512]{2,1,0:T(8,128)(2,1)S(1)} %fusion.7), channel_id=1, source_target_pairs={{0,4},{2,6},{4,0},{6,2},{1,5},{3,7},{5,1},{7,3},{8,12},{10,14},{12... | collective-permute-start | bytes 24584 | tf_op jit(solution)/shard_map/ppermute | solution.py:329
  34.0 2.5 %collective-permute-start.4 = (bf16[1,8,512]{2,1,0:T(8,128)(2,1)S(1)}, bf16[1,8,512]{2,1,0:T(8,128)(2,1)S(1)}, u32[]{:S(2)}, u32[]{:S(2)}) collective-permute-start(bf16[1,8,512]{2,1,0:T(8,128)(2,1)S(1)} %fusion.7), channel_id=1, source_target_pairs={{0,6},{2,0},{4,2},{6,4},{1,7},{3,1},{5,3},{7,5},{8,14},{10,8},{12,... | collective-permute-start | bytes 24584 | tf_op jit(solution)/shard_map/ppermute | solution.py:329
  49.2 7.2 %collective-permute-start.7 = (bf16[256,1024]{1,0:T(8,128)(2,1)S(1)}, bf16[256,1024]{1,0:T(8,128)(2,1)S(1)}, u32[]{:S(2)}, u32[]{:S(2)}) collective-permute-start(bf16[256,1024]{1,0:T(8,128)(2,1)S(1)} %bitcast.46), channel_id=1, source_target_pairs={{0,1},{1,0},{2,3},{3,2},{4,5},{5,4},{6,7},{7,6},{8,9},{9,8},{10,11... | collective-permute-start | bytes 1572872 | tf_op jit(solution)/shard_map/ppermute | solution.py:323
  69.3 1.8 %collective-permute-start.8 = (f32[704,128]{1,0:T(8,128)S(1)}, f32[704,128]{1,0:T(8,128)S(1)}, u32[]{:S(2)}, u32[]{:S(2)}) collective-permute-start(f32[704,128]{1,0:T(8,128)S(1)} %get-tuple-element.17), channel_id=1, source_target_pairs={{0,1},{1,0},{2,3},{3,2},{4,5},{5,4},{6,7},{7,6},{8,9},{9,8},{10,11... | collective-permute-start | bytes 1081352 | tf_op jit(solution)/shard_map/ppermute | solution.py:323
  115.2 6.6 %collective-permute-start.9 = (f32[704,128]{1,0:T(8,128)S(1)}, f32[704,128]{1,0:T(8,128)S(1)}, u32[]{:S(2)}, u32[]{:S(2)}) collective-permute-start(f32[704,128]{1,0:T(8,128)S(1)} %reshape.54.own_ref), channel_id=1, source_target_pairs={{0,1},{1,0},{2,3},{3,2},{4,5},{5,4},{6,7},{7,6},{8,9},{9,8},{10,11... | collective-permute-start | bytes 1081352 | tf_op jit(solution)/shard_map/ppermute | solution.py:323

commit v4 on v2

--- a/solution.py
+++ b/solution.py
@@ -10,6 +10,7 @@
 
 TILE = 128
 GROUP = 32
+PART = 16
 
 
 def spread_lane(value, lane):
@@ -37,12 +38,13 @@
 def factor_group(rows, first):
     groups = GROUP // 8
     sub = lax.broadcasted_iota(jnp.int32, (8, TILE), 0)
-    columns = [
-        [spread_lane(rows[s][0], first + j) if s >= j // 8 else None for s in range(groups)]
-        for j in range(GROUP)
-    ]
     pivots = [jnp.ones((8, TILE), jnp.float32) for _ in range(groups)]
     for k in range(0, GROUP, 2):
+        if k % PART == 0:
+            columns = {
+                j: [spread_lane(rows[s][0], first + j) if s >= j // 8 else None for s in range(groups)]
+                for j in range(k, k + PART)
+            }
         s0, r0, r1 = k // 8, k % 8, k % 8 + 1
         one, two = columns[k], columns[k + 1]
         a = spread_row(one[s0], r0)
@@ -57,7 +59,7 @@
         two_next = {s: two[s] - one[s] * ratio for s in live}
         m1 = {s: one[s] * inv_a for s in live}
         m2 = {s: two_next[s] * inv_s for s in live}
-        for j in range(k + 2, GROUP):
+        for j in range(k + 2, k - k % PART + PART):
             sj, rj = j // 8, j % 8
             u1 = spread_row(one[sj], rj)
             u2 = spread_row(two[sj], rj) - u1 * ratio
@@ -75,7 +77,9 @@
     return [[piece * scales[s] for piece in rows[s]] for s in range(groups)]
 
 
-def factor_kernel(core_ref, own_ref, other_ref, factor_ref, solved_ref, work, done, packed):
+def factor_kernel(
+    core_ref, own_ref, other_ref, factor_ref, solved_ref, work, done, packed, upper, sent
+):
     points = factor_ref.shape[0]
     tiles = points // TILE
     half = own_ref.shape[0]
@@ -105,6 +109,10 @@
                 precision=lax.Precision.HIGHEST,
                 preferred_element_type=jnp.float32,
             )
+
+    def leaving(top):
+        panel = pl.ds(top, TILE)
+        return pltpu.make_async_copy(upper.at[panel], factor_ref.at[panel], sent.at[top // TILE])
 
     for start in range(0, points, GROUP):
         top = start - start % TILE
@@ -130,9 +138,11 @@
                 done[at : at + 8, top + t * TILE : top + (t + 1) * TILE] = rows[s][t]
             for t in range(tiles):
                 own = t - top // TILE
-                factor_ref[at : at + 8, t * TILE : (t + 1) * TILE] = (
+                upper[at : at + 8, t * TILE : (t + 1) * TILE] = (
                     rows[s][own] if own >= 0 else jnp.zeros((8, TILE), jnp.float32)
                 )
+        if follow % TILE == 0:
+            leaving(top).start()
         if follow % TILE:
             take_off(follow, GROUP, start, follow)
         elif follow < points:
@@ -141,6 +151,8 @@
     for t in range(tiles):
         flipped = jnp.transpose(done[t * TILE : (t + 1) * TILE, points:])
         solved_ref[t : t + 1, :] = flipped[0:1, :]
+    for t in range(tiles):
+        leaving(t * TILE).wait()
 
 
 def factor_and_solve(core, own, other, points):
@@ -156,11 +168,13 @@
             pl.BlockSpec(memory_space=pltpu.VMEM),
             pl.BlockSpec(memory_space=pltpu.VMEM),
         ],
-        out_specs=(pl.BlockSpec(memory_space=pltpu.VMEM),) * 2,
+        out_specs=(pl.BlockSpec(memory_space=pl.ANY), pl.BlockSpec(memory_space=pltpu.VMEM)),
         scratch_shapes=[
             pltpu.VMEM((points, points + TILE), jnp.float32),
             pltpu.VMEM((points, points + TILE), jnp.float32),
             pltpu.VMEM((2 * own.shape[0], TILE), jnp.float32),
+            pltpu.VMEM((points, points), jnp.float32),
+            pltpu.SemaphoreType.DMA((tiles,)),
         ],
         compiler_params=pltpu.CompilerParams(vmem_limit_bytes=32 * 1024 * 1024),
         name="factor_and_solve",
@@ -185,87 +199,102 @@
 
 
 def gram_kernel(
-    scale, weight, info_ref, sizes_ref, energies_ref, own_ref, other_ref, atoms_ref, derivs_ref,
-    forces_ref, keep_ref, send_ref, panel_ref, square, cross, rhs_part, energy_part, packed,
+    scale, weight, info_ref, sizes_ref, energies_ref, own_ref, other_ref, forces_ref, atoms_ref,
+    derivs_ref, keep_ref, send_ref, panel_ref, held, square, cross, rhs_part, energy_part, packed,
+    arrived,
 ):
-    step = pl.program_id(0)
     points = panel_ref.shape[0]
-    block_rows = atoms_ref.shape[0]
+    blocks, block_rows = held.shape[1:3]
     slots = sizes_ref.shape[1]
     half = points // 2
-
-    @pl.when(step == 0)
-    def _():
-        core = info_ref[2]
-        panel_ref[pl.ds(pl.multiple_of(core * half, half), half), :] = own_ref[...]
-        panel_ref[pl.ds(pl.multiple_of((1 - core) * half, half), half), :] = other_ref[...]
-        square[...] = jnp.zeros_like(square)
-        cross[...] = jnp.zeros_like(cross)
-        rhs_part[...] = jnp.zeros_like(rhs_part)
-        energy_part[...] = jnp.zeros_like(energy_part)
-
-    @pl.when(step < info_ref[1])
-    def _():
-        panel = panel_ref[...]
-        before = lax.broadcasted_iota(jnp.int32, (slots, slots), 1)
-        after = lax.broadcasted_iota(jnp.int32, (slots, slots), 0)
-        wide = jnp.broadcast_to(sizes_ref[...], (slots, slots))
-        ends = jnp.sum(jnp.where(before <= after, wide, 0), axis=1, keepdims=True)
-        starts = jnp.sum(jnp.where(before < after, wide, 0), axis=1, keepdims=True)
-        slot = step * block_rows + lax.broadcasted_iota(jnp.int32, (slots, block_rows), 1)
-        member = jnp.where((slot >= starts) & (slot < ends), 1.0, 0.0).astype(jnp.bfloat16)
-        atom = step * block_rows + lax.broadcasted_iota(jnp.int32, (1, block_rows), 1)
-        live = jnp.where(atom < info_ref[0], 1.0, 0.0)
-        scores = against(panel, atoms_ref[...])
-        slopes = against(panel, derivs_ref[0])
-        squares = scores * scores
-        kernel_high, kernel_low = split(squares * squares)
-        cubes = squares * scores * (live * (-4.0 * weight * scale**4))
-        grams = []
-        folded = rhs_part[...]
-        for c in range(3):
-            design = cubes * slopes
-            if c < 2:
-                slopes = against(panel, derivs_ref[c + 1])
-            else:
-                energy_part[...] += against(kernel_high, member) + against(kernel_low, member)
-            high, low = split(design)
-            term = design * forces_ref[c : c + 1, :]
-            for t in range(block_rows // TILE):
-                folded = folded + term[:, t * TILE : (t + 1) * TILE]
-            grams.append((high, low))
-        rhs_part[...] = folded
-        high = jnp.concatenate([pair[0] for pair in grams], axis=1)
-        low = jnp.concatenate([pair[1] for pair in grams], axis=1)
-        square[:half, :] += against(high[:half], high)
-        square[half:, half:] += against(high[half:], high[half:])
-        cross[...] += against(high, low)
-
-    @pl.when(step == pl.num_programs(0) - 1)
-    def _():
-        norms = jnp.sqrt(jnp.maximum(sizes_ref[...], 1).astype(jnp.float32))
-        energy_ratio = energy_part[...] / norms
-        energy_rows = energy_ratio * (weight * scale**4)
-        gram = square[...] + cross[...] + jnp.transpose(cross[...])
-        gram = gram + against(energy_rows, energy_rows, exact_mode)
-        tiles = points // TILE
-        blocks = packed_blocks(tiles)
-        for n, (p, t) in enumerate(blocks):
-            packed[n * TILE : (n + 1) * TILE, :] = gram[
-                p * TILE : (p + 1) * TILE, t * TILE : (t + 1) * TILE
-            ]
-        ones = jnp.ones((8, TILE), jnp.float32)
-        rhs = against(ones, rhs_part[...], exact_mode)
-        rhs = rhs + against(
-            jnp.broadcast_to(energies_ref[...], (8, slots)), energy_ratio, exact_mode
-        )
-        for t in range(tiles):
-            at = len(blocks) * TILE + t
-            packed[at : at + 1, :] = rhs[0:1, t * TILE : (t + 1) * TILE]
-        core = info_ref[2]
-        count = keep_ref.shape[0]
-        keep_ref[...] = packed[pl.ds(pl.multiple_of(core * count, 8), count), :]
-        send_ref[...] = packed[pl.ds(pl.multiple_of((1 - core) * count, 8), count), :]
+    core = info_ref[2]
+
+    def copy(part, i):
+        rows = pl.ds(pl.multiple_of(i * block_rows, block_rows), block_rows)
+        source = derivs_ref.at[part - 1, rows] if part else atoms_ref.at[rows]
+        return pltpu.make_async_copy(source, held.at[part, i], arrived.at[part, i])
+
+    for i in range(blocks):
+        for part in range(4):
+            copy(part, i).start()
+
+    panel_ref[pl.ds(pl.multiple_of(core * half, half), half), :] = own_ref[...]
+    panel_ref[pl.ds(pl.multiple_of((1 - core) * half, half), half), :] = other_ref[...]
+    square[...] = jnp.zeros_like(square)
+    cross[...] = jnp.zeros_like(cross)
+    rhs_part[...] = jnp.zeros_like(rhs_part)
+    energy_part[...] = jnp.zeros_like(energy_part)
+    before = lax.broadcasted_iota(jnp.int32, (slots, slots), 1)
+    after = lax.broadcasted_iota(jnp.int32, (slots, slots), 0)
+    wide = jnp.broadcast_to(sizes_ref[...], (slots, slots))
+    ends = jnp.sum(jnp.where(before <= after, wide, 0), axis=1, keepdims=True)
+    starts = jnp.sum(jnp.where(before < after, wide, 0), axis=1, keepdims=True)
+
+    @pl.loop(0, blocks)
+    def _(i):
+        copy(0, i).wait()
+
+        @pl.when(i < info_ref[1])
+        def _():
+            panel = panel_ref[...]
+            slot = i * block_rows + lax.broadcasted_iota(jnp.int32, (slots, block_rows), 1)
+            member = jnp.where((slot >= starts) & (slot < ends), 1.0, 0.0).astype(jnp.bfloat16)
+            atom = i * block_rows + lax.broadcasted_iota(jnp.int32, (1, block_rows), 1)
+            live = jnp.where(atom < info_ref[0], 1.0, 0.0)
+            scores = against(panel, held[0, i])
+            for part in range(1, 4):
+                copy(part, i).wait()
+            slopes = against(panel, held[1, i])
+            squares = scores * scores
+            kernel_high, kernel_low = split(squares * squares)
+            cubes = squares * scores * (live * (-4.0 * weight * scale**4))
+            pairs = []
+            folded = rhs_part[...]
+            for c in range(3):
+                design = cubes * slopes
+                if c < 2:
+                    slopes = against(panel, held[c + 2, i])
+                else:
+                    energy_part[...] += against(kernel_high, member) + against(kernel_low, member)
+                pairs.append(split(design))
+                forces = forces_ref[c : c + 1, pl.ds(pl.multiple_of(i * block_rows, TILE), block_rows)]
+                term = design * forces
+                for t in range(block_rows // TILE):
+                    folded = folded + term[:, t * TILE : (t + 1) * TILE]
+            rhs_part[...] = folded
+            high = jnp.concatenate([pair[0] for pair in pairs], axis=1)
+            low = jnp.concatenate([pair[1] for pair in pairs], axis=1)
+            square[:half, :] += against(high[:half], high)
+            square[half:, half:] += against(high[half:], high[half:])
+            cross[...] += against(high, low)
+
+        @pl.when(i >= info_ref[1])
+        def _():
+            for part in range(1, 4):
+                copy(part, i).wait()
+
+    norms = jnp.sqrt(jnp.maximum(sizes_ref[...], 1).astype(jnp.float32))
+    energy_ratio = energy_part[...] / norms
+    energy_rows = energy_ratio * (weight * scale**4)
+    gram = square[...] + cross[...] + jnp.transpose(cross[...])
+    gram = gram + against(energy_rows, energy_rows, exact_mode)
+    tiles = points // TILE
+    places = packed_blocks(tiles)
+    for n, (p, t) in enumerate(places):
+        packed[n * TILE : (n + 1) * TILE, :] = gram[
+            p * TILE : (p + 1) * TILE, t * TILE : (t + 1) * TILE
+        ]
+    ones = jnp.ones((8, TILE), jnp.float32)
+    rhs = against(ones, rhs_part[...], exact_mode)
+    rhs = rhs + against(
+        jnp.broadcast_to(energies_ref[...], (8, slots)), energy_ratio, exact_mode
+    )
+    for t in range(tiles):
+        at = len(places) * TILE + t
+        packed[at : at + 1, :] = rhs[0:1, t * TILE : (t + 1) * TILE]
+    count = keep_ref.shape[0]
+    keep_ref[...] = packed[pl.ds(pl.multiple_of(core * count, 8), count), :]
+    send_ref[...] = packed[pl.ds(pl.multiple_of((1 - core) * count, 8), count), :]
 
 
 def block_rows_of(capacity):
@@ -277,38 +306,27 @@
     points = 2 * own.shape[0]
     slots = sizes.shape[1]
     block_rows = block_rows_of(capacity)
-
-    def row_block(i, info):
-        return jnp.minimum(i, info[1] - 1)
-
+    blocks = capacity // block_rows
+    in_vmem = pl.BlockSpec(memory_space=pltpu.VMEM)
+    anywhere = pl.BlockSpec(memory_space=pl.ANY)
     return pl.pallas_call(
         functools.partial(gram_kernel, scale, weight),
         out_shape=(jax.ShapeDtypeStruct((rows // 2, TILE), jnp.float32),) * 2,
-        grid_spec=pltpu.PrefetchScalarGridSpec(
-            num_scalar_prefetch=1,
-            grid=(capacity // block_rows,),
-            in_specs=[
-                pl.BlockSpec((1, slots), lambda i, info: (0, 0)),
-                pl.BlockSpec((1, slots), lambda i, info: (0, 0)),
-                pl.BlockSpec((points // 2, width), lambda i, info: (0, 0)),
-                pl.BlockSpec((points // 2, width), lambda i, info: (0, 0)),
-                pl.BlockSpec((block_rows, width), lambda i, info: (row_block(i, info), 0)),
-                pl.BlockSpec((3, block_rows, width), lambda i, info: (0, row_block(i, info), 0)),
-                pl.BlockSpec((3, block_rows), lambda i, info: (0, row_block(i, info))),
-            ],
-            out_specs=(pl.BlockSpec((rows // 2, TILE), lambda i, info: (0, 0)),) * 2,
-            scratch_shapes=[
-                pltpu.VMEM((points, width), jnp.bfloat16),
-                pltpu.VMEM((points, points), jnp.float32),
-                pltpu.VMEM((points, points), jnp.float32),
-                pltpu.VMEM((points, TILE), jnp.float32),
-                pltpu.VMEM((points, slots), jnp.float32),
-                pltpu.VMEM((rows, TILE), jnp.float32),
-            ],
-        ),
-        compiler_params=pltpu.CompilerParams(vmem_limit_bytes=58 * 1024 * 1024),
+        in_specs=[pl.BlockSpec(memory_space=pltpu.SMEM)] + [in_vmem] * 5 + [anywhere] * 2,
+        out_specs=(in_vmem,) * 2,
+        scratch_shapes=[
+            pltpu.VMEM((points, width), jnp.bfloat16),
+            pltpu.VMEM((4, blocks, block_rows, width), jnp.bfloat16),
+            pltpu.VMEM((points, points), jnp.float32),
+            pltpu.VMEM((points, points), jnp.float32),
+            pltpu.VMEM((points, TILE), jnp.float32),
+            pltpu.VMEM((points, slots), jnp.float32),
+            pltpu.VMEM((rows, TILE), jnp.float32),
+            pltpu.SemaphoreType.DMA((4, blocks)),
+        ],
+        compiler_params=pltpu.CompilerParams(vmem_limit_bytes=50 * 1024 * 1024),
         name="gram_halves",
-    )(info, sizes, energies, own, other, atoms, derivs, forces)
+    )(info, sizes, energies, own, other, forces, atoms, derivs)
 CHIPS = ("rows", "z")
 EVERY = ("rows", "z", "core")
 ridge_total = 1.0

time: 126 us -> 123 us (0.976)
  blocking collectives: 47.5 us -> 53.2 us
  starting transfers between devices: 23.5 us -> 19.2 us
  Pallas kernels: 31.5 us -> 28.6 us
  other arithmetic: 7.25 us -> 4.67 us
  waiting for transfers between devices: 11 us -> 13 us
  local copies, waits for them, and re-layouts: 2.95 us -> 1.58 us
    all_to_all x3, blocking collectives: 47.5 us -> 53.2 us  [exchange(): return lax.all_to_all(pieces, axes, 0, 0, tiled=True)]
    ppermute x4, starting transfers between devices: 12.3 us -> 7.99 us  [swap(): return lax.ppermute(value, 'core', [(0, 1), (1, 0)])]
    all_to_all x1, waiting for transfers between devices: 5.77 us -> 7.94 us  [exchange(): return lax.all_to_all(pieces, axes, 0, 0, tiled=True)]
    pallas_call x1, Pallas kernels: 17.2 us -> 15.4 us  [factor_and_solve(): pl.pallas_call(factor_kernel, out_shape=(jax.ShapeDtypeStruct((points, po...]
  transfers between devices with their start and end apart: 5 -> 5, of which waited for: 5 -> 5; matrix products, arithmetic and copies ran while one was open for 5% -> 3% of each run, Pallas kernels for 0% -> 0%
where the time goes in v4:
time: 123 us; the launch traced here: 122 us
  blocking collectives  53.2 us (43%)
  Pallas kernels  28.6 us (23%)
  starting transfers between devices  19.2 us (16%)
  waiting for transfers between devices  13 us (11%)
  other arithmetic  4.67 us (4%)
  between operations  2.18 us (2%)
  local copies, waits for them, and re-layouts  1.58 us (1%)
    all_to_all x3, blocking collectives, exchange(): return lax.all_to_all(pieces, axes, 0, 0, tiled=True)  53.2 us
    pallas_call x1, Pallas kernels, factor_and_solve(): pl.pallas_call(factor_kernel, out_shape=(jax.ShapeDtypeStruct((points, po...  15.4 us
    pallas_call x1, Pallas kernels, gram_halves(): pl.pallas_call(functools.partial(gram_kernel, scale, weight), out_shape=(...  13.2 us
    all_to_all x1, starting transfers between devices, exchange(): return lax.all_to_all(pieces, axes, 0, 0, tiled=True)  11.2 us
    ppermute x4, starting transfers between devices, swap(): return lax.ppermute(value, 'core', [(0, 1), (1, 0)])  7.99 us
    all_to_all x1, waiting for transfers between devices, exchange(): return lax.all_to_all(pieces, axes, 0, 0, tiled=True)  7.94 us
    ppermute x4, waiting for transfers between devices, swap(): return lax.ppermute(value, 'core', [(0, 1), (1, 0)])  5.02 us
  transfers between devices with their start and end apart: 5, of which 5 were waited for; matrix products, arithmetic and copies ran while one was open for 3% of the time, Pallas kernels for 0%

profile of v4, /device:TPU:1, one launch (start us, length us, event | category | flops | bytes accessed | tf_op | source)
XLA Modules:
  0.0 122.4 jit_solution(10991995221027600227)
XLA Ops:
  0.6 1.3 %dynamic-slice_bitcast_fusion = (bf16[256,1024]{1,0:T(8,128)(2,1)S(1)}, bf16[256,1024]{1,0:T(8,128)(2,1)S(1)}) fusion(bf16[1,512,1024]{2,1,0:T(8,128)(2,1)} %param.12, s32[]{:T(128)S(6)} %select_n.23, s32[]{:T(128)S(6)} %select_n.22), kind=kLoop, calls=%fused_computation | loop fusion | bytes 2097160 | tf_op jit(solution)/shard_map/dynamic_slice | solution.py:348
  1.9 1.5 %collective-permute-start = (bf16[256,1024]{1,0:T(8,128)(2,1)S(1)}, bf16[256,1024]{1,0:T(8,128)(2,1)S(1)}, u32[]{:S(2)}, u32[]{:S(2)}) collective-permute-start(bf16[256,1024]{1,0:T(8,128)(2,1)S(1)} %get-tuple-element.22), channel_id=1, source_target_pairs={{0,1},{1,0},{2,3},{3,2},{4,5},{5,4},{6,7},{7,6},{8,9},{9,8},{10,11... | collective-permute-start | bytes 1572872 | tf_op jit(solution)/shard_map/ppermute | solution.py:340
  4.1 0.9 collective-permute-done
  5.0 0.8 broadcast_select_fusion
  5.8 11.2 %all-to-all-start = ((bf16[64,8,512]{2,1,0:T(8,128)(2,1)}), bf16[64,8,512]{2,1,0:T(8,128)(2,1)S(1)}, u32[]{:S(2)}, u32[]{:S(2)}) async-start(bf16[64,8,512]{2,1,0:T(8,128)(2,1)} %bitcast.6), calls=%async_computation | async-start | bytes 1048576 | tf_op jit(solution)/shard_map/all_to_all | solution.py:336
  17.0 1.4 %fusion = (s32[]{:T(128)}, s32[1,32]{0,1:T(8,128)S(1)}) fusion(s32[128,32]{0,1:T(8,128)} %param.11, s32[]{:T(128)S(6)} %select_n.26), kind=kLoop, calls=%fused_computation.7 | loop fusion | flops 31 | bytes 264 | tf_op jit(solution)/shard_map/reduce_sum | solution.py:379
  19.1 0.1 copy.12.sizes_ref
  19.2 0.7 convert_element_type.3.forces_ref
  19.9 0.7 pad_add_fusion.info_ref
  20.7 0.7 multiply_bitcast_fusion.energies_ref
  21.3 7.9 %all-to-all-done = bf16[64,8,512]{2,1,0:T(8,128)(2,1)S(1)} async-done(((bf16[64,8,512]{2,1,0:T(8,128)(2,1)}), bf16[64,8,512]{2,1,0:T(8,128)(2,1)S(1)}, u32[]{:S(2)}, u32[]{:S(2)}) %all-to-all-start) | async-done | bytes 524320 | tf_op jit(solution)/shard_map/all_to_all | solution.py:336
  29.3 15.5 %all_to_all.20 = bf16[64,8,512]{2,1,0:T(8,128)(2,1)S(1)} all-to-all(bf16[64,8,512]{2,1,0:T(8,128)(2,1)S(1)} %broadcast_in_dim.7), channel_id=1, replica_groups=mesh['rows'=16,'z'=4,'core'=2] {'rows','z'}, dimensions={0} | all-to-all | bytes 1048576 | tf_op jit(solution)/shard_map/all_to_all | solution.py:336
  44.8 3.2 %collective-permute-start.1 = (bf16[256,1024]{1,0:T(8,128)(2,1)S(1)}, bf16[256,1024]{1,0:T(8,128)(2,1)S(1)}, u32[]{:S(2)}, u32[]{:S(2)}) collective-permute-start(bf16[256,1024]{1,0:T(8,128)(2,1)S(1)} %bitcast.27), channel_id=1, source_target_pairs={{0,1},{1,0},{2,3},{3,2},{4,5},{5,4},{6,7},{7,6},{8,9},{9,8},{10,11... | collective-permute-start | bytes 1572872 | tf_op jit(solution)/shard_map/ppermute | solution.py:340
  48.0 1.5 %collective-permute-done.1.other_ref = bf16[256,1024]{1,0:T(8,128)(2,1)S(1)} collective-permute-done((bf16[256,1024]{1,0:T(8,128)(2,1)S(1)}, bf16[256,1024]{1,0:T(8,128)(2,1)S(1)}, u32[]{:S(2)}, u32[]{:S(2)}) %collective-permute-start.1) | collective-permute-done | bytes 524320 | tf_op jit(solution)/shard_map/ppermute | solution.py:340
  49.6 13.2 %gram_halves.1 = (f32[704,128]{1,0:T(8,128)S(1)}, f32[704,128]{1,0:T(8,128)S(1)}) custom-call(s32[3]{0:T(128)S(1)} %pad_add_fusion.info_ref, s32[1,32]{1,0:T(1,128)S(1)} %copy.12.sizes_ref, f32[1,32]{1,0:T(1,128)S(1)} %multiply_bitcast_fusion.energies_ref, bf16[256,1024]{1,0:T(8,128)(2,1)S(1)} %bitcast.28, ...), custom_call_target="tpu_custom_call" | custom-call | tf_op jit(solution)/shard_map/gram_halves/pallas_call | solution.py:312
  62.7 0.5 collective-permute-start.2
  63.2 1.3 %collective-permute-done.2 = f32[704,128]{1,0:T(8,128)S(1)} collective-permute-done((f32[704,128]{1,0:T(8,128)S(1)}, f32[704,128]{1,0:T(8,128)S(1)}, u32[]{:S(2)}, u32[]{:S(2)}) %collective-permute-start.2) | collective-permute-done | bytes 360480 | tf_op jit(solution)/shard_map/ppermute | solution.py:340
  64.5 23.1 %all_to_all.21 = f32[64,1,1408]{2,1,0:T(1,128)S(1)} all-to-all(f32[64,1,1408]{2,1,0:T(1,128)S(1)} %bitcast.31), channel_id=1, replica_groups=mesh['rows'=16,'z'=4,'core'=2] {'rows','z'}, dimensions={0} | all-to-all | bytes 720896 | tf_op jit(solution)/shard_map/all_to_all | solution.py:336
  87.6 0.2 reduce_sum.19
  87.9 0.2 broadcast_in_dim.16
  88.0 14.6 %all_to_all.22 = f32[64,1,1408]{2,1,0:T(1,128)S(1)} all-to-all(f32[64,1,1408]{2,1,0:T(1,128)S(1)} %broadcast_in_dim.16), channel_id=1, replica_groups=mesh['rows'=16,'z'=4,'core'=2] {'rows','z'}, dimensions={0} | all-to-all | bytes 720896 | tf_op jit(solution)/shard_map/all_to_all | solution.py:336
  102.6 2.8 %collective-permute-start.3 = (f32[704,128]{1,0:T(8,128)S(1)}, f32[704,128]{1,0:T(8,128)S(1)}, u32[]{:S(2)}, u32[]{:S(2)}) collective-permute-start(f32[704,128]{1,0:T(8,128)S(1)} %bitcast.29), channel_id=1, source_target_pairs={{0,1},{1,0},{2,3},{3,2},{4,5},{5,4},{6,7},{7,6},{8,9},{9,8},{10,11... | collective-permute-start | bytes 1081352 | tf_op jit(solution)/shard_map/ppermute | solution.py:340
  105.5 1.3 %collective-permute-done.3.other_ref = f32[704,128]{1,0:T(8,128)S(1)} collective-permute-done((f32[704,128]{1,0:T(8,128)S(1)}, f32[704,128]{1,0:T(8,128)S(1)}, u32[]{:S(2)}, u32[]{:S(2)}) %collective-permute-start.3) | collective-permute-done | bytes 360480 | tf_op jit(solution)/shard_map/ppermute | solution.py:340
  106.8 15.4 %factor_and_solve.1 = (f32[512,512]{1,0:T(8,128)}, f32[4,128]{1,0:T(4,128)}) custom-call(s32[1]{0:T(128)} %bitcast.core_ref, f32[704,128]{1,0:T(8,128)S(1)} %bitcast.30, f32[704,128]{1,0:T(8,128)S(1)} %collective-permute-done.3.other_ref), custom_call_target="tpu_custom_call" | custom-call | tf_op jit(solution)/shard_map/factor_and_solve/pallas_call | solution.py:160
  (3 shorter events, 0.1 us)
Async XLA Ops:
  1.9 3.0 %collective-permute-start = (bf16[256,1024]{1,0:T(8,128)(2,1)S(1)}, bf16[256,1024]{1,0:T(8,128)(2,1)S(1)}, u32[]{:S(2)}, u32[]{:S(2)}) collective-permute-start(bf16[256,1024]{1,0:T(8,128)(2,1)S(1)} %get-tuple-element.22), channel_id=1, source_target_pairs={{0,1},{1,0},{2,3},{3,2},{4,5},{5,4},{6,7},{7,6},{8,9},{9,8},{10,11... | collective-permute-start | bytes 1572872 | tf_op jit(solution)/shard_map/ppermute | solution.py:340
  5.8 23.5 %all-to-all-start = ((bf16[64,8,512]{2,1,0:T(8,128)(2,1)}), bf16[64,8,512]{2,1,0:T(8,128)(2,1)S(1)}, u32[]{:S(2)}, u32[]{:S(2)}) async-start(bf16[64,8,512]{2,1,0:T(8,128)(2,1)} %bitcast.6), calls=%async_computation | async-start | bytes 1048576 | tf_op jit(solution)/shard_map/all_to_all | solution.py:336
  44.8 4.7 %collective-permute-start.1 = (bf16[256,1024]{1,0:T(8,128)(2,1)S(1)}, bf16[256,1024]{1,0:T(8,128)(2,1)S(1)}, u32[]{:S(2)}, u32[]{:S(2)}) collective-permute-start(bf16[256,1024]{1,0:T(8,128)(2,1)S(1)} %bitcast.27), channel_id=1, source_target_pairs={{0,1},{1,0},{2,3},{3,2},{4,5},{5,4},{6,7},{7,6},{8,9},{9,8},{10,11... | collective-permute-start | bytes 1572872 | tf_op jit(solution)/shard_map/ppermute | solution.py:340
  62.7 1.8 %collective-permute-start.2 = (f32[704,128]{1,0:T(8,128)S(1)}, f32[704,128]{1,0:T(8,128)S(1)}, u32[]{:S(2)}, u32[]{:S(2)}) collective-permute-start(f32[704,128]{1,0:T(8,128)S(1)} %get-tuple-element.17), channel_id=1, source_target_pairs={{0,1},{1,0},{2,3},{3,2},{4,5},{5,4},{6,7},{7,6},{8,9},{9,8},{10,11... | collective-permute-start | bytes 1081352 | tf_op jit(solution)/shard_map/ppermute | solution.py:340
  102.6 4.1 %collective-permute-start.3 = (f32[704,128]{1,0:T(8,128)S(1)}, f32[704,128]{1,0:T(8,128)S(1)}, u32[]{:S(2)}, u32[]{:S(2)}) collective-permute-start(f32[704,128]{1,0:T(8,128)S(1)} %bitcast.29), channel_id=1, source_target_pairs={{0,1},{1,0},{2,3},{3,2},{4,5},{5,4},{6,7},{7,6},{8,9},{9,8},{10,11... | collective-permute-start | bytes 1081352 | tf_op jit(solution)/shard_map/ppermute | solution.py:340

commit v5 on v4

--- a/solution.py
+++ b/solution.py
@@ -78,7 +78,7 @@
 
 
 def factor_kernel(
-    core_ref, own_ref, other_ref, factor_ref, solved_ref, work, done, packed, upper, sent
+    core_ref, own_ref, other_ref, factor_ref, solved_ref, work, done, packed
 ):
     points = factor_ref.shape[0]
     tiles = points // TILE
@@ -109,10 +109,6 @@
                 precision=lax.Precision.HIGHEST,
                 preferred_element_type=jnp.float32,
             )
-
-    def leaving(top):
-        panel = pl.ds(top, TILE)
-        return pltpu.make_async_copy(upper.at[panel], factor_ref.at[panel], sent.at[top // TILE])
 
     for start in range(0, points, GROUP):
         top = start - start % TILE
@@ -138,11 +134,9 @@
                 done[at : at + 8, top + t * TILE : top + (t + 1) * TILE] = rows[s][t]
             for t in range(tiles):
                 own = t - top // TILE
-                upper[at : at + 8, t * TILE : (t + 1) * TILE] = (
+                factor_ref[at : at + 8, t * TILE : (t + 1) * TILE] = (
                     rows[s][own] if own >= 0 else jnp.zeros((8, TILE), jnp.float32)
                 )
-        if follow % TILE == 0:
-            leaving(top).start()
         if follow % TILE:
             take_off(follow, GROUP, start, follow)
         elif follow < points:
@@ -151,8 +145,6 @@
     for t in range(tiles):
         flipped = jnp.transpose(done[t * TILE : (t + 1) * TILE, points:])
         solved_ref[t : t + 1, :] = flipped[0:1, :]
-    for t in range(tiles):
-        leaving(t * TILE).wait()
 
 
 def factor_and_solve(core, own, other, points):
@@ -168,13 +160,11 @@
             pl.BlockSpec(memory_space=pltpu.VMEM),
             pl.BlockSpec(memory_space=pltpu.VMEM),
         ],
-        out_specs=(pl.BlockSpec(memory_space=pl.ANY), pl.BlockSpec(memory_space=pltpu.VMEM)),
+        out_specs=(pl.BlockSpec(memory_space=pltpu.VMEM),) * 2,
         scratch_shapes=[
             pltpu.VMEM((points, points + TILE), jnp.float32),
             pltpu.VMEM((points, points + TILE), jnp.float32),
             pltpu.VMEM((2 * own.shape[0], TILE), jnp.float32),
-            pltpu.VMEM((points, points), jnp.float32),
-            pltpu.SemaphoreType.DMA((tiles,)),
         ],
         compiler_params=pltpu.CompilerParams(vmem_limit_bytes=32 * 1024 * 1024),
         name="factor_and_solve",
@@ -199,22 +189,30 @@
 
 
 def gram_kernel(
-    scale, weight, info_ref, sizes_ref, energies_ref, own_ref, other_ref, forces_ref, atoms_ref,
-    derivs_ref, keep_ref, send_ref, panel_ref, held, square, cross, rhs_part, energy_part, packed,
-    arrived,
+    scale, weight, device_ref, own_ref, other_ref, sizes_hbm, energies_hbm, forces_hbm, atoms_ref,
+    derivs_ref, keep_ref, send_ref, panel_ref, held, high, low, square, cross, rhs_part,
+    energy_part, packed, sizes_ref, energies_ref, forces_ref, arrived, small,
 ):
     points = panel_ref.shape[0]
-    blocks, block_rows = held.shape[1:3]
-    slots = sizes_ref.shape[1]
+    room, block_rows = held.shape[1:3]
+    slots = sizes_ref.shape[0]
     half = points // 2
-    core = info_ref[2]
+    device = device_ref[0]
+    core = lax.rem(device, 2)
 
     def copy(part, i):
         rows = pl.ds(pl.multiple_of(i * block_rows, block_rows), block_rows)
         source = derivs_ref.at[part - 1, rows] if part else atoms_ref.at[rows]
         return pltpu.make_async_copy(source, held.at[part, i], arrived.at[part, i])
 
-    for i in range(blocks):
+    first = [
+        pltpu.make_async_copy(sizes_hbm, sizes_ref, small.at[0]),
+        pltpu.make_async_copy(energies_hbm, energies_ref, small.at[1]),
+        pltpu.make_async_copy(forces_hbm, forces_ref, small.at[2]),
+    ]
+    for one in first:
+        one.start()
+    for i in range(room):
         for part in range(4):
             copy(part, i).start()
 
@@ -224,58 +222,71 @@
     cross[...] = jnp.zeros_like(cross)
     rhs_part[...] = jnp.zeros_like(rhs_part)
     energy_part[...] = jnp.zeros_like(energy_part)
+    for one in first:
+        one.wait()
+    every = lax.broadcasted_iota(jnp.int32, sizes_ref.shape, 1)
+    column = jnp.sum(jnp.where(every == device, sizes_ref[...], 0), axis=1, keepdims=True)
+    total = jnp.sum(column)
+    blocks = lax.div(total + (block_rows - 1), block_rows)
     before = lax.broadcasted_iota(jnp.int32, (slots, slots), 1)
     after = lax.broadcasted_iota(jnp.int32, (slots, slots), 0)
-    wide = jnp.broadcast_to(sizes_ref[...], (slots, slots))
+    tall = jnp.broadcast_to(column, (slots, slots))
+    sizes = jnp.sum(jnp.where(before == after, tall, 0), axis=0, keepdims=True)
+    wide = jnp.broadcast_to(sizes, (slots, slots))
     ends = jnp.sum(jnp.where(before <= after, wide, 0), axis=1, keepdims=True)
-    starts = jnp.sum(jnp.where(before < after, wide, 0), axis=1, keepdims=True)
-
-    @pl.loop(0, blocks)
+    starts = ends - column
+
+    def add_gram(lanes):
+        left = high[:, lanes]
+        square[:half, :] += against(left[:half], left)
+        square[half:, half:] += against(left[half:], left[half:])
+        cross[...] += against(left, low[:, lanes])
+
+    def visit(i, with_gram):
+        for part in range(4):
+            copy(part, i).wait()
+        panel = panel_ref[...]
+        slot = i * block_rows + lax.broadcasted_iota(jnp.int32, (slots, block_rows), 1)
+        member = jnp.where((slot >= starts) & (slot < ends), 1.0, 0.0).astype(jnp.bfloat16)
+        atom = i * block_rows + lax.broadcasted_iota(jnp.int32, (1, block_rows), 1)
+        live = jnp.where(atom < total, 1.0, 0.0)
+        scores = against(panel, held[0, i])
+        slopes = against(panel, held[1, i])
+        squares = scores * scores
+        kernel_high, kernel_low = split(squares * squares)
+        cubes = squares * scores * (live * (-4.0 * weight * scale**4))
+        rows = pl.ds(pl.multiple_of(i * block_rows, TILE), block_rows)
+        for c in range(3):
+            lanes = slice(c * block_rows, (c + 1) * block_rows)
+            if with_gram:
+                add_gram(lanes)
+            design = cubes * slopes
+            if c < 2:
+                slopes = against(panel, held[c + 2, i])
+            else:
+                energy_part[...] += against(kernel_high, member) + against(kernel_low, member)
+            high[:, lanes], low[:, lanes] = split(design)
+            term = design * forces_ref[c : c + 1, rows].astype(jnp.float32)
+            folded = rhs_part[...]
+            for t in range(block_rows // TILE):
+                folded = folded + term[:, t * TILE : (t + 1) * TILE]
+            rhs_part[...] = folded
+
+    visit(0, False)
+
+    @pl.loop(1, blocks)
     def _(i):
-        copy(0, i).wait()
-
-        @pl.when(i < info_ref[1])
-        def _():
-            panel = panel_ref[...]
-            slot = i * block_rows + lax.broadcasted_iota(jnp.int32, (slots, block_rows), 1)
-            member = jnp.where((slot >= starts) & (slot < ends), 1.0, 0.0).astype(jnp.bfloat16)
-            atom = i * block_rows + lax.broadcasted_iota(jnp.int32, (1, block_rows), 1)
-            live = jnp.where(atom < info_ref[0], 1.0, 0.0)
-            scores = against(panel, held[0, i])
-            for part in range(1, 4):
-                copy(part, i).wait()
-            slopes = against(panel, held[1, i])
-            squares = scores * scores
-            kernel_high, kernel_low = split(squares * squares)
-            cubes = squares * scores * (live * (-4.0 * weight * scale**4))
-            pairs = []
-            folded = rhs_part[...]
-            for c in range(3):
-                design = cubes * slopes
-                if c < 2:
-                    slopes = against(panel, held[c + 2, i])
-                else:
-                    energy_part[...] += against(kernel_high, member) + against(kernel_low, member)
-                pairs.append(split(design))
-                forces = forces_ref[c : c + 1, pl.ds(pl.multiple_of(i * block_rows, TILE), block_rows)]
-                term = design * forces
-                for t in range(block_rows // TILE):
-                    folded = folded + term[:, t * TILE : (t + 1) * TILE]
-            rhs_part[...] = folded
-            high = jnp.concatenate([pair[0] for pair in pairs], axis=1)
-            low = jnp.concatenate([pair[1] for pair in pairs], axis=1)
-            square[:half, :] += against(high[:half], high)
-            square[half:, half:] += against(high[half:], high[half:])
-            cross[...] += against(high, low)
-
-        @pl.when(i >= info_ref[1])
-        def _():
-            for part in range(1, 4):
-                copy(part, i).wait()
-
-    norms = jnp.sqrt(jnp.maximum(sizes_ref[...], 1).astype(jnp.float32))
-    energy_ratio = energy_part[...] / norms
-    energy_rows = energy_ratio * (weight * scale**4)
+        visit(i, True)
+
+    add_gram(slice(None))
+
+    @pl.loop(blocks, room)
+    def _(i):
+        for part in range(4):
+            copy(part, i).wait()
+
+    norms = jnp.sqrt(jnp.maximum(sizes, 1).astype(jnp.float32))
+    energy_rows = energy_part[...] * (weight * scale**4) / norms
     gram = square[...] + cross[...] + jnp.transpose(cross[...])
     gram = gram + against(energy_rows, energy_rows, exact_mode)
     tiles = points // TILE
@@ -287,7 +298,7 @@
     ones = jnp.ones((8, TILE), jnp.float32)
     rhs = against(ones, rhs_part[...], exact_mode)
     rhs = rhs + against(
-        jnp.broadcast_to(energies_ref[...], (8, slots)), energy_ratio, exact_mode
+        jnp.broadcast_to(energies_ref[...], (8, slots)), energy_rows, exact_mode
     )
     for t in range(tiles):
         at = len(places) * TILE + t
@@ -297,36 +308,38 @@
     send_ref[...] = packed[pl.ds(pl.multiple_of((1 - core) * count, 8), count), :]
 
 
-def block_rows_of(capacity):
-    return min(512, capacity)
-
-
-def gram_halves(info, sizes, energies, own, other, atoms, derivs, forces, scale, weight, rows):
+def gram_halves(device, own, other, sizes, energies, forces, atoms, derivs, scale, weight, rows):
     capacity, width = atoms.shape
     points = 2 * own.shape[0]
-    slots = sizes.shape[1]
-    block_rows = block_rows_of(capacity)
+    slots = sizes.shape[0]
+    block_rows = min(512, capacity)
     blocks = capacity // block_rows
     in_vmem = pl.BlockSpec(memory_space=pltpu.VMEM)
     anywhere = pl.BlockSpec(memory_space=pl.ANY)
     return pl.pallas_call(
         functools.partial(gram_kernel, scale, weight),
         out_shape=(jax.ShapeDtypeStruct((rows // 2, TILE), jnp.float32),) * 2,
-        in_specs=[pl.BlockSpec(memory_space=pltpu.SMEM)] + [in_vmem] * 5 + [anywhere] * 2,
+        in_specs=[pl.BlockSpec(memory_space=pltpu.SMEM)] + [in_vmem] * 2 + [anywhere] * 5,
         out_specs=(in_vmem,) * 2,
         scratch_shapes=[
             pltpu.VMEM((points, width), jnp.bfloat16),
             pltpu.VMEM((4, blocks, block_rows, width), jnp.bfloat16),
+            pltpu.VMEM((points, 3 * block_rows), jnp.bfloat16),
+            pltpu.VMEM((points, 3 * block_rows), jnp.bfloat16),
             pltpu.VMEM((points, points), jnp.float32),
             pltpu.VMEM((points, points), jnp.float32),
             pltpu.VMEM((points, TILE), jnp.float32),
             pltpu.VMEM((points, slots), jnp.float32),
             pltpu.VMEM((rows, TILE), jnp.float32),
+            pltpu.VMEM(sizes.shape, jnp.int32),
+            pltpu.VMEM((1, slots), jnp.float32),
+            pltpu.VMEM(forces.shape, forces.dtype),
             pltpu.SemaphoreType.DMA((4, blocks)),
+            pltpu.SemaphoreType.DMA((3,)),
         ],
         compiler_params=pltpu.CompilerParams(vmem_limit_bytes=50 * 1024 * 1024),
         name="gram_halves",
-    )(info, sizes, energies, own, other, forces, atoms, derivs)
+    )(device, own, other, sizes, energies, forces, atoms, derivs)
 CHIPS = ("rows", "z")
 EVERY = ("rows", "z", "core")
 ridge_total = 1.0
@@ -340,7 +353,7 @@
     return lax.ppermute(value, "core", [(0, 1), (1, 0)])
 
 
-def panel_halves(panels, owner, others):
+def panel_halves(panels, owner):
     core = lax.axis_index("core")
     chips = lax.axis_size(CHIPS)
     points, width = panels.shape
@@ -353,10 +366,9 @@
     cut = held.reshape(tall, 8, wide, width // wide).transpose(0, 2, 1, 3)
     pieces = exchange(cut.reshape(chips, 8, width // wide), CHIPS)
     piece = lax.dynamic_index_in_dim(pieces, lax.div(owner, 2), 0, keepdims=True)
-    piece, others = lax.optimization_barrier((piece, others))
     own = exchange(jnp.broadcast_to(piece, pieces.shape), CHIPS)
     own = own.reshape(tall, wide, 8, width // wide).transpose(0, 2, 1, 3).reshape(half, width)
-    return own, swap(own), others
+    return own, swap(own)
 
 
 def sum_halves(keep, send):
@@ -375,25 +387,16 @@
     core = lax.axis_index("core")
     scale = 1.0 / math.sqrt(width)
     weight = 1.0 / math.sqrt(48.0 * capacity * lax.axis_size(EVERY))
-    sizes = lax.dynamic_slice_in_dim(struct_atoms, lax.axis_index(EVERY), 1, 0)
-    total = jnp.sum(sizes)
-    block_rows = block_rows_of(capacity)
-    blocks = lax.div(total + (block_rows - 1), block_rows)
-    info = jnp.stack([total, blocks, core]).astype(jnp.int32)
-    scaled = energies[None, :] * (weight * scale**4)
-    forces = force_targets.astype(jnp.float32)
-    own, other, (info, sizes, scaled, forces) = panel_halves(
-        sparse_points[0], owner[0], (info, sizes, scaled, forces)
-    )
+    own, other = panel_halves(sparse_points[0], owner[0])
     keep, send = gram_halves(
-        info,
-        sizes,
-        scaled,
+        lax.axis_index(EVERY).reshape(1),
         own,
         other,
+        struct_atoms.T,
+        energies[None, :],
+        force_targets,
         descriptors,
         derivatives,
-        forces,
         scale,
         weight,
         packed_rows(points, lax.axis_size(EVERY)),

time: 123 us -> 124 us (level)
  waiting for transfers between devices: 13 us -> 17.2 us
  other arithmetic: 4.67 us -> 1.12 us
  local copies, waits for them, and re-layouts: 1.58 us -> 3.59 us
    all_to_all x1, waiting for transfers between devices: 7.94 us -> 12.2 us  [exchange(): return lax.all_to_all(pieces, axes, 0, 0, tiled=True)]
    unnamed x0 -> x6, local copies, waits for them, and re-layouts: none -> 2.09 us
    reduce_sum x1 -> x0, other arithmetic: 1.43 us -> none  [per_device(): total = jnp.sum(sizes)]
  transfers between devices with their start and end apart: 5 -> 5, of which waited for: 5 -> 5; matrix products, arithmetic and copies ran while one was open for 3% -> 0% of each run, Pallas kernels for 0% -> 0%
where the time goes in v5:
time: 124 us
  blocking collectives  52.6 us (42%)
  Pallas kernels  28.7 us (23%)
  starting transfers between devices  19.2 us (15%)
  waiting for transfers between devices  17.2 us (14%)
  local copies, waits for them, and re-layouts  3.59 us (3%)
  between operations  1.36 us (1%)
    all_to_all x3, blocking collectives, exchange(): return lax.all_to_all(pieces, axes, 0, 0, tiled=True)  52.6 us
    pallas_call x1, Pallas kernels, factor_and_solve(): pl.pallas_call(factor_kernel, out_shape=(jax.ShapeDtypeStruct((points, po...  15.1 us
    pallas_call x1, Pallas kernels, gram_halves(): pl.pallas_call(functools.partial(gram_kernel, scale, weight), out_shape=(...  13.5 us
    all_to_all x1, waiting for transfers between devices, exchange(): return lax.all_to_all(pieces, axes, 0, 0, tiled=True)  12.2 us
    all_to_all x1, starting transfers between devices, exchange(): return lax.all_to_all(pieces, axes, 0, 0, tiled=True)  11.2 us
    ppermute x4, starting transfers between devices, swap(): return lax.ppermute(value, 'core', [(0, 1), (1, 0)])  7.98 us
    ppermute x4, waiting for transfers between devices, swap(): return lax.ppermute(value, 'core', [(0, 1), (1, 0)])  5.02 us
  transfers between devices with their start and end apart: 5, of which 5 were waited for; matrix products, arithmetic and copies ran while one was open for 0% of the time, Pallas kernels for 0%

profile of v5, /device:TPU:1, one launch (start us, length us, event | category | flops | bytes accessed | tf_op | source)
XLA Modules:
  0.0 123.8 jit_solution(1159670378271600817)
XLA Ops:
  0.6 1.3 %dynamic-slice_bitcast_fusion = (bf16[256,1024]{1,0:T(8,128)(2,1)S(1)}, bf16[256,1024]{1,0:T(8,128)(2,1)S(1)}) fusion(bf16[1,512,1024]{2,1,0:T(8,128)(2,1)} %param.12, s32[]{:T(128)S(6)} %select_n.20, s32[]{:T(128)S(6)} %select_n.19), kind=kLoop, calls=%fused_computation | loop fusion | bytes 2097160 | tf_op jit(solution)/shard_map/dynamic_slice | solution.py:361
  1.9 1.5 %collective-permute-start = (bf16[256,1024]{1,0:T(8,128)(2,1)S(1)}, bf16[256,1024]{1,0:T(8,128)(2,1)S(1)}, u32[]{:S(2)}, u32[]{:S(2)}) collective-permute-start(bf16[256,1024]{1,0:T(8,128)(2,1)S(1)} %get-tuple-element.10), channel_id=1, source_target_pairs={{0,1},{1,0},{2,3},{3,2},{4,5},{5,4},{6,7},{7,6},{8,9},{9,8},{10,11... | collective-permute-start | bytes 1572872 | tf_op jit(solution)/shard_map/ppermute | solution.py:353
  4.1 0.9 collective-permute-done
  5.0 0.8 broadcast_select_fusion
  5.8 11.2 %all-to-all-start = ((bf16[64,8,512]{2,1,0:T(8,128)(2,1)}), bf16[64,8,512]{2,1,0:T(8,128)(2,1)S(1)}, u32[]{:S(2)}, u32[]{:S(2)}) async-start(bf16[64,8,512]{2,1,0:T(8,128)(2,1)} %bitcast.7), calls=%async_computation | async-start | bytes 1048576 | tf_op jit(solution)/shard_map/all_to_all | solution.py:349
  17.0 12.2 %all-to-all-done = bf16[64,8,512]{2,1,0:T(8,128)(2,1)S(1)} async-done(((bf16[64,8,512]{2,1,0:T(8,128)(2,1)}), bf16[64,8,512]{2,1,0:T(8,128)(2,1)S(1)}, u32[]{:S(2)}, u32[]{:S(2)}) %all-to-all-start) | async-done | bytes 524320 | tf_op jit(solution)/shard_map/all_to_all | solution.py:349
  29.3 15.5 %all_to_all.20 = bf16[64,8,512]{2,1,0:T(8,128)(2,1)S(1)} all-to-all(bf16[64,8,512]{2,1,0:T(8,128)(2,1)S(1)} %broadcast_in_dim.17), channel_id=1, replica_groups=mesh['rows'=16,'z'=4,'core'=2] {'rows','z'}, dimensions={0} | all-to-all | bytes 1048576 | tf_op jit(solution)/shard_map/all_to_all | solution.py:349
  44.8 3.2 %collective-permute-start.1 = (bf16[256,1024]{1,0:T(8,128)(2,1)S(1)}, bf16[256,1024]{1,0:T(8,128)(2,1)S(1)}, u32[]{:S(2)}, u32[]{:S(2)}) collective-permute-start(bf16[256,1024]{1,0:T(8,128)(2,1)S(1)} %bitcast.27), channel_id=1, source_target_pairs={{0,1},{1,0},{2,3},{3,2},{4,5},{5,4},{6,7},{7,6},{8,9},{9,8},{10,11... | collective-permute-start | bytes 1572872 | tf_op jit(solution)/shard_map/ppermute | solution.py:353
  48.0 1.5 %collective-permute-done.1.other_ref = bf16[256,1024]{1,0:T(8,128)(2,1)S(1)} collective-permute-done((bf16[256,1024]{1,0:T(8,128)(2,1)S(1)}, bf16[256,1024]{1,0:T(8,128)(2,1)S(1)}, u32[]{:S(2)}, u32[]{:S(2)}) %collective-permute-start.1) | collective-permute-done | bytes 524320 | tf_op jit(solution)/shard_map/ppermute | solution.py:353
  49.6 0.0 copy-start
  49.6 0.7 copy-done
  50.3 0.0 copy-start.1
  50.3 0.7 copy-done.1
  51.0 0.0 copy-start.2
  51.0 0.7 copy-done.2
  51.7 13.5 %gram_halves.1 = (f32[704,128]{1,0:T(8,128)S(1)}, f32[704,128]{1,0:T(8,128)S(1)}) custom-call(s32[1]{0:T(128)} %bitcast.1.device_ref, bf16[256,1024]{1,0:T(8,128)(2,1)S(1)} %bitcast.28, bf16[256,1024]{1,0:T(8,128)(2,1)S(1)} %collective-permute-done.1.other_ref, s32[32,128]{1,0:T(8,128)S(1)} %bitcast.31, f32[1,32]{1,0:T(1,128)S(1)} %bitcast.32, ...), custom_call_target="tpu_custom_call" | custom-call | tf_op jit(solution)/shard_map/gram_halves/pallas_call | solution.py:319
  65.2 0.4 collective-permute-start.2
  65.7 1.3 %collective-permute-done.2 = f32[704,128]{1,0:T(8,128)S(1)} collective-permute-done((f32[704,128]{1,0:T(8,128)S(1)}, f32[704,128]{1,0:T(8,128)S(1)}, u32[]{:S(2)}, u32[]{:S(2)}) %collective-permute-start.2) | collective-permute-done | bytes 360480 | tf_op jit(solution)/shard_map/ppermute | solution.py:353
  67.0 22.5 %all_to_all.21 = f32[64,1,1408]{2,1,0:T(1,128)S(1)} all-to-all(f32[64,1,1408]{2,1,0:T(1,128)S(1)} %bitcast.33), channel_id=1, replica_groups=mesh['rows'=16,'z'=4,'core'=2] {'rows','z'}, dimensions={0} | all-to-all | bytes 720896 | tf_op jit(solution)/shard_map/all_to_all | solution.py:349
  89.5 0.2 reduce_sum.9
  89.7 0.2 broadcast_in_dim.19
  89.9 14.6 %all_to_all.22 = f32[64,1,1408]{2,1,0:T(1,128)S(1)} all-to-all(f32[64,1,1408]{2,1,0:T(1,128)S(1)} %broadcast_in_dim.19), channel_id=1, replica_groups=mesh['rows'=16,'z'=4,'core'=2] {'rows','z'}, dimensions={0} | all-to-all | bytes 720896 | tf_op jit(solution)/shard_map/all_to_all | solution.py:349
  104.5 2.8 %collective-permute-start.3 = (f32[704,128]{1,0:T(8,128)S(1)}, f32[704,128]{1,0:T(8,128)S(1)}, u32[]{:S(2)}, u32[]{:S(2)}) collective-permute-start(f32[704,128]{1,0:T(8,128)S(1)} %bitcast.29), channel_id=1, source_target_pairs={{0,1},{1,0},{2,3},{3,2},{4,5},{5,4},{6,7},{7,6},{8,9},{9,8},{10,11... | collective-permute-start | bytes 1081352 | tf_op jit(solution)/shard_map/ppermute | solution.py:353
  107.3 1.3 %collective-permute-done.3.other_ref = f32[704,128]{1,0:T(8,128)S(1)} collective-permute-done((f32[704,128]{1,0:T(8,128)S(1)}, f32[704,128]{1,0:T(8,128)S(1)}, u32[]{:S(2)}, u32[]{:S(2)}) %collective-permute-start.3) | collective-permute-done | bytes 360480 | tf_op jit(solution)/shard_map/ppermute | solution.py:353
  108.7 15.1 %factor_and_solve.1 = (f32[512,512]{1,0:T(8,128)}, f32[4,128]{1,0:T(4,128)}) custom-call(s32[1]{0:T(128)} %bitcast.core_ref, f32[704,128]{1,0:T(8,128)S(1)} %bitcast.30, f32[704,128]{1,0:T(8,128)S(1)} %collective-permute-done.3.other_ref), custom_call_target="tpu_custom_call" | custom-call | tf_op jit(solution)/shard_map/factor_and_solve/pallas_call | solution.py:152
  (3 shorter events, 0.1 us)
Async XLA Ops:
  1.9 3.0 %collective-permute-start = (bf16[256,1024]{1,0:T(8,128)(2,1)S(1)}, bf16[256,1024]{1,0:T(8,128)(2,1)S(1)}, u32[]{:S(2)}, u32[]{:S(2)}) collective-permute-start(bf16[256,1024]{1,0:T(8,128)(2,1)S(1)} %get-tuple-element.10), channel_id=1, source_target_pairs={{0,1},{1,0},{2,3},{3,2},{4,5},{5,4},{6,7},{7,6},{8,9},{9,8},{10,11... | collective-permute-start | bytes 1572872 | tf_op jit(solution)/shard_map/ppermute | solution.py:353
  5.8 23.5 %all-to-all-start = ((bf16[64,8,512]{2,1,0:T(8,128)(2,1)}), bf16[64,8,512]{2,1,0:T(8,128)(2,1)S(1)}, u32[]{:S(2)}, u32[]{:S(2)}) async-start(bf16[64,8,512]{2,1,0:T(8,128)(2,1)} %bitcast.7), calls=%async_computation | async-start | bytes 1048576 | tf_op jit(solution)/shard_map/all_to_all | solution.py:349
  44.8 4.7 %collective-permute-start.1 = (bf16[256,1024]{1,0:T(8,128)(2,1)S(1)}, bf16[256,1024]{1,0:T(8,128)(2,1)S(1)}, u32[]{:S(2)}, u32[]{:S(2)}) collective-permute-start(bf16[256,1024]{1,0:T(8,128)(2,1)S(1)} %bitcast.27), channel_id=1, source_target_pairs={{0,1},{1,0},{2,3},{3,2},{4,5},{5,4},{6,7},{7,6},{8,9},{9,8},{10,11... | collective-permute-start | bytes 1572872 | tf_op jit(solution)/shard_map/ppermute | solution.py:353
  49.6 0.7 copy-start
  50.3 0.7 copy-start.1
  51.0 0.7 copy-start.2
  65.2 1.8 %collective-permute-start.2 = (f32[704,128]{1,0:T(8,128)S(1)}, f32[704,128]{1,0:T(8,128)S(1)}, u32[]{:S(2)}, u32[]{:S(2)}) collective-permute-start(f32[704,128]{1,0:T(8,128)S(1)} %get-tuple-element.7), channel_id=1, source_target_pairs={{0,1},{1,0},{2,3},{3,2},{4,5},{5,4},{6,7},{7,6},{8,9},{9,8},{10,11... | collective-permute-start | bytes 1081352 | tf_op jit(solution)/shard_map/ppermute | solution.py:353
  104.5 4.1 %collective-permute-start.3 = (f32[704,128]{1,0:T(8,128)S(1)}, f32[704,128]{1,0:T(8,128)S(1)}, u32[]{:S(2)}, u32[]{:S(2)}) collective-permute-start(f32[704,128]{1,0:T(8,128)S(1)} %bitcast.29), channel_id=1, source_target_pairs={{0,1},{1,0},{2,3},{3,2},{4,5},{5,4},{6,7},{7,6},{8,9},{9,8},{10,11... | collective-permute-start | bytes 1081352 | tf_op jit(solution)/shard_map/ppermute | solution.py:353

commit v6 on v2

--- a/solution.py
+++ b/solution.py
@@ -10,6 +10,7 @@
 
 TILE = 128
 GROUP = 32
+PART = 16
 
 
 def spread_lane(value, lane):
@@ -37,17 +38,22 @@
 def factor_group(rows, first):
     groups = GROUP // 8
     sub = lax.broadcasted_iota(jnp.int32, (8, TILE), 0)
-    columns = [
-        [spread_lane(rows[s][0], first + j) if s >= j // 8 else None for s in range(groups)]
-        for j in range(GROUP)
-    ]
     pivots = [jnp.ones((8, TILE), jnp.float32) for _ in range(groups)]
     for k in range(0, GROUP, 2):
+        if k % PART == 0:
+            columns = {
+                j: [spread_lane(rows[s][0], first + j) if s >= j // 8 else None for s in range(groups)]
+                for j in range(k, k + PART)
+            }
+        if k % 8 == 0:
+            corner = {
+                (i, j): spread_row(columns[j][k // 8], i % 8)
+                for j in range(k, k + 8)
+                for i in range(j, k + 8)
+            }
         s0, r0, r1 = k // 8, k % 8, k % 8 + 1
         one, two = columns[k], columns[k + 1]
-        a = spread_row(one[s0], r0)
-        b = spread_row(one[s0], r1)
-        c = spread_row(two[s0], r1)
+        a, b, c = corner[k, k], corner[k + 1, k], corner[k + 1, k + 1]
         det = a * c - b * b
         inv_a = inverse_of(a)
         inv_det = inverse_of(det)
@@ -57,11 +63,19 @@
         two_next = {s: two[s] - one[s] * ratio for s in live}
         m1 = {s: one[s] * inv_a for s in live}
         m2 = {s: two_next[s] * inv_s for s in live}
-        for j in range(k + 2, GROUP):
-            sj, rj = j // 8, j % 8
-            u1 = spread_row(one[sj], rj)
-            u2 = spread_row(two[sj], rj) - u1 * ratio
-            for s in range(sj, groups):
+        factors = {}
+        for j in range(k + 2, k - k % PART + PART):
+            if (j, k) in corner:
+                u1, raw = corner[j, k], corner[j, k + 1]
+            else:
+                u1, raw = spread_row(one[j // 8], j % 8), spread_row(two[j // 8], j % 8)
+            factors[j] = (u1, raw - u1 * ratio)
+        for i, j in corner:
+            if j > k + 1:
+                (u1, u2), (v1, v2) = factors[i], factors[j]
+                corner[i, j] = corner[i, j] - (u1 * inv_a) * v1 - (u2 * inv_s) * v2
+        for j, (u1, u2) in factors.items():
+            for s in range(j // 8, groups):
                 columns[j][s] = columns[j][s] - m1[s] * u1 - m2[s] * u2
         pivots[s0] = jnp.where(sub == r0, a, jnp.where(sub == r1, det * inv_a, pivots[s0]))
         m1[s0] = jnp.where(sub > r0, m1[s0], 0.0)
@@ -75,7 +89,9 @@
     return [[piece * scales[s] for piece in rows[s]] for s in range(groups)]
 
 
-def factor_kernel(core_ref, own_ref, other_ref, factor_ref, solved_ref, work, done, packed):
+def factor_kernel(
+    core_ref, own_ref, other_ref, factor_ref, solved_ref, work, done, packed
+):
     points = factor_ref.shape[0]
     tiles = points // TILE
     half = own_ref.shape[0]
@@ -306,7 +322,7 @@
                 pltpu.VMEM((rows, TILE), jnp.float32),
             ],
         ),
-        compiler_params=pltpu.CompilerParams(vmem_limit_bytes=58 * 1024 * 1024),
+        compiler_params=pltpu.CompilerParams(vmem_limit_bytes=50 * 1024 * 1024),
         name="gram_halves",
     )(info, sizes, energies, own, other, atoms, derivs, forces)
 CHIPS = ("rows", "z")

time: 126 us -> 123 us (0.976)
  Pallas kernels: 31.5 us -> 25.1 us
  blocking collectives: 47.5 us -> 51.8 us
  other arithmetic: 7.25 us -> 4.67 us
  waiting for transfers between devices: 11 us -> 12.9 us
  local copies, waits for them, and re-layouts: 2.95 us -> 1.58 us
    pallas_call x1, Pallas kernels: 14.2 us -> 8.76 us  [gram_halves(): pl.pallas_call(functools.partial(gram_kernel, scale, weight), out_shape=(...]
    all_to_all x3, blocking collectives: 47.5 us -> 51.8 us  [exchange(): return lax.all_to_all(pieces, axes, 0, 0, tiled=True)]
    all_to_all x1, waiting for transfers between devices: 5.77 us -> 7.94 us  [exchange(): return lax.all_to_all(pieces, axes, 0, 0, tiled=True)]
  transfers between devices with their start and end apart: 5 -> 5, of which waited for: 5 -> 5; matrix products, arithmetic and copies ran while one was open for 5% -> 3% of each run, Pallas kernels for 0% -> 0%
where the time goes in v6:
time: 123 us; the launch traced here: 122 us
  blocking collectives  51.8 us (42%)
  Pallas kernels  25.1 us (20%)
  starting transfers between devices  23.6 us (19%)
  waiting for transfers between devices  12.9 us (10%)
  other arithmetic  4.67 us (4%)
  between operations  2.02 us (2%)
  local copies, waits for them, and re-layouts  1.58 us (1%)
    all_to_all x3, blocking collectives, exchange(): return lax.all_to_all(pieces, axes, 0, 0, tiled=True)  51.8 us
    pallas_call x1, Pallas kernels, factor_and_solve(): pl.pallas_call(factor_kernel, out_shape=(jax.ShapeDtypeStruct((points, po...  16.4 us
    ppermute x4, starting transfers between devices, swap(): return lax.ppermute(value, 'core', [(0, 1), (1, 0)])  12.4 us
    all_to_all x1, starting transfers between devices, exchange(): return lax.all_to_all(pieces, axes, 0, 0, tiled=True)  11.2 us
    pallas_call x1, Pallas kernels, gram_halves(): pl.pallas_call(functools.partial(gram_kernel, scale, weight), out_shape=(...  8.76 us
    all_to_all x1, waiting for transfers between devices, exchange(): return lax.all_to_all(pieces, axes, 0, 0, tiled=True)  7.94 us
    ppermute x4, waiting for transfers between devices, swap(): return lax.ppermute(value, 'core', [(0, 1), (1, 0)])  5.01 us
  transfers between devices with their start and end apart: 5, of which 5 were waited for; matrix products, arithmetic and copies ran while one was open for 3% of the time, Pallas kernels for 0%

profile of v6, /device:TPU:1, one launch (start us, length us, event | category | flops | bytes accessed | tf_op | source)
XLA Modules:
  0.0 121.8 jit_solution(11040071499129060493)
XLA Ops:
  0.6 1.3 %dynamic-slice_bitcast_fusion = (bf16[256,1024]{1,0:T(8,128)(2,1)S(1)}, bf16[256,1024]{1,0:T(8,128)(2,1)S(1)}) fusion(bf16[1,512,1024]{2,1,0:T(8,128)(2,1)} %param.12, s32[]{:T(128)S(6)} %select_n.23, s32[]{:T(128)S(6)} %select_n.22), kind=kLoop, calls=%fused_computation | loop fusion | bytes 2097160 | tf_op jit(solution)/shard_map/dynamic_slice | solution.py:346
  1.9 1.5 %collective-permute-start = (bf16[256,1024]{1,0:T(8,128)(2,1)S(1)}, bf16[256,1024]{1,0:T(8,128)(2,1)S(1)}, u32[]{:S(2)}, u32[]{:S(2)}) collective-permute-start(bf16[256,1024]{1,0:T(8,128)(2,1)S(1)} %get-tuple-element.22), channel_id=1, source_target_pairs={{0,1},{1,0},{2,3},{3,2},{4,5},{5,4},{6,7},{7,6},{8,9},{9,8},{10,11... | collective-permute-start | bytes 1572872 | tf_op jit(solution)/shard_map/ppermute | solution.py:338
  4.1 0.9 collective-permute-done
  5.0 0.8 broadcast_select_fusion
  5.8 11.2 %all-to-all-start = ((bf16[64,8,512]{2,1,0:T(8,128)(2,1)}), bf16[64,8,512]{2,1,0:T(8,128)(2,1)S(1)}, u32[]{:S(2)}, u32[]{:S(2)}) async-start(bf16[64,8,512]{2,1,0:T(8,128)(2,1)} %bitcast.6), calls=%async_computation | async-start | bytes 1048576 | tf_op jit(solution)/shard_map/all_to_all | solution.py:334
  17.0 1.4 %fusion = (s32[]{:T(128)}, s32[1,32]{0,1:T(8,128)S(1)}) fusion(s32[128,32]{0,1:T(8,128)} %param.11, s32[]{:T(128)S(6)} %select_n.26), kind=kLoop, calls=%fused_computation.7 | loop fusion | flops 31 | bytes 264 | tf_op jit(solution)/shard_map/reduce_sum | solution.py:377
  19.1 0.1 copy.12.sizes_ref
  19.2 0.7 convert_element_type.3.forces_ref
  19.9 0.7 pad_add_fusion.info_ref
  20.7 0.7 multiply_bitcast_fusion.energies_ref
  21.3 7.9 %all-to-all-done = bf16[64,8,512]{2,1,0:T(8,128)(2,1)S(1)} async-done(((bf16[64,8,512]{2,1,0:T(8,128)(2,1)}), bf16[64,8,512]{2,1,0:T(8,128)(2,1)S(1)}, u32[]{:S(2)}, u32[]{:S(2)}) %all-to-all-start) | async-done | bytes 524320 | tf_op jit(solution)/shard_map/all_to_all | solution.py:334
  29.3 15.5 %all_to_all.20 = bf16[64,8,512]{2,1,0:T(8,128)(2,1)S(1)} all-to-all(bf16[64,8,512]{2,1,0:T(8,128)(2,1)S(1)} %broadcast_in_dim.7), channel_id=1, replica_groups=mesh['rows'=16,'z'=4,'core'=2] {'rows','z'}, dimensions={0} | all-to-all | bytes 1048576 | tf_op jit(solution)/shard_map/all_to_all | solution.py:334
  44.8 3.2 %collective-permute-start.1 = (bf16[256,1024]{1,0:T(8,128)(2,1)S(1)}, bf16[256,1024]{1,0:T(8,128)(2,1)S(1)}, u32[]{:S(2)}, u32[]{:S(2)}) collective-permute-start(bf16[256,1024]{1,0:T(8,128)(2,1)S(1)} %bitcast.27), channel_id=1, source_target_pairs={{0,1},{1,0},{2,3},{3,2},{4,5},{5,4},{6,7},{7,6},{8,9},{9,8},{10,11... | collective-permute-start | bytes 1572872 | tf_op jit(solution)/shard_map/ppermute | solution.py:338
  48.0 1.5 %collective-permute-done.1.other_ref = bf16[256,1024]{1,0:T(8,128)(2,1)S(1)} collective-permute-done((bf16[256,1024]{1,0:T(8,128)(2,1)S(1)}, bf16[256,1024]{1,0:T(8,128)(2,1)S(1)}, u32[]{:S(2)}, u32[]{:S(2)}) %collective-permute-start.1) | collective-permute-done | bytes 524320 | tf_op jit(solution)/shard_map/ppermute | solution.py:338
  49.6 8.8 %gram_halves.1 = (f32[704,128]{1,0:T(8,128)S(1)}, f32[704,128]{1,0:T(8,128)S(1)}) custom-call(s32[3]{0:T(128)S(1)} %pad_add_fusion.info_ref, s32[1,32]{1,0:T(1,128)S(1)} %copy.12.sizes_ref, f32[1,32]{1,0:T(1,128)S(1)} %multiply_bitcast_fusion.energies_ref, bf16[256,1024]{1,0:T(8,128)(2,1)S(1)} %bitcast.28, ...), custom_call_target="tpu_custom_call" | custom-call | tf_op jit(solution)/shard_map/gram_halves/pallas_call | solution.py:300
  58.3 4.6 %collective-permute-start.2 = (f32[704,128]{1,0:T(8,128)S(1)}, f32[704,128]{1,0:T(8,128)S(1)}, u32[]{:S(2)}, u32[]{:S(2)}) collective-permute-start(f32[704,128]{1,0:T(8,128)S(1)} %get-tuple-element.17), channel_id=1, source_target_pairs={{0,1},{1,0},{2,3},{3,2},{4,5},{5,4},{6,7},{7,6},{8,9},{9,8},{10,11... | collective-permute-start | bytes 1081352 | tf_op jit(solution)/shard_map/ppermute | solution.py:338
  62.9 1.3 %collective-permute-done.2 = f32[704,128]{1,0:T(8,128)S(1)} collective-permute-done((f32[704,128]{1,0:T(8,128)S(1)}, f32[704,128]{1,0:T(8,128)S(1)}, u32[]{:S(2)}, u32[]{:S(2)}) %collective-permute-start.2) | collective-permute-done | bytes 360480 | tf_op jit(solution)/shard_map/ppermute | solution.py:338
  64.3 21.7 %all_to_all.21 = f32[64,1,1408]{2,1,0:T(1,128)S(1)} all-to-all(f32[64,1,1408]{2,1,0:T(1,128)S(1)} %bitcast.31), channel_id=1, replica_groups=mesh['rows'=16,'z'=4,'core'=2] {'rows','z'}, dimensions={0} | all-to-all | bytes 720896 | tf_op jit(solution)/shard_map/all_to_all | solution.py:334
  86.0 0.2 reduce_sum.19
  86.2 0.2 broadcast_in_dim.16
  86.4 14.5 %all_to_all.22 = f32[64,1,1408]{2,1,0:T(1,128)S(1)} all-to-all(f32[64,1,1408]{2,1,0:T(1,128)S(1)} %broadcast_in_dim.16), channel_id=1, replica_groups=mesh['rows'=16,'z'=4,'core'=2] {'rows','z'}, dimensions={0} | all-to-all | bytes 720896 | tf_op jit(solution)/shard_map/all_to_all | solution.py:334
  100.9 3.1 %collective-permute-start.3 = (f32[704,128]{1,0:T(8,128)S(1)}, f32[704,128]{1,0:T(8,128)S(1)}, u32[]{:S(2)}, u32[]{:S(2)}) collective-permute-start(f32[704,128]{1,0:T(8,128)S(1)} %bitcast.29), channel_id=1, source_target_pairs={{0,1},{1,0},{2,3},{3,2},{4,5},{5,4},{6,7},{7,6},{8,9},{9,8},{10,11... | collective-permute-start | bytes 1081352 | tf_op jit(solution)/shard_map/ppermute | solution.py:338
  104.1 1.3 %collective-permute-done.3.other_ref = f32[704,128]{1,0:T(8,128)S(1)} collective-permute-done((f32[704,128]{1,0:T(8,128)S(1)}, f32[704,128]{1,0:T(8,128)S(1)}, u32[]{:S(2)}, u32[]{:S(2)}) %collective-permute-start.3) | collective-permute-done | bytes 360480 | tf_op jit(solution)/shard_map/ppermute | solution.py:338
  105.4 16.4 %factor_and_solve.1 = (f32[512,512]{1,0:T(8,128)}, f32[4,128]{1,0:T(4,128)}) custom-call(s32[1]{0:T(128)} %bitcast.core_ref, f32[704,128]{1,0:T(8,128)S(1)} %bitcast.30, f32[704,128]{1,0:T(8,128)S(1)} %collective-permute-done.3.other_ref), custom_call_target="tpu_custom_call" | custom-call | tf_op jit(solution)/shard_map/factor_and_solve/pallas_call | solution.py:164
  (3 shorter events, 0.1 us)
Async XLA Ops:
  1.9 3.0 %collective-permute-start = (bf16[256,1024]{1,0:T(8,128)(2,1)S(1)}, bf16[256,1024]{1,0:T(8,128)(2,1)S(1)}, u32[]{:S(2)}, u32[]{:S(2)}) collective-permute-start(bf16[256,1024]{1,0:T(8,128)(2,1)S(1)} %get-tuple-element.22), channel_id=1, source_target_pairs={{0,1},{1,0},{2,3},{3,2},{4,5},{5,4},{6,7},{7,6},{8,9},{9,8},{10,11... | collective-permute-start | bytes 1572872 | tf_op jit(solution)/shard_map/ppermute | solution.py:338
  5.8 23.5 %all-to-all-start = ((bf16[64,8,512]{2,1,0:T(8,128)(2,1)}), bf16[64,8,512]{2,1,0:T(8,128)(2,1)S(1)}, u32[]{:S(2)}, u32[]{:S(2)}) async-start(bf16[64,8,512]{2,1,0:T(8,128)(2,1)} %bitcast.6), calls=%async_computation | async-start | bytes 1048576 | tf_op jit(solution)/shard_map/all_to_all | solution.py:334
  44.8 4.7 %collective-permute-start.1 = (bf16[256,1024]{1,0:T(8,128)(2,1)S(1)}, bf16[256,1024]{1,0:T(8,128)(2,1)S(1)}, u32[]{:S(2)}, u32[]{:S(2)}) collective-permute-start(bf16[256,1024]{1,0:T(8,128)(2,1)S(1)} %bitcast.27), channel_id=1, source_target_pairs={{0,1},{1,0},{2,3},{3,2},{4,5},{5,4},{6,7},{7,6},{8,9},{9,8},{10,11... | collective-permute-start | bytes 1572872 | tf_op jit(solution)/shard_map/ppermute | solution.py:338
  58.3 5.9 %collective-permute-start.2 = (f32[704,128]{1,0:T(8,128)S(1)}, f32[704,128]{1,0:T(8,128)S(1)}, u32[]{:S(2)}, u32[]{:S(2)}) collective-permute-start(f32[704,128]{1,0:T(8,128)S(1)} %get-tuple-element.17), channel_id=1, source_target_pairs={{0,1},{1,0},{2,3},{3,2},{4,5},{5,4},{6,7},{7,6},{8,9},{9,8},{10,11... | collective-permute-start | bytes 1081352 | tf_op jit(solution)/shard_map/ppermute | solution.py:338
  100.9 4.5 %collective-permute-start.3 = (f32[704,128]{1,0:T(8,128)S(1)}, f32[704,128]{1,0:T(8,128)S(1)}, u32[]{:S(2)}, u32[]{:S(2)}) collective-permute-start(f32[704,128]{1,0:T(8,128)S(1)} %bitcast.29), channel_id=1, source_target_pairs={{0,1},{1,0},{2,3},{3,2},{4,5},{5,4},{6,7},{7,6},{8,9},{9,8},{10,11... | collective-permute-start | bytes 1081352 | tf_op jit(solution)/shard_map/ppermute | solution.py:338

commit v7 on v2

--- a/solution.py
+++ b/solution.py
@@ -10,6 +10,7 @@
 
 TILE = 128
 GROUP = 32
+PART = 8
 
 
 def spread_lane(value, lane):
@@ -37,12 +38,13 @@
 def factor_group(rows, first):
     groups = GROUP // 8
     sub = lax.broadcasted_iota(jnp.int32, (8, TILE), 0)
-    columns = [
-        [spread_lane(rows[s][0], first + j) if s >= j // 8 else None for s in range(groups)]
-        for j in range(GROUP)
-    ]
     pivots = [jnp.ones((8, TILE), jnp.float32) for _ in range(groups)]
     for k in range(0, GROUP, 2):
+        if k % PART == 0:
+            columns = {
+                j: [spread_lane(rows[s][0], first + j) if s >= j // 8 else None for s in range(groups)]
+                for j in range(k, k + PART)
+            }
         s0, r0, r1 = k // 8, k % 8, k % 8 + 1
         one, two = columns[k], columns[k + 1]
         a = spread_row(one[s0], r0)
@@ -57,7 +59,7 @@
         two_next = {s: two[s] - one[s] * ratio for s in live}
         m1 = {s: one[s] * inv_a for s in live}
         m2 = {s: two_next[s] * inv_s for s in live}
-        for j in range(k + 2, GROUP):
+        for j in range(k + 2, k - k % PART + PART):
             sj, rj = j // 8, j % 8
             u1 = spread_row(one[sj], rj)
             u2 = spread_row(two[sj], rj) - u1 * ratio
@@ -75,7 +77,9 @@
     return [[piece * scales[s] for piece in rows[s]] for s in range(groups)]
 
 
-def factor_kernel(core_ref, own_ref, other_ref, factor_ref, solved_ref, work, done, packed):
+def factor_kernel(
+    core_ref, own_ref, other_ref, factor_ref, solved_ref, work, done, packed
+):
     points = factor_ref.shape[0]
     tiles = points // TILE
     half = own_ref.shape[0]
@@ -246,14 +250,20 @@
         norms = jnp.sqrt(jnp.maximum(sizes_ref[...], 1).astype(jnp.float32))
         energy_ratio = energy_part[...] / norms
         energy_rows = energy_ratio * (weight * scale**4)
-        gram = square[...] + cross[...] + jnp.transpose(cross[...])
-        gram = gram + against(energy_rows, energy_rows, exact_mode)
         tiles = points // TILE
         blocks = packed_blocks(tiles)
+        own_energy = [
+            against(energy_rows[p * TILE : (p + 1) * TILE], energy_rows[p * TILE :], exact_mode)
+            for p in range(tiles)
+        ]
         for n, (p, t) in enumerate(blocks):
-            packed[n * TILE : (n + 1) * TILE, :] = gram[
-                p * TILE : (p + 1) * TILE, t * TILE : (t + 1) * TILE
-            ]
+            above = (slice(p * TILE, (p + 1) * TILE), slice(t * TILE, (t + 1) * TILE))
+            packed[n * TILE : (n + 1) * TILE, :] = (
+                square[above]
+                + cross[above]
+                + jnp.transpose(cross[above[1], above[0]])
+                + own_energy[p][:, (t - p) * TILE : (t - p + 1) * TILE]
+            )
         ones = jnp.ones((8, TILE), jnp.float32)
         rhs = against(ones, rhs_part[...], exact_mode)
         rhs = rhs + against(
@@ -306,7 +316,7 @@
                 pltpu.VMEM((rows, TILE), jnp.float32),
             ],
         ),
-        compiler_params=pltpu.CompilerParams(vmem_limit_bytes=58 * 1024 * 1024),
+        compiler_params=pltpu.CompilerParams(vmem_limit_bytes=50 * 1024 * 1024),
         name="gram_halves",
     )(info, sizes, energies, own, other, atoms, derivs, forces)
 CHIPS = ("rows", "z")

time: 126 us -> 123 us (0.976); the launches traced: 126 us -> 121 us
  starting transfers between devices: 23.5 us -> 19.1 us
  blocking collectives: 47.5 us -> 50.1 us
  other arithmetic: 7.25 us -> 4.67 us
  waiting for transfers between devices: 11 us -> 13.3 us
  local copies, waits for them, and re-layouts: 2.95 us -> 1.58 us
    ppermute x4, starting transfers between devices: 12.3 us -> 7.93 us  [swap(): return lax.ppermute(value, 'core', [(0, 1), (1, 0)])]
    all_to_all x3, blocking collectives: 47.5 us -> 50.1 us  [exchange(): return lax.all_to_all(pieces, axes, 0, 0, tiled=True)]
    all_to_all x1, waiting for transfers between devices: 5.77 us -> 7.94 us  [exchange(): return lax.all_to_all(pieces, axes, 0, 0, tiled=True)]
    pallas_call x1, Pallas kernels: 14.2 us -> 12.7 us  [gram_halves(): pl.pallas_call(functools.partial(gram_kernel, scale, weight), out_shape=(...]
  transfers between devices with their start and end apart: 5 -> 5, of which waited for: 5 -> 5; matrix products, arithmetic and copies ran while one was open for 5% -> 3% of each run, Pallas kernels for 0% -> 0%
where the time goes in v7:
time: 123 us; the launch traced here: 121 us
  blocking collectives  50.1 us (41%)
  Pallas kernels  30.4 us (25%)
  starting transfers between devices  19.1 us (16%)
  waiting for transfers between devices  13.3 us (11%)
  other arithmetic  4.67 us (4%)
  between operations  2.03 us (2%)
  local copies, waits for them, and re-layouts  1.58 us (1%)
    all_to_all x3, blocking collectives, exchange(): return lax.all_to_all(pieces, axes, 0, 0, tiled=True)  50.1 us
    pallas_call x1, Pallas kernels, factor_and_solve(): pl.pallas_call(factor_kernel, out_shape=(jax.ShapeDtypeStruct((points, po...  17.7 us
    pallas_call x1, Pallas kernels, gram_halves(): pl.pallas_call(functools.partial(gram_kernel, scale, weight), out_shape=(...  12.7 us
    all_to_all x1, starting transfers between devices, exchange(): return lax.all_to_all(pieces, axes, 0, 0, tiled=True)  11.2 us
    all_to_all x1, waiting for transfers between devices, exchange(): return lax.all_to_all(pieces, axes, 0, 0, tiled=True)  7.94 us
    ppermute x4, starting transfers between devices, swap(): return lax.ppermute(value, 'core', [(0, 1), (1, 0)])  7.93 us
    ppermute x4, waiting for transfers between devices, swap(): return lax.ppermute(value, 'core', [(0, 1), (1, 0)])  5.37 us
  transfers between devices with their start and end apart: 5, of which 5 were waited for; matrix products, arithmetic and copies ran while one was open for 3% of the time, Pallas kernels for 0%

profile of v7, /device:TPU:1, one launch (start us, length us, event | category | flops | bytes accessed | tf_op | source)
XLA Modules:
  0.0 121.2 jit_solution(15589378817273891388)
XLA Ops:
  0.6 1.3 %dynamic-slice_bitcast_fusion = (bf16[256,1024]{1,0:T(8,128)(2,1)S(1)}, bf16[256,1024]{1,0:T(8,128)(2,1)S(1)}) fusion(bf16[1,512,1024]{2,1,0:T(8,128)(2,1)} %param.12, s32[]{:T(128)S(6)} %select_n.23, s32[]{:T(128)S(6)} %select_n.22), kind=kLoop, calls=%fused_computation | loop fusion | bytes 2097160 | tf_op jit(solution)/shard_map/dynamic_slice | solution.py:340
  1.9 1.5 %collective-permute-start = (bf16[256,1024]{1,0:T(8,128)(2,1)S(1)}, bf16[256,1024]{1,0:T(8,128)(2,1)S(1)}, u32[]{:S(2)}, u32[]{:S(2)}) collective-permute-start(bf16[256,1024]{1,0:T(8,128)(2,1)S(1)} %get-tuple-element.22), channel_id=1, source_target_pairs={{0,1},{1,0},{2,3},{3,2},{4,5},{5,4},{6,7},{7,6},{8,9},{9,8},{10,11... | collective-permute-start | bytes 1572872 | tf_op jit(solution)/shard_map/ppermute | solution.py:332
  4.1 0.9 collective-permute-done
  5.0 0.8 broadcast_select_fusion
  5.8 11.2 %all-to-all-start = ((bf16[64,8,512]{2,1,0:T(8,128)(2,1)}), bf16[64,8,512]{2,1,0:T(8,128)(2,1)S(1)}, u32[]{:S(2)}, u32[]{:S(2)}) async-start(bf16[64,8,512]{2,1,0:T(8,128)(2,1)} %bitcast.6), calls=%async_computation | async-start | bytes 1048576 | tf_op jit(solution)/shard_map/all_to_all | solution.py:328
  17.0 1.4 %fusion = (s32[]{:T(128)}, s32[1,32]{0,1:T(8,128)S(1)}) fusion(s32[128,32]{0,1:T(8,128)} %param.11, s32[]{:T(128)S(6)} %select_n.26), kind=kLoop, calls=%fused_computation.7 | loop fusion | flops 31 | bytes 264 | tf_op jit(solution)/shard_map/reduce_sum | solution.py:371
  19.1 0.1 copy.12.sizes_ref
  19.2 0.7 convert_element_type.3.forces_ref
  19.9 0.7 pad_add_fusion.info_ref
  20.7 0.7 multiply_bitcast_fusion.energies_ref
  21.3 7.9 %all-to-all-done = bf16[64,8,512]{2,1,0:T(8,128)(2,1)S(1)} async-done(((bf16[64,8,512]{2,1,0:T(8,128)(2,1)}), bf16[64,8,512]{2,1,0:T(8,128)(2,1)S(1)}, u32[]{:S(2)}, u32[]{:S(2)}) %all-to-all-start) | async-done | bytes 524320 | tf_op jit(solution)/shard_map/all_to_all | solution.py:328
  29.3 15.5 %all_to_all.20 = bf16[64,8,512]{2,1,0:T(8,128)(2,1)S(1)} all-to-all(bf16[64,8,512]{2,1,0:T(8,128)(2,1)S(1)} %broadcast_in_dim.7), channel_id=1, replica_groups=mesh['rows'=16,'z'=4,'core'=2] {'rows','z'}, dimensions={0} | all-to-all | bytes 1048576 | tf_op jit(solution)/shard_map/all_to_all | solution.py:328
  44.8 3.2 %collective-permute-start.1 = (bf16[256,1024]{1,0:T(8,128)(2,1)S(1)}, bf16[256,1024]{1,0:T(8,128)(2,1)S(1)}, u32[]{:S(2)}, u32[]{:S(2)}) collective-permute-start(bf16[256,1024]{1,0:T(8,128)(2,1)S(1)} %bitcast.27), channel_id=1, source_target_pairs={{0,1},{1,0},{2,3},{3,2},{4,5},{5,4},{6,7},{7,6},{8,9},{9,8},{10,11... | collective-permute-start | bytes 1572872 | tf_op jit(solution)/shard_map/ppermute | solution.py:332
  48.0 1.5 %collective-permute-done.1.other_ref = bf16[256,1024]{1,0:T(8,128)(2,1)S(1)} collective-permute-done((bf16[256,1024]{1,0:T(8,128)(2,1)S(1)}, bf16[256,1024]{1,0:T(8,128)(2,1)S(1)}, u32[]{:S(2)}, u32[]{:S(2)}) %collective-permute-start.1) | collective-permute-done | bytes 524320 | tf_op jit(solution)/shard_map/ppermute | solution.py:332
  49.6 12.7 %gram_halves.1 = (f32[704,128]{1,0:T(8,128)S(1)}, f32[704,128]{1,0:T(8,128)S(1)}) custom-call(s32[3]{0:T(128)S(1)} %pad_add_fusion.info_ref, s32[1,32]{1,0:T(1,128)S(1)} %copy.12.sizes_ref, f32[1,32]{1,0:T(1,128)S(1)} %multiply_bitcast_fusion.energies_ref, bf16[256,1024]{1,0:T(8,128)(2,1)S(1)} %bitcast.28, ...), custom_call_target="tpu_custom_call" | custom-call | tf_op jit(solution)/shard_map/gram_halves/pallas_call | solution.py:294
  62.3 0.1 collective-permute-start.2
  62.4 1.7 %collective-permute-done.2 = f32[704,128]{1,0:T(8,128)S(1)} collective-permute-done((f32[704,128]{1,0:T(8,128)S(1)}, f32[704,128]{1,0:T(8,128)S(1)}, u32[]{:S(2)}, u32[]{:S(2)}) %collective-permute-start.2) | collective-permute-done | bytes 360480 | tf_op jit(solution)/shard_map/ppermute | solution.py:332
  64.1 20.0 %all_to_all.21 = f32[64,1,1408]{2,1,0:T(1,128)S(1)} all-to-all(f32[64,1,1408]{2,1,0:T(1,128)S(1)} %bitcast.31), channel_id=1, replica_groups=mesh['rows'=16,'z'=4,'core'=2] {'rows','z'}, dimensions={0} | all-to-all | bytes 720896 | tf_op jit(solution)/shard_map/all_to_all | solution.py:328
  84.1 0.2 reduce_sum.19
  84.3 0.2 broadcast_in_dim.16
  84.5 14.5 %all_to_all.22 = f32[64,1,1408]{2,1,0:T(1,128)S(1)} all-to-all(f32[64,1,1408]{2,1,0:T(1,128)S(1)} %broadcast_in_dim.16), channel_id=1, replica_groups=mesh['rows'=16,'z'=4,'core'=2] {'rows','z'}, dimensions={0} | all-to-all | bytes 720896 | tf_op jit(solution)/shard_map/all_to_all | solution.py:328
  99.1 3.1 %collective-permute-start.3 = (f32[704,128]{1,0:T(8,128)S(1)}, f32[704,128]{1,0:T(8,128)S(1)}, u32[]{:S(2)}, u32[]{:S(2)}) collective-permute-start(f32[704,128]{1,0:T(8,128)S(1)} %bitcast.29), channel_id=1, source_target_pairs={{0,1},{1,0},{2,3},{3,2},{4,5},{5,4},{6,7},{7,6},{8,9},{9,8},{10,11... | collective-permute-start | bytes 1081352 | tf_op jit(solution)/shard_map/ppermute | solution.py:332
  102.2 1.3 %collective-permute-done.3.other_ref = f32[704,128]{1,0:T(8,128)S(1)} collective-permute-done((f32[704,128]{1,0:T(8,128)S(1)}, f32[704,128]{1,0:T(8,128)S(1)}, u32[]{:S(2)}, u32[]{:S(2)}) %collective-permute-start.3) | collective-permute-done | bytes 360480 | tf_op jit(solution)/shard_map/ppermute | solution.py:332
  103.5 17.7 %factor_and_solve.1 = (f32[512,512]{1,0:T(8,128)}, f32[4,128]{1,0:T(4,128)}) custom-call(s32[1]{0:T(128)} %bitcast.core_ref, f32[704,128]{1,0:T(8,128)S(1)} %bitcast.30, f32[704,128]{1,0:T(8,128)S(1)} %collective-permute-done.3.other_ref), custom_call_target="tpu_custom_call" | custom-call | tf_op jit(solution)/shard_map/factor_and_solve/pallas_call | solution.py:152
  (3 shorter events, 0.1 us)
Async XLA Ops:
  1.9 3.0 %collective-permute-start = (bf16[256,1024]{1,0:T(8,128)(2,1)S(1)}, bf16[256,1024]{1,0:T(8,128)(2,1)S(1)}, u32[]{:S(2)}, u32[]{:S(2)}) collective-permute-start(bf16[256,1024]{1,0:T(8,128)(2,1)S(1)} %get-tuple-element.22), channel_id=1, source_target_pairs={{0,1},{1,0},{2,3},{3,2},{4,5},{5,4},{6,7},{7,6},{8,9},{9,8},{10,11... | collective-permute-start | bytes 1572872 | tf_op jit(solution)/shard_map/ppermute | solution.py:332
  5.8 23.5 %all-to-all-start = ((bf16[64,8,512]{2,1,0:T(8,128)(2,1)}), bf16[64,8,512]{2,1,0:T(8,128)(2,1)S(1)}, u32[]{:S(2)}, u32[]{:S(2)}) async-start(bf16[64,8,512]{2,1,0:T(8,128)(2,1)} %bitcast.6), calls=%async_computation | async-start | bytes 1048576 | tf_op jit(solution)/shard_map/all_to_all | solution.py:328
  44.8 4.7 %collective-permute-start.1 = (bf16[256,1024]{1,0:T(8,128)(2,1)S(1)}, bf16[256,1024]{1,0:T(8,128)(2,1)S(1)}, u32[]{:S(2)}, u32[]{:S(2)}) collective-permute-start(bf16[256,1024]{1,0:T(8,128)(2,1)S(1)} %bitcast.27), channel_id=1, source_target_pairs={{0,1},{1,0},{2,3},{3,2},{4,5},{5,4},{6,7},{7,6},{8,9},{9,8},{10,11... | collective-permute-start | bytes 1572872 | tf_op jit(solution)/shard_map/ppermute | solution.py:332
  62.3 1.8 %collective-permute-start.2 = (f32[704,128]{1,0:T(8,128)S(1)}, f32[704,128]{1,0:T(8,128)S(1)}, u32[]{:S(2)}, u32[]{:S(2)}) collective-permute-start(f32[704,128]{1,0:T(8,128)S(1)} %get-tuple-element.17), channel_id=1, source_target_pairs={{0,1},{1,0},{2,3},{3,2},{4,5},{5,4},{6,7},{7,6},{8,9},{9,8},{10,11... | collective-permute-start | bytes 1081352 | tf_op jit(solution)/shard_map/ppermute | solution.py:332
  99.1 4.5 %collective-permute-start.3 = (f32[704,128]{1,0:T(8,128)S(1)}, f32[704,128]{1,0:T(8,128)S(1)}, u32[]{:S(2)}, u32[]{:S(2)}) collective-permute-start(f32[704,128]{1,0:T(8,128)S(1)} %bitcast.29), channel_id=1, source_target_pairs={{0,1},{1,0},{2,3},{3,2},{4,5},{5,4},{6,7},{7,6},{8,9},{9,8},{10,11... | collective-permute-start | bytes 1081352 | tf_op jit(solution)/shard_map/ppermute | solution.py:332

commit v8 on v7

--- a/solution.py
+++ b/solution.py
@@ -10,7 +10,8 @@
 
 TILE = 128
 GROUP = 32
-PART = 8
+PART = 16
+TERMS = 6
 
 
 def spread_lane(value, lane):
@@ -78,7 +79,7 @@
 
 
 def factor_kernel(
-    core_ref, own_ref, other_ref, factor_ref, solved_ref, work, done, packed
+    core_ref, own_ref, other_ref, factor_ref, solved_ref, work, left, right, answers, packed
 ):
     points = factor_ref.shape[0]
     tiles = points // TILE
@@ -99,24 +100,25 @@
     lane = lax.broadcasted_iota(jnp.int32, (8, TILE), 1)
     sub = lax.broadcasted_iota(jnp.int32, (8, TILE), 0)
 
-    def take_off(at, count, first, last):
-        if last > first:
-            left = at - at % TILE
-            work[at : at + count, left:] -= lax.dot_general(
-                done[first:last, at : at + count],
-                done[first:last, left:],
+    def take_off(at, count, first, last, lanes):
+        if last > first and lanes.start < lanes.stop:
+            stacked = slice(TERMS * first, TERMS * last)
+            work[at : at + count, lanes] -= lax.dot_general(
+                left[stacked, at : at + count],
+                right[stacked, lanes],
                 (((0,), (0,)), ((), ())),
-                precision=lax.Precision.HIGHEST,
                 preferred_element_type=jnp.float32,
             )
 
     for start in range(0, points, GROUP):
         top = start - start % TILE
         follow = start + GROUP
+        edge = follow - follow % TILE
+        ahead, beside = slice(edge, edge + TILE), slice(edge + TILE, points + TILE)
         if follow % TILE:
-            take_off(follow, GROUP, top, start)
+            take_off(follow, GROUP, top, start, slice(edge, points + TILE))
         elif follow < points:
-            take_off(follow, TILE, 0, start)
+            take_off(follow, TILE, 0, start, slice(edge, points + TILE))
         count = tiles - top // TILE + 1
         rows = []
         for s in range(GROUP // 8):
@@ -130,20 +132,33 @@
         for s in range(GROUP // 8):
             at = start + s * 8
             rows[s][0] = jnp.where(lane >= sub + (at - top), rows[s][0], 0.0)
-            for t in range(count):
-                done[at : at + 8, top + t * TILE : top + (t + 1) * TILE] = rows[s][t]
             for t in range(tiles):
                 own = t - top // TILE
                 factor_ref[at : at + 8, t * TILE : (t + 1) * TILE] = (
                     rows[s][own] if own >= 0 else jnp.zeros((8, TILE), jnp.float32)
                 )
-        if follow % TILE:
-            take_off(follow, GROUP, start, follow)
-        elif follow < points:
-            take_off(follow, GROUP, start, follow)
-            take_off(follow + GROUP, TILE - GROUP, start, follow)
+            answers[at : at + 8, :] = rows[s][count - 1]
+        for s in range(0, GROUP // 8, 2):
+            for t in range(count):
+                value = jnp.concatenate([rows[s][t], rows[s + 1][t]], axis=0)
+                high = value.astype(jnp.bfloat16)
+                value = value - high.astype(jnp.float32)
+                mid = value.astype(jnp.bfloat16)
+                low = (value - mid.astype(jnp.float32)).astype(jnp.bfloat16)
+                lanes = slice(top + t * TILE, top + (t + 1) * TILE)
+                terms = [(high, high), (mid, high), (high, mid), (low, high), (mid, mid), (high, low)]
+                for n, (one, two) in enumerate(terms):
+                    at = TERMS * start + n * GROUP + s * 8
+                    left[at : at + 16, lanes] = one
+                    right[at : at + 16, lanes] = two
+        if follow < points:
+            take_off(follow, GROUP, start, follow, ahead)
+            take_off(follow, GROUP, start, follow, beside)
+            if follow % TILE == 0:
+                rest = slice(edge, points + TILE)
+                take_off(follow + GROUP, TILE - GROUP, start, follow, rest)
     for t in range(tiles):
-        flipped = jnp.transpose(done[t * TILE : (t + 1) * TILE, points:])
+        flipped = jnp.transpose(answers[t * TILE : (t + 1) * TILE, :])
         solved_ref[t : t + 1, :] = flipped[0:1, :]
 
 
@@ -163,7 +178,9 @@
         out_specs=(pl.BlockSpec(memory_space=pltpu.VMEM),) * 2,
         scratch_shapes=[
             pltpu.VMEM((points, points + TILE), jnp.float32),
-            pltpu.VMEM((points, points + TILE), jnp.float32),
+            pltpu.VMEM((TERMS * points, points + TILE), jnp.bfloat16),
+            pltpu.VMEM((TERMS * points, points + TILE), jnp.bfloat16),
+            pltpu.VMEM((points, TILE), jnp.float32),
             pltpu.VMEM((2 * own.shape[0], TILE), jnp.float32),
         ],
         compiler_params=pltpu.CompilerParams(vmem_limit_bytes=32 * 1024 * 1024),

time: 123 us -> 120 us (0.976)
  blocking collectives: 50.1 us -> 47.4 us
    pallas_call x1, Pallas kernels: 12.7 us -> 16.8 us  [gram_halves(): pl.pallas_call(functools.partial(gram_kernel, scale, weight), out_shape=(...]
    pallas_call x1, Pallas kernels: 17.7 us -> 14.3 us  [factor_and_solve(): pl.pallas_call(factor_kernel, out_shape=(jax.ShapeDtypeStruct((points, po...]
    all_to_all x3, blocking collectives: 50.1 us -> 47.4 us  [exchange(): return lax.all_to_all(pieces, axes, 0, 0, tiled=True)]
where the time goes in v8:
time: 120 us; the launch traced here: 119 us
  blocking collectives  47.4 us (40%)
  Pallas kernels  31.1 us (26%)
  starting transfers between devices  19.1 us (16%)
  waiting for transfers between devices  13.3 us (11%)
  other arithmetic  4.67 us (4%)
  between operations  2.03 us (2%)
  local copies, waits for them, and re-layouts  1.58 us (1%)
    all_to_all x3, blocking collectives, exchange(): return lax.all_to_all(pieces, axes, 0, 0, tiled=True)  47.4 us
    pallas_call x1, Pallas kernels, gram_halves(): pl.pallas_call(functools.partial(gram_kernel, scale, weight), out_shape=(...  16.8 us
    pallas_call x1, Pallas kernels, factor_and_solve(): pl.pallas_call(factor_kernel, out_shape=(jax.ShapeDtypeStruct((points, po...  14.3 us
    all_to_all x1, starting transfers between devices, exchange(): return lax.all_to_all(pieces, axes, 0, 0, tiled=True)  11.2 us
    all_to_all x1, waiting for transfers between devices, exchange(): return lax.all_to_all(pieces, axes, 0, 0, tiled=True)  7.94 us
    ppermute x4, starting transfers between devices, swap(): return lax.ppermute(value, 'core', [(0, 1), (1, 0)])  7.93 us
    ppermute x4, waiting for transfers between devices, swap(): return lax.ppermute(value, 'core', [(0, 1), (1, 0)])  5.37 us
  transfers between devices with their start and end apart: 5, of which 5 were waited for; matrix products, arithmetic and copies ran while one was open for 3% of the time, Pallas kernels for 0%

profile of v8, /device:TPU:1, one launch (start us, length us, event | category | flops | bytes accessed | tf_op | source)
XLA Modules:
  0.0 119.3 jit_solution(8213354848004776749)
XLA Ops:
  0.6 1.3 %dynamic-slice_bitcast_fusion = (bf16[256,1024]{1,0:T(8,128)(2,1)S(1)}, bf16[256,1024]{1,0:T(8,128)(2,1)S(1)}) fusion(bf16[1,512,1024]{2,1,0:T(8,128)(2,1)} %param.12, s32[]{:T(128)S(6)} %select_n.23, s32[]{:T(128)S(6)} %select_n.22), kind=kLoop, calls=%fused_computation | loop fusion | bytes 2097160 | tf_op jit(solution)/shard_map/dynamic_slice | solution.py:357
  1.9 1.5 %collective-permute-start = (bf16[256,1024]{1,0:T(8,128)(2,1)S(1)}, bf16[256,1024]{1,0:T(8,128)(2,1)S(1)}, u32[]{:S(2)}, u32[]{:S(2)}) collective-permute-start(bf16[256,1024]{1,0:T(8,128)(2,1)S(1)} %get-tuple-element.22), channel_id=1, source_target_pairs={{0,1},{1,0},{2,3},{3,2},{4,5},{5,4},{6,7},{7,6},{8,9},{9,8},{10,11... | collective-permute-start | bytes 1572872 | tf_op jit(solution)/shard_map/ppermute | solution.py:349
  4.1 0.9 collective-permute-done
  5.0 0.8 broadcast_select_fusion
  5.8 11.2 %all-to-all-start = ((bf16[64,8,512]{2,1,0:T(8,128)(2,1)}), bf16[64,8,512]{2,1,0:T(8,128)(2,1)S(1)}, u32[]{:S(2)}, u32[]{:S(2)}) async-start(bf16[64,8,512]{2,1,0:T(8,128)(2,1)} %bitcast.6), calls=%async_computation | async-start | bytes 1048576 | tf_op jit(solution)/shard_map/all_to_all | solution.py:345
  17.0 1.4 %fusion = (s32[]{:T(128)}, s32[1,32]{0,1:T(8,128)S(1)}) fusion(s32[128,32]{0,1:T(8,128)} %param.11, s32[]{:T(128)S(6)} %select_n.26), kind=kLoop, calls=%fused_computation.7 | loop fusion | flops 31 | bytes 264 | tf_op jit(solution)/shard_map/reduce_sum | solution.py:388
  19.1 0.1 copy.12.sizes_ref
  19.2 0.7 convert_element_type.3.forces_ref
  19.9 0.7 pad_add_fusion.info_ref
  20.7 0.7 multiply_bitcast_fusion.energies_ref
  21.3 7.9 %all-to-all-done = bf16[64,8,512]{2,1,0:T(8,128)(2,1)S(1)} async-done(((bf16[64,8,512]{2,1,0:T(8,128)(2,1)}), bf16[64,8,512]{2,1,0:T(8,128)(2,1)S(1)}, u32[]{:S(2)}, u32[]{:S(2)}) %all-to-all-start) | async-done | bytes 524320 | tf_op jit(solution)/shard_map/all_to_all | solution.py:345
  29.3 15.5 %all_to_all.20 = bf16[64,8,512]{2,1,0:T(8,128)(2,1)S(1)} all-to-all(bf16[64,8,512]{2,1,0:T(8,128)(2,1)S(1)} %broadcast_in_dim.7), channel_id=1, replica_groups=mesh['rows'=16,'z'=4,'core'=2] {'rows','z'}, dimensions={0} | all-to-all | bytes 1048576 | tf_op jit(solution)/shard_map/all_to_all | solution.py:345
  44.8 3.2 %collective-permute-start.1 = (bf16[256,1024]{1,0:T(8,128)(2,1)S(1)}, bf16[256,1024]{1,0:T(8,128)(2,1)S(1)}, u32[]{:S(2)}, u32[]{:S(2)}) collective-permute-start(bf16[256,1024]{1,0:T(8,128)(2,1)S(1)} %bitcast.27), channel_id=1, source_target_pairs={{0,1},{1,0},{2,3},{3,2},{4,5},{5,4},{6,7},{7,6},{8,9},{9,8},{10,11... | collective-permute-start | bytes 1572872 | tf_op jit(solution)/shard_map/ppermute | solution.py:349
  48.0 1.5 %collective-permute-done.1.other_ref = bf16[256,1024]{1,0:T(8,128)(2,1)S(1)} collective-permute-done((bf16[256,1024]{1,0:T(8,128)(2,1)S(1)}, bf16[256,1024]{1,0:T(8,128)(2,1)S(1)}, u32[]{:S(2)}, u32[]{:S(2)}) %collective-permute-start.1) | collective-permute-done | bytes 524320 | tf_op jit(solution)/shard_map/ppermute | solution.py:349
  49.6 16.8 %gram_halves.1 = (f32[704,128]{1,0:T(8,128)S(1)}, f32[704,128]{1,0:T(8,128)S(1)}) custom-call(s32[3]{0:T(128)S(1)} %pad_add_fusion.info_ref, s32[1,32]{1,0:T(1,128)S(1)} %copy.12.sizes_ref, f32[1,32]{1,0:T(1,128)S(1)} %multiply_bitcast_fusion.energies_ref, bf16[256,1024]{1,0:T(8,128)(2,1)S(1)} %bitcast.28, ...), custom_call_target="tpu_custom_call" | custom-call | tf_op jit(solution)/shard_map/gram_halves/pallas_call | solution.py:311
  66.4 0.1 collective-permute-start.2
  66.5 1.7 %collective-permute-done.2 = f32[704,128]{1,0:T(8,128)S(1)} collective-permute-done((f32[704,128]{1,0:T(8,128)S(1)}, f32[704,128]{1,0:T(8,128)S(1)}, u32[]{:S(2)}, u32[]{:S(2)}) %collective-permute-start.2) | collective-permute-done | bytes 360480 | tf_op jit(solution)/shard_map/ppermute | solution.py:349
  68.2 17.4 %all_to_all.21 = f32[64,1,1408]{2,1,0:T(1,128)S(1)} all-to-all(f32[64,1,1408]{2,1,0:T(1,128)S(1)} %bitcast.31), channel_id=1, replica_groups=mesh['rows'=16,'z'=4,'core'=2] {'rows','z'}, dimensions={0} | all-to-all | bytes 720896 | tf_op jit(solution)/shard_map/all_to_all | solution.py:345
  85.6 0.2 reduce_sum.19
  85.8 0.2 broadcast_in_dim.16
  86.0 14.5 %all_to_all.22 = f32[64,1,1408]{2,1,0:T(1,128)S(1)} all-to-all(f32[64,1,1408]{2,1,0:T(1,128)S(1)} %broadcast_in_dim.16), channel_id=1, replica_groups=mesh['rows'=16,'z'=4,'core'=2] {'rows','z'}, dimensions={0} | all-to-all | bytes 720896 | tf_op jit(solution)/shard_map/all_to_all | solution.py:345
  100.5 3.1 %collective-permute-start.3 = (f32[704,128]{1,0:T(8,128)S(1)}, f32[704,128]{1,0:T(8,128)S(1)}, u32[]{:S(2)}, u32[]{:S(2)}) collective-permute-start(f32[704,128]{1,0:T(8,128)S(1)} %bitcast.29), channel_id=1, source_target_pairs={{0,1},{1,0},{2,3},{3,2},{4,5},{5,4},{6,7},{7,6},{8,9},{9,8},{10,11... | collective-permute-start | bytes 1081352 | tf_op jit(solution)/shard_map/ppermute | solution.py:349
  103.7 1.3 %collective-permute-done.3.other_ref = f32[704,128]{1,0:T(8,128)S(1)} collective-permute-done((f32[704,128]{1,0:T(8,128)S(1)}, f32[704,128]{1,0:T(8,128)S(1)}, u32[]{:S(2)}, u32[]{:S(2)}) %collective-permute-start.3) | collective-permute-done | bytes 360480 | tf_op jit(solution)/shard_map/ppermute | solution.py:349
  105.0 14.3 %factor_and_solve.1 = (f32[512,512]{1,0:T(8,128)}, f32[4,128]{1,0:T(4,128)}) custom-call(s32[1]{0:T(128)} %bitcast.core_ref, f32[704,128]{1,0:T(8,128)S(1)} %bitcast.30, f32[704,128]{1,0:T(8,128)S(1)} %collective-permute-done.3.other_ref), custom_call_target="tpu_custom_call" | custom-call | tf_op jit(solution)/shard_map/factor_and_solve/pallas_call | solution.py:167
  (3 shorter events, 0.1 us)
Async XLA Ops:
  1.9 3.0 %collective-permute-start = (bf16[256,1024]{1,0:T(8,128)(2,1)S(1)}, bf16[256,1024]{1,0:T(8,128)(2,1)S(1)}, u32[]{:S(2)}, u32[]{:S(2)}) collective-permute-start(bf16[256,1024]{1,0:T(8,128)(2,1)S(1)} %get-tuple-element.22), channel_id=1, source_target_pairs={{0,1},{1,0},{2,3},{3,2},{4,5},{5,4},{6,7},{7,6},{8,9},{9,8},{10,11... | collective-permute-start | bytes 1572872 | tf_op jit(solution)/shard_map/ppermute | solution.py:349
  5.8 23.5 %all-to-all-start = ((bf16[64,8,512]{2,1,0:T(8,128)(2,1)}), bf16[64,8,512]{2,1,0:T(8,128)(2,1)S(1)}, u32[]{:S(2)}, u32[]{:S(2)}) async-start(bf16[64,8,512]{2,1,0:T(8,128)(2,1)} %bitcast.6), calls=%async_computation | async-start | bytes 1048576 | tf_op jit(solution)/shard_map/all_to_all | solution.py:345
  44.8 4.7 %collective-permute-start.1 = (bf16[256,1024]{1,0:T(8,128)(2,1)S(1)}, bf16[256,1024]{1,0:T(8,128)(2,1)S(1)}, u32[]{:S(2)}, u32[]{:S(2)}) collective-permute-start(bf16[256,1024]{1,0:T(8,128)(2,1)S(1)} %bitcast.27), channel_id=1, source_target_pairs={{0,1},{1,0},{2,3},{3,2},{4,5},{5,4},{6,7},{7,6},{8,9},{9,8},{10,11... | collective-permute-start | bytes 1572872 | tf_op jit(solution)/shard_map/ppermute | solution.py:349
  66.4 1.8 %collective-permute-start.2 = (f32[704,128]{1,0:T(8,128)S(1)}, f32[704,128]{1,0:T(8,128)S(1)}, u32[]{:S(2)}, u32[]{:S(2)}) collective-permute-start(f32[704,128]{1,0:T(8,128)S(1)} %get-tuple-element.17), channel_id=1, source_target_pairs={{0,1},{1,0},{2,3},{3,2},{4,5},{5,4},{6,7},{7,6},{8,9},{9,8},{10,11... | collective-permute-start | bytes 1081352 | tf_op jit(solution)/shard_map/ppermute | solution.py:349
  100.5 4.5 %collective-permute-start.3 = (f32[704,128]{1,0:T(8,128)S(1)}, f32[704,128]{1,0:T(8,128)S(1)}, u32[]{:S(2)}, u32[]{:S(2)}) collective-permute-start(f32[704,128]{1,0:T(8,128)S(1)} %bitcast.29), channel_id=1, source_target_pairs={{0,1},{1,0},{2,3},{3,2},{4,5},{5,4},{6,7},{7,6},{8,9},{9,8},{10,11... | collective-permute-start | bytes 1081352 | tf_op jit(solution)/shard_map/ppermute | solution.py:349

commit v9 on v8

--- a/solution.py
+++ b/solution.py
@@ -249,7 +249,7 @@
             if c < 2:
                 slopes = against(panel, derivs_ref[c + 1])
             else:
-                energy_part[...] += against(kernel_high, member) + against(kernel_low, member)
+                energy_part[...] += against(member, kernel_high) + against(member, kernel_low)
             high, low = split(design)
             term = design * forces_ref[c : c + 1, :]
             for t in range(block_rows // TILE):
@@ -264,13 +264,22 @@
 
     @pl.when(step == pl.num_programs(0) - 1)
     def _():
-        norms = jnp.sqrt(jnp.maximum(sizes_ref[...], 1).astype(jnp.float32))
-        energy_ratio = energy_part[...] / norms
+        row = lax.broadcasted_iota(jnp.int32, (slots, slots), 0)
+        lane = lax.broadcasted_iota(jnp.int32, (slots, slots), 1)
+        wide = jnp.broadcast_to(sizes_ref[...], (slots, slots))
+        tall = jnp.sum(jnp.where(row == lane, wide, 0), axis=1, keepdims=True)
+        energy_ratio = energy_part[...] / jnp.sqrt(jnp.maximum(tall, 1).astype(jnp.float32))
         energy_rows = energy_ratio * (weight * scale**4)
         tiles = points // TILE
         blocks = packed_blocks(tiles)
         own_energy = [
-            against(energy_rows[p * TILE : (p + 1) * TILE], energy_rows[p * TILE :], exact_mode)
+            lax.dot_general(
+                energy_rows[:, p * TILE : (p + 1) * TILE],
+                energy_rows[:, p * TILE :],
+                (((0,), (0,)), ((), ())),
+                precision=exact_mode,
+                preferred_element_type=jnp.float32,
+            )
             for p in range(tiles)
         ]
         for n, (p, t) in enumerate(blocks):
@@ -283,8 +292,11 @@
             )
         ones = jnp.ones((8, TILE), jnp.float32)
         rhs = against(ones, rhs_part[...], exact_mode)
-        rhs = rhs + against(
-            jnp.broadcast_to(energies_ref[...], (8, slots)), energy_ratio, exact_mode
+        rhs = rhs + jnp.dot(
+            jnp.broadcast_to(energies_ref[...], (8, slots)),
+            energy_ratio,
+            precision=exact_mode,
+            preferred_element_type=jnp.float32,
         )
         for t in range(tiles):
             at = len(blocks) * TILE + t
@@ -329,7 +341,7 @@
                 pltpu.VMEM((points, points), jnp.float32),
                 pltpu.VMEM((points, points), jnp.float32),
                 pltpu.VMEM((points, TILE), jnp.float32),
-                pltpu.VMEM((points, slots), jnp.float32),
+                pltpu.VMEM((slots, points), jnp.float32),
                 pltpu.VMEM((rows, TILE), jnp.float32),
             ],
         ),
@@ -356,13 +368,15 @@
     half = points // 2
     far = swap(lax.dynamic_slice_in_dim(panels, (1 - core) * half, half, 0))
     near = lax.optimization_barrier(lax.dynamic_slice_in_dim(panels, core * half, half, 0))
+    chip = lax.div(owner, 2).astype(jnp.uint32)
     held = jnp.where(lax.rem(owner, 2) == core, near, far)
+    held, chip, others = lax.optimization_barrier((held, chip, others))
     tall = half // 8
     wide = chips // tall
     cut = held.reshape(tall, 8, wide, width // wide).transpose(0, 2, 1, 3)
     pieces = exchange(cut.reshape(chips, 8, width // wide), CHIPS)
-    piece = lax.dynamic_index_in_dim(pieces, lax.div(owner, 2), 0, keepdims=True)
-    piece, others = lax.optimization_barrier((piece, others))
+    zero = jnp.uint32(0)
+    piece = lax.dynamic_slice(pieces, (chip, zero, zero), (1,) + pieces.shape[1:])
     own = exchange(jnp.broadcast_to(piece, pieces.shape), CHIPS)
     own = own.reshape(tall, wide, 8, width // wide).transpose(0, 2, 1, 3).reshape(half, width)
     return own, swap(own), others

time: 120 us -> 123 us (1.025)
  blocking collectives: 47.4 us -> 73.1 us
  waiting for transfers between devices: 13.3 us -> 4.14 us
  starting transfers between devices: 19.1 us -> 11.7 us
  Pallas kernels: 31.1 us -> 26.8 us
    all_to_all x3 -> x4, blocking collectives: 47.4 us -> 73.1 us  [exchange(): return lax.all_to_all(pieces, axes, 0, 0, tiled=True)]
    all_to_all x1 -> x0, starting transfers between devices: 11.2 us -> none  [exchange(): return lax.all_to_all(pieces, axes, 0, 0, tiled=True)]
    all_to_all x1 -> x0, waiting for transfers between devices: 7.94 us -> none  [exchange(): return lax.all_to_all(pieces, axes, 0, 0, tiled=True)]
    pallas_call x1, Pallas kernels: 16.8 us -> 12.5 us  [gram_halves(): pl.pallas_call(functools.partial(gram_kernel, scale, weight), out_shape=(...]
    ppermute x4, starting transfers between devices: 7.93 us -> 11.7 us  [swap(): return lax.ppermute(value, 'core', [(0, 1), (1, 0)])]
  transfers between devices with their start and end apart: 5 -> 4, of which waited for: 5 -> 3; matrix products, arithmetic and copies ran while one was open for 3% -> 3% of each run, Pallas kernels for 0% -> 0%
where the time goes in v9:
time: 123 us
  blocking collectives  73.1 us (59%)
  Pallas kernels  26.8 us (22%)
  starting transfers between devices  11.7 us (10%)
  waiting for transfers between devices  4.14 us (3%)
  other arithmetic  3.88 us (3%)
  between operations  2.01 us (2%)
  local copies, waits for them, and re-layouts  1.58 us (1%)
    all_to_all x4, blocking collectives, exchange(): return lax.all_to_all(pieces, axes, 0, 0, tiled=True)  73.1 us
    pallas_call x1, Pallas kernels, factor_and_solve(): pl.pallas_call(factor_kernel, out_shape=(jax.ShapeDtypeStruct((points, po...  14.3 us
    pallas_call x1, Pallas kernels, gram_halves(): pl.pallas_call(functools.partial(gram_kernel, scale, weight), out_shape=(...  12.5 us
    ppermute x4, starting transfers between devices, swap(): return lax.ppermute(value, 'core', [(0, 1), (1, 0)])  11.7 us
    ppermute x4, waiting for transfers between devices, swap(): return lax.ppermute(value, 'core', [(0, 1), (1, 0)])  4.14 us
  transfers between devices with their start and end apart: 4, of which 3 were waited for; matrix products, arithmetic and copies ran while one was open for 3% of the time, Pallas kernels for 0%

profile of v9, /device:TPU:1, one launch (start us, length us, event | category | flops | bytes accessed | tf_op | source)
XLA Modules:
  0.0 123.3 jit_solution(1384505121970409387)
XLA Ops:
  0.6 1.3 %dynamic-slice_bitcast_fusion = (bf16[256,1024]{1,0:T(8,128)(2,1)S(1)}, bf16[256,1024]{1,0:T(8,128)(2,1)S(1)}) fusion(bf16[1,512,1024]{2,1,0:T(8,128)(2,1)} %param.12, s32[]{:T(128)S(6)} %select_n.19, s32[]{:T(128)S(6)} %select_n.18), kind=kLoop, calls=%fused_computation | loop fusion | bytes 2097160 | tf_op jit(solution)/shard_map/dynamic_slice | solution.py:369
  1.9 1.5 %collective-permute-start = (bf16[256,1024]{1,0:T(8,128)(2,1)S(1)}, bf16[256,1024]{1,0:T(8,128)(2,1)S(1)}, u32[]{:S(2)}, u32[]{:S(2)}) collective-permute-start(bf16[256,1024]{1,0:T(8,128)(2,1)S(1)} %get-tuple-element.24), channel_id=1, source_target_pairs={{0,1},{1,0},{2,3},{3,2},{4,5},{5,4},{6,7},{7,6},{8,9},{9,8},{10,11... | collective-permute-start | bytes 1572872 | tf_op jit(solution)/shard_map/ppermute | solution.py:361
  4.1 1.4 %fusion = (s32[]{:T(128)}, s32[1,32]{0,1:T(8,128)S(1)}) fusion(s32[128,32]{0,1:T(8,128)} %param.11, s32[]{:T(128)S(6)} %select_n.21), kind=kLoop, calls=%fused_computation.7 | loop fusion | flops 31 | bytes 264 | tf_op jit(solution)/shard_map/reduce_sum | solution.py:402
  6.2 0.1 copy.12.sizes_ref
  6.3 0.7 convert_element_type.7.forces_ref
  7.0 0.7 pad_add_fusion.info_ref
  7.7 0.7 multiply_bitcast_fusion.energies_ref
  8.4 0.0 collective-permute-done
  8.4 0.1 broadcast_select_fusion
  8.4 23.7 %all_to_all.20 = bf16[64,8,512]{2,1,0:T(8,128)(2,1)S(1)} all-to-all(bf16[64,8,512]{2,1,0:T(8,128)(2,1)S(1)} %bitcast.32), channel_id=1, replica_groups=mesh['rows'=16,'z'=4,'core'=2] {'rows','z'}, dimensions={0} | all-to-all | bytes 1048576 | tf_op jit(solution)/shard_map/all_to_all | solution.py:357
  32.1 15.9 %all_to_all.21 = bf16[64,8,512]{2,1,0:T(8,128)(2,1)S(1)} all-to-all(bf16[64,8,512]{2,1,0:T(8,128)(2,1)S(1)} %broadcast_in_dim.7), channel_id=1, replica_groups=mesh['rows'=16,'z'=4,'core'=2] {'rows','z'}, dimensions={0} | all-to-all | bytes 1048576 | tf_op jit(solution)/shard_map/all_to_all | solution.py:357
  48.0 2.8 %collective-permute-start.1 = (bf16[256,1024]{1,0:T(8,128)(2,1)S(1)}, bf16[256,1024]{1,0:T(8,128)(2,1)S(1)}, u32[]{:S(2)}, u32[]{:S(2)}) collective-permute-start(bf16[256,1024]{1,0:T(8,128)(2,1)S(1)} %bitcast.28), channel_id=1, source_target_pairs={{0,1},{1,0},{2,3},{3,2},{4,5},{5,4},{6,7},{7,6},{8,9},{9,8},{10,11... | collective-permute-start | bytes 1572872 | tf_op jit(solution)/shard_map/ppermute | solution.py:361
  50.9 1.5 %collective-permute-done.1.other_ref = bf16[256,1024]{1,0:T(8,128)(2,1)S(1)} collective-permute-done((bf16[256,1024]{1,0:T(8,128)(2,1)S(1)}, bf16[256,1024]{1,0:T(8,128)(2,1)S(1)}, u32[]{:S(2)}, u32[]{:S(2)}) %collective-permute-start.1) | collective-permute-done | bytes 524320 | tf_op jit(solution)/shard_map/ppermute | solution.py:361
  52.4 12.5 %gram_halves.1 = (f32[704,128]{1,0:T(8,128)S(1)}, f32[704,128]{1,0:T(8,128)S(1)}) custom-call(s32[3]{0:T(128)S(1)} %pad_add_fusion.info_ref, s32[1,32]{1,0:T(1,128)S(1)} %copy.12.sizes_ref, f32[1,32]{1,0:T(1,128)S(1)} %multiply_bitcast_fusion.energies_ref, bf16[256,1024]{1,0:T(8,128)(2,1)S(1)} %bitcast.29, ...), custom_call_target="tpu_custom_call" | custom-call | tf_op jit(solution)/shard_map/gram_halves/pallas_call | solution.py:323
  64.9 4.6 %collective-permute-start.2 = (f32[704,128]{1,0:T(8,128)S(1)}, f32[704,128]{1,0:T(8,128)S(1)}, u32[]{:S(2)}, u32[]{:S(2)}) collective-permute-start(f32[704,128]{1,0:T(8,128)S(1)} %get-tuple-element.19), channel_id=1, source_target_pairs={{0,1},{1,0},{2,3},{3,2},{4,5},{5,4},{6,7},{7,6},{8,9},{9,8},{10,11... | collective-permute-start | bytes 1081352 | tf_op jit(solution)/shard_map/ppermute | solution.py:361
  69.5 1.3 %collective-permute-done.2 = f32[704,128]{1,0:T(8,128)S(1)} collective-permute-done((f32[704,128]{1,0:T(8,128)S(1)}, f32[704,128]{1,0:T(8,128)S(1)}, u32[]{:S(2)}, u32[]{:S(2)}) %collective-permute-start.2) | collective-permute-done | bytes 360480 | tf_op jit(solution)/shard_map/ppermute | solution.py:361
  70.8 19.0 %all_to_all.22 = f32[64,1,1408]{2,1,0:T(1,128)S(1)} all-to-all(f32[64,1,1408]{2,1,0:T(1,128)S(1)} %bitcast.33), channel_id=1, replica_groups=mesh['rows'=16,'z'=4,'core'=2] {'rows','z'}, dimensions={0} | all-to-all | bytes 720896 | tf_op jit(solution)/shard_map/all_to_all | solution.py:357
  89.8 0.2 reduce_sum.19
  90.0 0.2 broadcast_in_dim.16
  90.2 14.6 %all_to_all.23 = f32[64,1,1408]{2,1,0:T(1,128)S(1)} all-to-all(f32[64,1,1408]{2,1,0:T(1,128)S(1)} %broadcast_in_dim.16), channel_id=1, replica_groups=mesh['rows'=16,'z'=4,'core'=2] {'rows','z'}, dimensions={0} | all-to-all | bytes 720896 | tf_op jit(solution)/shard_map/all_to_all | solution.py:357
  104.8 2.8 %collective-permute-start.3 = (f32[704,128]{1,0:T(8,128)S(1)}, f32[704,128]{1,0:T(8,128)S(1)}, u32[]{:S(2)}, u32[]{:S(2)}) collective-permute-start(f32[704,128]{1,0:T(8,128)S(1)} %bitcast.30), channel_id=1, source_target_pairs={{0,1},{1,0},{2,3},{3,2},{4,5},{5,4},{6,7},{7,6},{8,9},{9,8},{10,11... | collective-permute-start | bytes 1081352 | tf_op jit(solution)/shard_map/ppermute | solution.py:361
  107.7 1.3 %collective-permute-done.3.other_ref = f32[704,128]{1,0:T(8,128)S(1)} collective-permute-done((f32[704,128]{1,0:T(8,128)S(1)}, f32[704,128]{1,0:T(8,128)S(1)}, u32[]{:S(2)}, u32[]{:S(2)}) %collective-permute-start.3) | collective-permute-done | bytes 360480 | tf_op jit(solution)/shard_map/ppermute | solution.py:361
  109.0 14.3 %factor_and_solve.1 = (f32[512,512]{1,0:T(8,128)}, f32[4,128]{1,0:T(4,128)}) custom-call(s32[1]{0:T(128)} %bitcast.core_ref, f32[704,128]{1,0:T(8,128)S(1)} %bitcast.31, f32[704,128]{1,0:T(8,128)S(1)} %collective-permute-done.3.other_ref), custom_call_target="tpu_custom_call" | custom-call | tf_op jit(solution)/shard_map/factor_and_solve/pallas_call | solution.py:167
  (3 shorter events, 0.1 us)
Async XLA Ops:
  1.9 6.5 %collective-permute-start = (bf16[256,1024]{1,0:T(8,128)(2,1)S(1)}, bf16[256,1024]{1,0:T(8,128)(2,1)S(1)}, u32[]{:S(2)}, u32[]{:S(2)}) collective-permute-start(bf16[256,1024]{1,0:T(8,128)(2,1)S(1)} %get-tuple-element.24), channel_id=1, source_target_pairs={{0,1},{1,0},{2,3},{3,2},{4,5},{5,4},{6,7},{7,6},{8,9},{9,8},{10,11... | collective-permute-start | bytes 1572872 | tf_op jit(solution)/shard_map/ppermute | solution.py:361
  48.0 4.4 %collective-permute-start.1 = (bf16[256,1024]{1,0:T(8,128)(2,1)S(1)}, bf16[256,1024]{1,0:T(8,128)(2,1)S(1)}, u32[]{:S(2)}, u32[]{:S(2)}) collective-permute-start(bf16[256,1024]{1,0:T(8,128)(2,1)S(1)} %bitcast.28), channel_id=1, source_target_pairs={{0,1},{1,0},{2,3},{3,2},{4,5},{5,4},{6,7},{7,6},{8,9},{9,8},{10,11... | collective-permute-start | bytes 1572872 | tf_op jit(solution)/shard_map/ppermute | solution.py:361
  64.9 5.9 %collective-permute-start.2 = (f32[704,128]{1,0:T(8,128)S(1)}, f32[704,128]{1,0:T(8,128)S(1)}, u32[]{:S(2)}, u32[]{:S(2)}) collective-permute-start(f32[704,128]{1,0:T(8,128)S(1)} %get-tuple-element.19), channel_id=1, source_target_pairs={{0,1},{1,0},{2,3},{3,2},{4,5},{5,4},{6,7},{7,6},{8,9},{9,8},{10,11... | collective-permute-start | bytes 1081352 | tf_op jit(solution)/shard_map/ppermute | solution.py:361
  104.8 4.1 %collective-permute-start.3 = (f32[704,128]{1,0:T(8,128)S(1)}, f32[704,128]{1,0:T(8,128)S(1)}, u32[]{:S(2)}, u32[]{:S(2)}) collective-permute-start(f32[704,128]{1,0:T(8,128)S(1)} %bitcast.30), channel_id=1, source_target_pairs={{0,1},{1,0},{2,3},{3,2},{4,5},{5,4},{6,7},{7,6},{8,9},{9,8},{10,11... | collective-permute-start | bytes 1081352 | tf_op jit(solution)/shard_map/ppermute | solution.py:361

commit v10 on v8

--- a/solution.py
+++ b/solution.py
@@ -11,6 +11,7 @@
 TILE = 128
 GROUP = 32
 PART = 16
+EARLY = 4
 TERMS = 6
 
 
@@ -40,12 +41,15 @@
     groups = GROUP // 8
     sub = lax.broadcasted_iota(jnp.int32, (8, TILE), 0)
     pivots = [jnp.ones((8, TILE), jnp.float32) for _ in range(groups)]
+    columns = {}
     for k in range(0, GROUP, 2):
-        if k % PART == 0:
-            columns = {
-                j: [spread_lane(rows[s][0], first + j) if s >= j // 8 else None for s in range(groups)]
-                for j in range(k, k + PART)
-            }
+        soon = k + EARLY if k else 0
+        if soon % PART == 0 and soon < GROUP:
+            for j in range(soon, soon + PART):
+                columns[j] = [
+                    spread_lane(rows[s][0], first + j) if s >= j // 8 else None
+                    for s in range(groups)
+                ]
         s0, r0, r1 = k // 8, k % 8, k % 8 + 1
         one, two = columns[k], columns[k + 1]
         a = spread_row(one[s0], r0)
@@ -60,7 +64,7 @@
         two_next = {s: two[s] - one[s] * ratio for s in live}
         m1 = {s: one[s] * inv_a for s in live}
         m2 = {s: two_next[s] * inv_s for s in live}
-        for j in range(k + 2, k - k % PART + PART):
+        for j in range(k + 2, len(columns)):
             sj, rj = j // 8, j % 8
             u1 = spread_row(one[sj], rj)
             u2 = spread_row(two[sj], rj) - u1 * ratio

time: 120 us -> 118 us (0.983); the launches traced: 119 us -> 118 us
  Pallas kernels: 31.1 us -> 26.4 us
  blocking collectives: 47.4 us -> 51.3 us
    pallas_call x1, Pallas kernels: 16.8 us -> 12.7 us  [gram_halves(): pl.pallas_call(functools.partial(gram_kernel, scale, weight), out_shape=(...]
    all_to_all x3, blocking collectives: 47.4 us -> 51.3 us  [exchange(): return lax.all_to_all(pieces, axes, 0, 0, tiled=True)]
where the time goes in v10:
time: 118 us
  blocking collectives  51.3 us (43%)
  Pallas kernels  26.4 us (22%)
  starting transfers between devices  19.5 us (17%)
  waiting for transfers between devices  12.9 us (11%)
  other arithmetic  4.67 us (4%)
  between operations  2.02 us (2%)
  local copies, waits for them, and re-layouts  1.58 us (1%)
    all_to_all x3, blocking collectives, exchange(): return lax.all_to_all(pieces, axes, 0, 0, tiled=True)  51.3 us
    pallas_call x1, Pallas kernels, factor_and_solve(): pl.pallas_call(factor_kernel, out_shape=(jax.ShapeDtypeStruct((points, po...  13.7 us
    pallas_call x1, Pallas kernels, gram_halves(): pl.pallas_call(functools.partial(gram_kernel, scale, weight), out_shape=(...  12.7 us
    all_to_all x1, starting transfers between devices, exchange(): return lax.all_to_all(pieces, axes, 0, 0, tiled=True)  11.2 us
    ppermute x4, starting transfers between devices, swap(): return lax.ppermute(value, 'core', [(0, 1), (1, 0)])  8.3 us
    all_to_all x1, waiting for transfers between devices, exchange(): return lax.all_to_all(pieces, axes, 0, 0, tiled=True)  7.94 us
    ppermute x4, waiting for transfers between devices, swap(): return lax.ppermute(value, 'core', [(0, 1), (1, 0)])  5.01 us
  transfers between devices with their start and end apart: 5, of which 5 were waited for; matrix products, arithmetic and copies ran while one was open for 3% of the time, Pallas kernels for 0%

profile of v10, /device:TPU:1, one launch (start us, length us, event | category | flops | bytes accessed | tf_op | source)
XLA Modules:
  0.0 118.5 jit_solution(10806227000109325743)
XLA Ops:
  0.6 1.3 %dynamic-slice_bitcast_fusion = (bf16[256,1024]{1,0:T(8,128)(2,1)S(1)}, bf16[256,1024]{1,0:T(8,128)(2,1)S(1)}) fusion(bf16[1,512,1024]{2,1,0:T(8,128)(2,1)} %param.12, s32[]{:T(128)S(6)} %select_n.23, s32[]{:T(128)S(6)} %select_n.22), kind=kLoop, calls=%fused_computation | loop fusion | bytes 2097160 | tf_op jit(solution)/shard_map/dynamic_slice | solution.py:361
  1.9 1.5 %collective-permute-start = (bf16[256,1024]{1,0:T(8,128)(2,1)S(1)}, bf16[256,1024]{1,0:T(8,128)(2,1)S(1)}, u32[]{:S(2)}, u32[]{:S(2)}) collective-permute-start(bf16[256,1024]{1,0:T(8,128)(2,1)S(1)} %get-tuple-element.22), channel_id=1, source_target_pairs={{0,1},{1,0},{2,3},{3,2},{4,5},{5,4},{6,7},{7,6},{8,9},{9,8},{10,11... | collective-permute-start | bytes 1572872 | tf_op jit(solution)/shard_map/ppermute | solution.py:353
  4.1 0.9 collective-permute-done
  5.0 0.8 broadcast_select_fusion
  5.8 11.2 %all-to-all-start = ((bf16[64,8,512]{2,1,0:T(8,128)(2,1)}), bf16[64,8,512]{2,1,0:T(8,128)(2,1)S(1)}, u32[]{:S(2)}, u32[]{:S(2)}) async-start(bf16[64,8,512]{2,1,0:T(8,128)(2,1)} %bitcast.6), calls=%async_computation | async-start | bytes 1048576 | tf_op jit(solution)/shard_map/all_to_all | solution.py:349
  17.0 1.4 %fusion = (s32[]{:T(128)}, s32[1,32]{0,1:T(8,128)S(1)}) fusion(s32[128,32]{0,1:T(8,128)} %param.11, s32[]{:T(128)S(6)} %select_n.26), kind=kLoop, calls=%fused_computation.7 | loop fusion | flops 31 | bytes 264 | tf_op jit(solution)/shard_map/reduce_sum | solution.py:392
  19.1 0.1 copy.12.sizes_ref
  19.2 0.7 convert_element_type.3.forces_ref
  19.9 0.7 pad_add_fusion.info_ref
  20.7 0.7 multiply_bitcast_fusion.energies_ref
  21.3 7.9 %all-to-all-done = bf16[64,8,512]{2,1,0:T(8,128)(2,1)S(1)} async-done(((bf16[64,8,512]{2,1,0:T(8,128)(2,1)}), bf16[64,8,512]{2,1,0:T(8,128)(2,1)S(1)}, u32[]{:S(2)}, u32[]{:S(2)}) %all-to-all-start) | async-done | bytes 524320 | tf_op jit(solution)/shard_map/all_to_all | solution.py:349
  29.3 15.5 %all_to_all.20 = bf16[64,8,512]{2,1,0:T(8,128)(2,1)S(1)} all-to-all(bf16[64,8,512]{2,1,0:T(8,128)(2,1)S(1)} %broadcast_in_dim.7), channel_id=1, replica_groups=mesh['rows'=16,'z'=4,'core'=2] {'rows','z'}, dimensions={0} | all-to-all | bytes 1048576 | tf_op jit(solution)/shard_map/all_to_all | solution.py:349
  44.8 3.2 %collective-permute-start.1 = (bf16[256,1024]{1,0:T(8,128)(2,1)S(1)}, bf16[256,1024]{1,0:T(8,128)(2,1)S(1)}, u32[]{:S(2)}, u32[]{:S(2)}) collective-permute-start(bf16[256,1024]{1,0:T(8,128)(2,1)S(1)} %bitcast.27), channel_id=1, source_target_pairs={{0,1},{1,0},{2,3},{3,2},{4,5},{5,4},{6,7},{7,6},{8,9},{9,8},{10,11... | collective-permute-start | bytes 1572872 | tf_op jit(solution)/shard_map/ppermute | solution.py:353
  48.0 1.5 %collective-permute-done.1.other_ref = bf16[256,1024]{1,0:T(8,128)(2,1)S(1)} collective-permute-done((bf16[256,1024]{1,0:T(8,128)(2,1)S(1)}, bf16[256,1024]{1,0:T(8,128)(2,1)S(1)}, u32[]{:S(2)}, u32[]{:S(2)}) %collective-permute-start.1) | collective-permute-done | bytes 524320 | tf_op jit(solution)/shard_map/ppermute | solution.py:353
  49.6 12.7 %gram_halves.1 = (f32[704,128]{1,0:T(8,128)S(1)}, f32[704,128]{1,0:T(8,128)S(1)}) custom-call(s32[3]{0:T(128)S(1)} %pad_add_fusion.info_ref, s32[1,32]{1,0:T(1,128)S(1)} %copy.12.sizes_ref, f32[1,32]{1,0:T(1,128)S(1)} %multiply_bitcast_fusion.energies_ref, bf16[256,1024]{1,0:T(8,128)(2,1)S(1)} %bitcast.28, ...), custom_call_target="tpu_custom_call" | custom-call | tf_op jit(solution)/shard_map/gram_halves/pallas_call | solution.py:315
  62.3 0.5 collective-permute-start.2
  62.7 1.3 %collective-permute-done.2 = f32[704,128]{1,0:T(8,128)S(1)} collective-permute-done((f32[704,128]{1,0:T(8,128)S(1)}, f32[704,128]{1,0:T(8,128)S(1)}, u32[]{:S(2)}, u32[]{:S(2)}) %collective-permute-start.2) | collective-permute-done | bytes 360480 | tf_op jit(solution)/shard_map/ppermute | solution.py:353
  64.1 21.3 %all_to_all.21 = f32[64,1,1408]{2,1,0:T(1,128)S(1)} all-to-all(f32[64,1,1408]{2,1,0:T(1,128)S(1)} %bitcast.31), channel_id=1, replica_groups=mesh['rows'=16,'z'=4,'core'=2] {'rows','z'}, dimensions={0} | all-to-all | bytes 720896 | tf_op jit(solution)/shard_map/all_to_all | solution.py:349
  85.4 0.2 reduce_sum.19
  85.6 0.2 broadcast_in_dim.16
  85.8 14.5 %all_to_all.22 = f32[64,1,1408]{2,1,0:T(1,128)S(1)} all-to-all(f32[64,1,1408]{2,1,0:T(1,128)S(1)} %broadcast_in_dim.16), channel_id=1, replica_groups=mesh['rows'=16,'z'=4,'core'=2] {'rows','z'}, dimensions={0} | all-to-all | bytes 720896 | tf_op jit(solution)/shard_map/all_to_all | solution.py:349
  100.3 3.1 %collective-permute-start.3 = (f32[704,128]{1,0:T(8,128)S(1)}, f32[704,128]{1,0:T(8,128)S(1)}, u32[]{:S(2)}, u32[]{:S(2)}) collective-permute-start(f32[704,128]{1,0:T(8,128)S(1)} %bitcast.29), channel_id=1, source_target_pairs={{0,1},{1,0},{2,3},{3,2},{4,5},{5,4},{6,7},{7,6},{8,9},{9,8},{10,11... | collective-permute-start | bytes 1081352 | tf_op jit(solution)/shard_map/ppermute | solution.py:353
  103.5 1.3 %collective-permute-done.3.other_ref = f32[704,128]{1,0:T(8,128)S(1)} collective-permute-done((f32[704,128]{1,0:T(8,128)S(1)}, f32[704,128]{1,0:T(8,128)S(1)}, u32[]{:S(2)}, u32[]{:S(2)}) %collective-permute-start.3) | collective-permute-done | bytes 360480 | tf_op jit(solution)/shard_map/ppermute | solution.py:353
  104.8 13.7 %factor_and_solve.1 = (f32[512,512]{1,0:T(8,128)}, f32[4,128]{1,0:T(4,128)}) custom-call(s32[1]{0:T(128)} %bitcast.core_ref, f32[704,128]{1,0:T(8,128)S(1)} %bitcast.30, f32[704,128]{1,0:T(8,128)S(1)} %collective-permute-done.3.other_ref), custom_call_target="tpu_custom_call" | custom-call | tf_op jit(solution)/shard_map/factor_and_solve/pallas_call | solution.py:171
  (3 shorter events, 0.1 us)
Async XLA Ops:
  1.9 3.0 %collective-permute-start = (bf16[256,1024]{1,0:T(8,128)(2,1)S(1)}, bf16[256,1024]{1,0:T(8,128)(2,1)S(1)}, u32[]{:S(2)}, u32[]{:S(2)}) collective-permute-start(bf16[256,1024]{1,0:T(8,128)(2,1)S(1)} %get-tuple-element.22), channel_id=1, source_target_pairs={{0,1},{1,0},{2,3},{3,2},{4,5},{5,4},{6,7},{7,6},{8,9},{9,8},{10,11... | collective-permute-start | bytes 1572872 | tf_op jit(solution)/shard_map/ppermute | solution.py:353
  5.8 23.5 %all-to-all-start = ((bf16[64,8,512]{2,1,0:T(8,128)(2,1)}), bf16[64,8,512]{2,1,0:T(8,128)(2,1)S(1)}, u32[]{:S(2)}, u32[]{:S(2)}) async-start(bf16[64,8,512]{2,1,0:T(8,128)(2,1)} %bitcast.6), calls=%async_computation | async-start | bytes 1048576 | tf_op jit(solution)/shard_map/all_to_all | solution.py:349
  44.8 4.7 %collective-permute-start.1 = (bf16[256,1024]{1,0:T(8,128)(2,1)S(1)}, bf16[256,1024]{1,0:T(8,128)(2,1)S(1)}, u32[]{:S(2)}, u32[]{:S(2)}) collective-permute-start(bf16[256,1024]{1,0:T(8,128)(2,1)S(1)} %bitcast.27), channel_id=1, source_target_pairs={{0,1},{1,0},{2,3},{3,2},{4,5},{5,4},{6,7},{7,6},{8,9},{9,8},{10,11... | collective-permute-start | bytes 1572872 | tf_op jit(solution)/shard_map/ppermute | solution.py:353
  62.3 1.8 %collective-permute-start.2 = (f32[704,128]{1,0:T(8,128)S(1)}, f32[704,128]{1,0:T(8,128)S(1)}, u32[]{:S(2)}, u32[]{:S(2)}) collective-permute-start(f32[704,128]{1,0:T(8,128)S(1)} %get-tuple-element.17), channel_id=1, source_target_pairs={{0,1},{1,0},{2,3},{3,2},{4,5},{5,4},{6,7},{7,6},{8,9},{9,8},{10,11... | collective-permute-start | bytes 1081352 | tf_op jit(solution)/shard_map/ppermute | solution.py:353
  100.3 4.5 %collective-permute-start.3 = (f32[704,128]{1,0:T(8,128)S(1)}, f32[704,128]{1,0:T(8,128)S(1)}, u32[]{:S(2)}, u32[]{:S(2)}) collective-permute-start(f32[704,128]{1,0:T(8,128)S(1)} %bitcast.29), channel_id=1, source_target_pairs={{0,1},{1,0},{2,3},{3,2},{4,5},{5,4},{6,7},{7,6},{8,9},{9,8},{10,11... | collective-permute-start | bytes 1081352 | tf_op jit(solution)/shard_map/ppermute | solution.py:353

commit v11 on v10

--- a/solution.py
+++ b/solution.py
@@ -10,7 +10,7 @@
 
 TILE = 128
 GROUP = 32
-PART = 16
+PART = 8
 EARLY = 4
 TERMS = 6
 

time: 118 us -> 119 us (level)
  no operation moved by 1% of the time
where the time goes in v11:
time: 119 us; the launch traced here: 118 us
  blocking collectives  51.5 us (43%)
  Pallas kernels  26.3 us (22%)
  starting transfers between devices  19.1 us (16%)
  waiting for transfers between devices  13.3 us (11%)
  other arithmetic  4.67 us (4%)
  between operations  2.03 us (2%)
  local copies, waits for them, and re-layouts  1.58 us (1%)
    all_to_all x3, blocking collectives, exchange(): return lax.all_to_all(pieces, axes, 0, 0, tiled=True)  51.5 us
    pallas_call x1, Pallas kernels, factor_and_solve(): pl.pallas_call(factor_kernel, out_shape=(jax.ShapeDtypeStruct((points, po...  13.6 us
    pallas_call x1, Pallas kernels, gram_halves(): pl.pallas_call(functools.partial(gram_kernel, scale, weight), out_shape=(...  12.7 us
    all_to_all x1, starting transfers between devices, exchange(): return lax.all_to_all(pieces, axes, 0, 0, tiled=True)  11.2 us
    all_to_all x1, waiting for transfers between devices, exchange(): return lax.all_to_all(pieces, axes, 0, 0, tiled=True)  7.94 us
    ppermute x4, starting transfers between devices, swap(): return lax.ppermute(value, 'core', [(0, 1), (1, 0)])  7.93 us
    ppermute x4, waiting for transfers between devices, swap(): return lax.ppermute(value, 'core', [(0, 1), (1, 0)])  5.37 us
  transfers between devices with their start and end apart: 5, of which 5 were waited for; matrix products, arithmetic and copies ran while one was open for 3% of the time, Pallas kernels for 0%

profile of v11, /device:TPU:1, one launch (start us, length us, event | category | flops | bytes accessed | tf_op | source)
XLA Modules:
  0.0 118.5 jit_solution(2282622533149239544)
XLA Ops:
  0.6 1.3 %dynamic-slice_bitcast_fusion = (bf16[256,1024]{1,0:T(8,128)(2,1)S(1)}, bf16[256,1024]{1,0:T(8,128)(2,1)S(1)}) fusion(bf16[1,512,1024]{2,1,0:T(8,128)(2,1)} %param.12, s32[]{:T(128)S(6)} %select_n.23, s32[]{:T(128)S(6)} %select_n.22), kind=kLoop, calls=%fused_computation | loop fusion | bytes 2097160 | tf_op jit(solution)/shard_map/dynamic_slice | solution.py:361
  1.9 1.5 %collective-permute-start = (bf16[256,1024]{1,0:T(8,128)(2,1)S(1)}, bf16[256,1024]{1,0:T(8,128)(2,1)S(1)}, u32[]{:S(2)}, u32[]{:S(2)}) collective-permute-start(bf16[256,1024]{1,0:T(8,128)(2,1)S(1)} %get-tuple-element.22), channel_id=1, source_target_pairs={{0,1},{1,0},{2,3},{3,2},{4,5},{5,4},{6,7},{7,6},{8,9},{9,8},{10,11... | collective-permute-start | bytes 1572872 | tf_op jit(solution)/shard_map/ppermute | solution.py:353
  4.1 0.9 collective-permute-done
  5.0 0.8 broadcast_select_fusion
  5.8 11.2 %all-to-all-start = ((bf16[64,8,512]{2,1,0:T(8,128)(2,1)}), bf16[64,8,512]{2,1,0:T(8,128)(2,1)S(1)}, u32[]{:S(2)}, u32[]{:S(2)}) async-start(bf16[64,8,512]{2,1,0:T(8,128)(2,1)} %bitcast.6), calls=%async_computation | async-start | bytes 1048576 | tf_op jit(solution)/shard_map/all_to_all | solution.py:349
  17.0 1.4 %fusion = (s32[]{:T(128)}, s32[1,32]{0,1:T(8,128)S(1)}) fusion(s32[128,32]{0,1:T(8,128)} %param.11, s32[]{:T(128)S(6)} %select_n.26), kind=kLoop, calls=%fused_computation.7 | loop fusion | flops 31 | bytes 264 | tf_op jit(solution)/shard_map/reduce_sum | solution.py:392
  19.1 0.1 copy.12.sizes_ref
  19.2 0.7 convert_element_type.3.forces_ref
  19.9 0.7 pad_add_fusion.info_ref
  20.7 0.7 multiply_bitcast_fusion.energies_ref
  21.3 7.9 %all-to-all-done = bf16[64,8,512]{2,1,0:T(8,128)(2,1)S(1)} async-done(((bf16[64,8,512]{2,1,0:T(8,128)(2,1)}), bf16[64,8,512]{2,1,0:T(8,128)(2,1)S(1)}, u32[]{:S(2)}, u32[]{:S(2)}) %all-to-all-start) | async-done | bytes 524320 | tf_op jit(solution)/shard_map/all_to_all | solution.py:349
  29.3 15.5 %all_to_all.20 = bf16[64,8,512]{2,1,0:T(8,128)(2,1)S(1)} all-to-all(bf16[64,8,512]{2,1,0:T(8,128)(2,1)S(1)} %broadcast_in_dim.7), channel_id=1, replica_groups=mesh['rows'=16,'z'=4,'core'=2] {'rows','z'}, dimensions={0} | all-to-all | bytes 1048576 | tf_op jit(solution)/shard_map/all_to_all | solution.py:349
  44.8 3.2 %collective-permute-start.1 = (bf16[256,1024]{1,0:T(8,128)(2,1)S(1)}, bf16[256,1024]{1,0:T(8,128)(2,1)S(1)}, u32[]{:S(2)}, u32[]{:S(2)}) collective-permute-start(bf16[256,1024]{1,0:T(8,128)(2,1)S(1)} %bitcast.27), channel_id=1, source_target_pairs={{0,1},{1,0},{2,3},{3,2},{4,5},{5,4},{6,7},{7,6},{8,9},{9,8},{10,11... | collective-permute-start | bytes 1572872 | tf_op jit(solution)/shard_map/ppermute | solution.py:353
  48.0 1.5 %collective-permute-done.1.other_ref = bf16[256,1024]{1,0:T(8,128)(2,1)S(1)} collective-permute-done((bf16[256,1024]{1,0:T(8,128)(2,1)S(1)}, bf16[256,1024]{1,0:T(8,128)(2,1)S(1)}, u32[]{:S(2)}, u32[]{:S(2)}) %collective-permute-start.1) | collective-permute-done | bytes 524320 | tf_op jit(solution)/shard_map/ppermute | solution.py:353
  49.6 12.7 %gram_halves.1 = (f32[704,128]{1,0:T(8,128)S(1)}, f32[704,128]{1,0:T(8,128)S(1)}) custom-call(s32[3]{0:T(128)S(1)} %pad_add_fusion.info_ref, s32[1,32]{1,0:T(1,128)S(1)} %copy.12.sizes_ref, f32[1,32]{1,0:T(1,128)S(1)} %multiply_bitcast_fusion.energies_ref, bf16[256,1024]{1,0:T(8,128)(2,1)S(1)} %bitcast.28, ...), custom_call_target="tpu_custom_call" | custom-call | tf_op jit(solution)/shard_map/gram_halves/pallas_call | solution.py:315
  62.3 0.1 collective-permute-start.2
  62.4 1.7 %collective-permute-done.2 = f32[704,128]{1,0:T(8,128)S(1)} collective-permute-done((f32[704,128]{1,0:T(8,128)S(1)}, f32[704,128]{1,0:T(8,128)S(1)}, u32[]{:S(2)}, u32[]{:S(2)}) %collective-permute-start.2) | collective-permute-done | bytes 360480 | tf_op jit(solution)/shard_map/ppermute | solution.py:353
  64.1 21.4 %all_to_all.21 = f32[64,1,1408]{2,1,0:T(1,128)S(1)} all-to-all(f32[64,1,1408]{2,1,0:T(1,128)S(1)} %bitcast.31), channel_id=1, replica_groups=mesh['rows'=16,'z'=4,'core'=2] {'rows','z'}, dimensions={0} | all-to-all | bytes 720896 | tf_op jit(solution)/shard_map/all_to_all | solution.py:349
  85.5 0.2 reduce_sum.19
  85.7 0.2 broadcast_in_dim.16
  85.9 14.5 %all_to_all.22 = f32[64,1,1408]{2,1,0:T(1,128)S(1)} all-to-all(f32[64,1,1408]{2,1,0:T(1,128)S(1)} %broadcast_in_dim.16), channel_id=1, replica_groups=mesh['rows'=16,'z'=4,'core'=2] {'rows','z'}, dimensions={0} | all-to-all | bytes 720896 | tf_op jit(solution)/shard_map/all_to_all | solution.py:349
  100.4 3.1 %collective-permute-start.3 = (f32[704,128]{1,0:T(8,128)S(1)}, f32[704,128]{1,0:T(8,128)S(1)}, u32[]{:S(2)}, u32[]{:S(2)}) collective-permute-start(f32[704,128]{1,0:T(8,128)S(1)} %bitcast.29), channel_id=1, source_target_pairs={{0,1},{1,0},{2,3},{3,2},{4,5},{5,4},{6,7},{7,6},{8,9},{9,8},{10,11... | collective-permute-start | bytes 1081352 | tf_op jit(solution)/shard_map/ppermute | solution.py:353
  103.6 1.3 %collective-permute-done.3.other_ref = f32[704,128]{1,0:T(8,128)S(1)} collective-permute-done((f32[704,128]{1,0:T(8,128)S(1)}, f32[704,128]{1,0:T(8,128)S(1)}, u32[]{:S(2)}, u32[]{:S(2)}) %collective-permute-start.3) | collective-permute-done | bytes 360480 | tf_op jit(solution)/shard_map/ppermute | solution.py:353
  104.9 13.6 %factor_and_solve.1 = (f32[512,512]{1,0:T(8,128)}, f32[4,128]{1,0:T(4,128)}) custom-call(s32[1]{0:T(128)} %bitcast.core_ref, f32[704,128]{1,0:T(8,128)S(1)} %bitcast.30, f32[704,128]{1,0:T(8,128)S(1)} %collective-permute-done.3.other_ref), custom_call_target="tpu_custom_call" | custom-call | tf_op jit(solution)/shard_map/factor_and_solve/pallas_call | solution.py:171
  (3 shorter events, 0.1 us)
Async XLA Ops:
  1.9 3.0 %collective-permute-start = (bf16[256,1024]{1,0:T(8,128)(2,1)S(1)}, bf16[256,1024]{1,0:T(8,128)(2,1)S(1)}, u32[]{:S(2)}, u32[]{:S(2)}) collective-permute-start(bf16[256,1024]{1,0:T(8,128)(2,1)S(1)} %get-tuple-element.22), channel_id=1, source_target_pairs={{0,1},{1,0},{2,3},{3,2},{4,5},{5,4},{6,7},{7,6},{8,9},{9,8},{10,11... | collective-permute-start | bytes 1572872 | tf_op jit(solution)/shard_map/ppermute | solution.py:353
  5.8 23.5 %all-to-all-start = ((bf16[64,8,512]{2,1,0:T(8,128)(2,1)}), bf16[64,8,512]{2,1,0:T(8,128)(2,1)S(1)}, u32[]{:S(2)}, u32[]{:S(2)}) async-start(bf16[64,8,512]{2,1,0:T(8,128)(2,1)} %bitcast.6), calls=%async_computation | async-start | bytes 1048576 | tf_op jit(solution)/shard_map/all_to_all | solution.py:349
  44.8 4.7 %collective-permute-start.1 = (bf16[256,1024]{1,0:T(8,128)(2,1)S(1)}, bf16[256,1024]{1,0:T(8,128)(2,1)S(1)}, u32[]{:S(2)}, u32[]{:S(2)}) collective-permute-start(bf16[256,1024]{1,0:T(8,128)(2,1)S(1)} %bitcast.27), channel_id=1, source_target_pairs={{0,1},{1,0},{2,3},{3,2},{4,5},{5,4},{6,7},{7,6},{8,9},{9,8},{10,11... | collective-permute-start | bytes 1572872 | tf_op jit(solution)/shard_map/ppermute | solution.py:353
  62.3 1.8 %collective-permute-start.2 = (f32[704,128]{1,0:T(8,128)S(1)}, f32[704,128]{1,0:T(8,128)S(1)}, u32[]{:S(2)}, u32[]{:S(2)}) collective-permute-start(f32[704,128]{1,0:T(8,128)S(1)} %get-tuple-element.17), channel_id=1, source_target_pairs={{0,1},{1,0},{2,3},{3,2},{4,5},{5,4},{6,7},{7,6},{8,9},{9,8},{10,11... | collective-permute-start | bytes 1081352 | tf_op jit(solution)/shard_map/ppermute | solution.py:353
  100.4 4.5 %collective-permute-start.3 = (f32[704,128]{1,0:T(8,128)S(1)}, f32[704,128]{1,0:T(8,128)S(1)}, u32[]{:S(2)}, u32[]{:S(2)}) collective-permute-start(f32[704,128]{1,0:T(8,128)S(1)} %bitcast.29), channel_id=1, source_target_pairs={{0,1},{1,0},{2,3},{3,2},{4,5},{5,4},{6,7},{7,6},{8,9},{9,8},{10,11... | collective-permute-start | bytes 1081352 | tf_op jit(solution)/shard_map/ppermute | solution.py:353
